TPU v7x, 32 devices: a whole 2x2x4 slice. The times are simulated.
32 devices in a mesh: doc: 4 (over y, core), seq: 8 (over z, x).
Axes of the slice: x: 2, y: 2, z: 4, core: 2. Of those that a mesh axis runs over, the one named last changes fastest.
Arguments:
- hidden: bfloat16 [4, 4096, 768], P('doc', 'seq'), may hold values from -6 to 6
- token_ids: int32 [4, 4096], P('doc', 'seq'), may hold values from 0 to 50264, as said below
- w_query: bfloat16 [768, 768], replicated, may hold values from -0.625 to 0.625
- w_keyval: bfloat16 [768, 1536], replicated, may hold values from -0.21875 to 0.21875
- w_out: bfloat16 [768, 768], replicated, may hold values from -0.21875 to 0.21875
- x_query: bfloat16 [768, 768], replicated, may hold values from -0.21875 to 0.21875
- x_out: bfloat16 [768, 768], replicated, may hold values from -0.21875 to 0.21875
- shortlist: int32 [4, 320], P('doc'), may hold values from 0 to 9215, as said below
- code_row: int32 [9216], replicated, may hold values from 0 to 9215, as said below
- code_cache: bfloat16 [9216, 2, 8, 768], P(('doc', 'seq')), may hold values from -10 to 10
Outputs:
- refined: bfloat16 [4, 4096, 768], P('doc', 'seq')
- cand_score: float32 [4, 320], P('doc')
Inputs may be any that keep to these rules, and one draw needn't show every extreme that they name: `token_ids`: each summary is a run of ids of 1 or more followed by padding ids 0 up to its end; every summary has 1024 or more nonzero ids and one summary has no padding. `shortlist`: the candidates of one summary are distinct codes; at most 16 of them have code_row in one block of 288 rows (row // 288 equal), and for every summary some block holds exactly 16 of them. `code_row`: each row of the cache holds exactly one code.
All inputs are finite; a program needn't handle non-finite values.
Results may differ from a plain program's by a relative error of at most 0.018.
Values may be sent and summed in bfloat16 or wider, within the bound.
A program may use at most 192 MiB of HBM per device.

v0:
```python
import math

import jax
import jax.numpy as jnp
from jax import lax
from jax.sharding import PartitionSpec as P

HEADS = 12
HALF_WIN = 256
DESC = 8


def extended(block, sides, width):
    for axis, dim in sides:
        count = lax.axis_size(axis)
        forward = [(i, i + 1) for i in range(count - 1)]
        backward = [(target, source) for source, target in forward]
        low = lax.ppermute(
            lax.slice_in_dim(block, block.shape[dim] - width, None, axis=dim), axis, forward
        )
        high = lax.ppermute(lax.slice_in_dim(block, 0, width, axis=dim), axis, backward)
        block = jnp.concatenate([low, block, high], axis=dim)
    return block


def layer_norm(values):
    centered = values - jnp.mean(values, axis=-1, keepdims=True)
    spread = jnp.mean(centered * centered, axis=-1, keepdims=True)
    return centered * lax.rsqrt(spread + 1e-05)


def attend(query, key_rows, value_rows, allowed, weigh):
    query_count, width = query.shape
    key_count = key_rows.shape[0]
    head_size = width // HEADS
    per_group = 4
    group_count = HEADS // per_group
    score_scale = 1.0 / math.sqrt(head_size)
    query_groups = query.reshape(query_count, group_count, per_group * head_size).transpose(1, 0, 2)
    key_groups = key_rows.reshape(key_count, group_count, per_group * head_size).transpose(1, 0, 2)
    value_groups = value_rows.reshape(key_count, group_count, per_group * head_size).transpose(
        1, 0, 2
    )

    def head_group(operands):
        group_query, group_keys, group_values = operands
        query_heads = group_query.reshape(query_count, per_group, head_size)
        key_heads = group_keys.reshape(key_count, per_group, head_size)
        value_heads = group_values.reshape(key_count, per_group, head_size)
        scores = (
            jnp.einsum("qhd,khd->hqk", query_heads, key_heads, preferred_element_type=jnp.float32)
            * score_scale
        )
        expd = jnp.where(allowed[None], jnp.exp(scores), 0.0)
        weights = expd / jnp.sum(expd, axis=-1, keepdims=True)
        context = jnp.einsum(
            "hqk,khd->qhd",
            weights.astype(jnp.bfloat16),
            value_heads,
            preferred_element_type=jnp.float32,
        )
        context = context.reshape(query_count, per_group * head_size).astype(jnp.bfloat16)
        if weigh is None:
            return (context, jnp.zeros((1,), jnp.float32))
        return (context, jnp.sum(jnp.where(weigh[None, :, None], weights, 0.0), axis=(0, 1)))

    contexts, masses = lax.map(head_group, (query_groups, key_groups, value_groups))
    context = contexts.transpose(1, 0, 2).reshape(query_count, width)
    return (context, jnp.sum(masses, axis=0))


def local(
    hidden, token_ids, w_query, w_keyval, w_out, x_query, x_out, shortlist, code_row, code_cache
):
    doc_hidden = hidden[0]
    doc_tokens = token_ids[0]
    tok_rows, width = doc_hidden.shape
    seq_count = lax.axis_size("seq")
    doc_count = lax.axis_size("doc")
    devices = seq_count * doc_count
    seq_index = lax.axis_index("seq")
    first_row = seq_index * tok_rows
    local_count = jnp.sum((doc_tokens != 0).astype(jnp.int32))
    length = lax.psum(local_count, "seq")
    normed = layer_norm(doc_hidden.astype(jnp.float32)).astype(jnp.bfloat16)
    query = jnp.dot(normed, w_query, preferred_element_type=jnp.float32).astype(jnp.bfloat16)
    keyval = jnp.dot(normed, w_keyval, preferred_element_type=jnp.float32).astype(jnp.bfloat16)
    padded = extended(keyval, (("seq", 0),), HALF_WIN)
    query_pos = first_row + jnp.arange(tok_rows, dtype=jnp.int32)
    key_pos = first_row - HALF_WIN + jnp.arange(tok_rows + 2 * HALF_WIN, dtype=jnp.int32)
    near = jnp.abs(query_pos[:, None] - key_pos[None, :]) <= HALF_WIN
    usable = ((key_pos >= 0) & (key_pos < length))[None, :] | (
        query_pos[:, None] == key_pos[None, :]
    )
    context, unused = attend(query, padded[:, :width], padded[:, width:], near & usable, None)
    middle = (
        doc_hidden.astype(jnp.float32) + jnp.dot(context, w_out, preferred_element_type=jnp.float32)
    ).astype(jnp.bfloat16)
    middle_wide = middle.astype(jnp.float32)
    cross_normed = layer_norm(middle_wide).astype(jnp.bfloat16)
    cross_query = jnp.dot(cross_normed, x_query, preferred_element_type=jnp.float32).astype(
        jnp.bfloat16
    )
    cand_count = shortlist.shape[1]
    code_dev = code_cache.shape[0]
    capacity = 8 * cand_count // (5 * devices)
    cache_rows = code_row[shortlist[0]]
    owner_dev = cache_rows // code_dev
    local_row = cache_rows % code_dev
    onehot = (owner_dev[:, None] == jnp.arange(devices, dtype=jnp.int32)[None, :]).astype(jnp.int32)
    slot_rank = jnp.sum((jnp.cumsum(onehot, axis=0) - 1) * onehot, axis=1)
    request = jnp.zeros((devices, capacity), jnp.int32).at[owner_dev, slot_rank].set(local_row)
    slot_live = jnp.zeros((devices, capacity), jnp.bool_).at[owner_dev, slot_rank].set(True)
    fetched_rows = lax.all_to_all(
        code_cache[
            lax.all_to_all(request, ("doc", "seq"), split_axis=0, concat_axis=0, tiled=True)
        ],
        ("doc", "seq"),
        split_axis=0,
        concat_axis=0,
        tiled=True,
    )
    live_keys = slot_live.reshape(-1)
    slot_index = owner_dev * capacity + slot_rank
    fetched_rows = fetched_rows.reshape(devices * capacity, 2, DESC, width)
    cand_keys = fetched_rows[:, 0].reshape(devices * capacity * DESC, width)
    cand_values = fetched_rows[:, 1].reshape(devices * capacity * DESC, width)
    key_live = jnp.repeat(live_keys, DESC)
    allowed = jnp.broadcast_to(key_live[None, :], (tok_rows, key_live.shape[0]))
    cross_context, key_mass = attend(
        cross_query, cand_keys, cand_values, allowed, query_pos < length
    )
    refined = (
        middle_wide + jnp.dot(cross_context, x_out, preferred_element_type=jnp.float32)
    ).astype(jnp.bfloat16)
    local_mass = jnp.sum(key_mass.reshape(devices * capacity, DESC), axis=1)
    slot_total = lax.psum(local_mass, "seq")
    cand_score = cand_count * slot_total[slot_index] / (HEADS * length.astype(jnp.float32))
    return (refined[None], cand_score[None])


def solution(mesh):
    return jax.shard_map(
        local,
        mesh=mesh,
        in_specs=(
            P("doc", "seq", None),
            P("doc", "seq"),
            P(),
            P(),
            P(),
            P(),
            P(),
            P("doc", None),
            P(),
            P(("doc", "seq"), None, None, None),
        ),
        out_specs=(P("doc", "seq", None), P("doc", None)),
        check_vma=False,
    )
```

profile of v0, /device:TPU:0, one launch (start us, length us, event | category | flops | bytes accessed | tf_op | source)
XLA Modules:
  0.0 661.9 jit_solution(4134632235557733211)
XLA Ops:
  1.5 3.5 gather_fusion
  6.3 17.1 %scatter_fusion = s32[32,16]{0,1:T(8,128)S(1)} fusion(s32[32,16]{0,1:T(8,128)S(1)} %broadcast.287, s32[320]{0:T(512)S(1)} %get-tuple-element.144, s32[320]{0:T(512)S(1)} %get-tuple-element.195), kind=kCustom, calls=%fused_computation.3 | custom fusion | bytes 6400 | tf_op jit(solution)/shard_map/scatter | solution.py:112
  23.5 14.2 %all_to_all.17 = s32[32,1,16]{2,1,0:T(1,128)S(1)} all-to-all(s32[32,1,16]{2,1,0:T(1,128)S(1)} %copy.33), channel_id=1, replica_groups=mesh['doc'=4,'seq'=8] {'doc','seq'}, dimensions={0} | all-to-all | bytes 4096 | tf_op jit(solution)/shard_map/all_to_all | solution.py:116
  37.8 17.9 %gather_fusion.1 = bf16[512,2,8,768]{3,2,1,0:T(8,128)(2,1)} fusion(bf16[288,2,8,768]{3,2,1,0:T(8,128)(2,1)} %param.23, s32[1024]{0:T(1024)S(1)} %pad_clamp_fusion.1), kind=kCustom, calls=%fused_computation.1 | custom fusion | bytes 25167872 | tf_op jit(solution)/shard_map/gather | solution.py:115
  55.7 3.9 all-to-all-start.1
  64.1 4.4 collective-permute-start
  70.4 287.7 %psum.14 = s32[]{:T(128)} all-reduce(s32[]{:T(128)} %fusion.40), channel_id=1, replica_groups=mesh['doc'=4,'seq'=8] {'seq'}, use_global_device_ids=true, to_apply=%region_3.0 | all-reduce | flops 1 | bytes 8 | tf_op jit(solution)/shard_map/psum | solution.py:84
  361.4 17.6 %scatter_fusion.1 = pred[32,16]{0,1:T(8,128)(4,1)S(1)} fusion(pred[32,16]{0,1:T(8,128)(4,1)S(1)} %broadcast_in_dim.57, s32[320]{0:T(512)S(1)} %get-tuple-element.144, pred[320]{0:T(512)(128)(4,1)S(1)} %broadcast.330), kind=kCustom, calls=%fused_computation.4 | custom fusion | bytes 3520 | tf_op jit(solution)/shard_map/scatter | solution.py:113
  384.3 2.6 copy.28
  389.5 23.4 %while.24 = (s32[]{:T(128)}, bf16[3,512,256]{1,2,0:T(8,128)(2,1)}, bf16[3,1024,256]{1,2,0:T(8,128)(2,1)}, bf16[3,512,256]{1,2,0:T(8,128)(2,1)S(1)}, bf16[3,1024,...) while((s32[]{:T(128)}, bf16[3,512,256]{1,2,0:T(8,128)(2,1)}, ...), condition=%wide.region_6.7_spmd.clone, body=%wide.region_4.6_spmd.clone.sunk | while | flops 554825728 | bytes 23092836 | solution.py:67
  413.0 2.7 convert_reduce_fusion
  417.2 6.4 copy.34
  423.6 5.1 fusion.49
  428.7 17.3 %reshape_reshape_squeeze.6 = bf16[4096,3,256]{2,1,0:T(4,128)(2,1)} reshape(bf16[512,1,8,768]{3,2,0,1:T(8,128)(2,1)} %get-tuple-element.190) | data formatting | bytes 12582912 | tf_op jit(solution)/shard_map/reshape;reshape;squeeze | solution.py:41
  446.0 13.1 %copy.37 = bf16[3,4096,256]{1,2,0:T(8,128)(2,1)} copy(bf16[3,4096,256]{2,0,1:T(4,128)(2,1)} %bitcast.130) | data formatting | bytes 12582912
  459.1 17.3 %reshape_reshape_squeeze.7 = bf16[4096,3,256]{2,1,0:T(4,128)(2,1)} reshape(bf16[512,1,8,768]{3,2,0,1:T(8,128)(2,1)} %get-tuple-element.189) | data formatting | bytes 12582912 | tf_op jit(solution)/shard_map/reshape;reshape;squeeze | solution.py:40
  476.4 13.1 %copy.38 = bf16[3,4096,256]{1,2,0:T(8,128)(2,1)} copy(bf16[3,4096,256]{2,0,1:T(4,128)(2,1)} %bitcast.131) | data formatting | bytes 12582912
  490.5 141.8 %while.25 = (s32[]{:T(128)}, bf16[3,512,256]{1,2,0:T(8,128)(2,1)}, f32[3,4096]{1,0:T(4,128)S(1)}, bf16[3,4096,256]{1,2,0:T(8,128)(2,1)}, bf16[3,512,256]{1,2,0:T...) while((s32[]{:T(128)}, bf16[3,512,256]{1,2,0:T(8,128)(2,1)}, ...), condition=%wide.region_17.18_spmd.clone, body=%wide.region_14.17_spmd.clone.sunk | while | flops 2248272896 | bytes 114906752 | solution.py:67
  490.5 2.6 constant_dynamic-slice_fusion.12
  493.1 14.1 %fusion.87 = (f32[4,512]{1,0:T(4,128)S(1)}, f32[4,512,4096]{2,1,0:T(8,128)}) fusion(pred[4096]{0:T(1024)(128)(4,1)S(1)} %get-tuple-element.374, bf16[512,4,64]{0,2,1:T(8,128)(2,1)S(1)} %bitcast.139, bf16[4096,4,64]{0,2,1:T(8,128)(2,1)S(1)} %bitcast.127), kind=kOutput, calls=%fused_computation.24.clone.1 | convolution fusion | flops 1098905600 | bytes 35926016 | tf_op jit(solution)/shard_map/while/body/eval_jaxpr/qhd,khd->hqk/dot_general | solution.py:51
  507.9 14.8 %select_reduce_fusion.2 = f32[4096]{0:T(1024)S(1)} fusion(pred[512]{0:T(512)(128)(4,1)S(1)} %add_compare_fusion.2, f32[4,512]{1,0:T(4,128)S(1)} %get-tuple-element.317, f32[4,512,4096]{2,1,0:T(8,128)} %get-tuple-element.318, pred[4096]{0:T(1024)(128)(4,1)S(1)} %get-tuple-element.374), kind=kLoop, calls=%fused_computation.21.clone.1 | loop fusion | flops 41938944 | bytes 33583616 | tf_op jit(solution)/shard_map/while/body/eval_jaxpr/reduce_sum | solution.py:65
  523.0 14.1 %fusion.88 = bf16[4,64,512]{2,1,0:T(8,128)(2,1)S(1)} fusion(bf16[4096,4,64]{0,2,1:T(8,128)(2,1)S(1)} %bitcast.126, f32[4,512]{1,0:T(4,128)S(1)} %get-tuple-element.317, f32[4,512,4096]{2,1,0:T(8,128)} %get-tuple-element.318, pred[4096]{0:T(1024)(128)(4,1)S(1)} %get-tuple-element.374), kind=kOutput, calls=%fused_computation.27.clone.1 | convolution fusion | flops 1107427328 | bytes 35926016 | tf_op jit(solution)/shard_map/while/body/eval_jaxpr/hqk,khd->qhd/dot_general | solution.py:56
  537.8 2.6 constant_dynamic-slice_fusion.12
  540.4 14.1 %fusion.87 = (f32[4,512]{1,0:T(4,128)S(1)}, f32[4,512,4096]{2,1,0:T(8,128)}) fusion(pred[4096]{0:T(1024)(128)(4,1)S(1)} %get-tuple-element.374, bf16[512,4,64]{0,2,1:T(8,128)(2,1)S(1)} %bitcast.139, bf16[4096,4,64]{0,2,1:T(8,128)(2,1)S(1)} %bitcast.127), kind=kOutput, calls=%fused_computation.24.clone.1 | convolution fusion | flops 1098905600 | bytes 35926016 | tf_op jit(solution)/shard_map/while/body/eval_jaxpr/qhd,khd->hqk/dot_general | solution.py:51
  555.2 14.8 %select_reduce_fusion.2 = f32[4096]{0:T(1024)S(1)} fusion(pred[512]{0:T(512)(128)(4,1)S(1)} %add_compare_fusion.2, f32[4,512]{1,0:T(4,128)S(1)} %get-tuple-element.317, f32[4,512,4096]{2,1,0:T(8,128)} %get-tuple-element.318, pred[4096]{0:T(1024)(128)(4,1)S(1)} %get-tuple-element.374), kind=kLoop, calls=%fused_computation.21.clone.1 | loop fusion | flops 41938944 | bytes 33583616 | tf_op jit(solution)/shard_map/while/body/eval_jaxpr/reduce_sum | solution.py:65
  570.2 14.1 %fusion.88 = bf16[4,64,512]{2,1,0:T(8,128)(2,1)S(1)} fusion(bf16[4096,4,64]{0,2,1:T(8,128)(2,1)S(1)} %bitcast.126, f32[4,512]{1,0:T(4,128)S(1)} %get-tuple-element.317, f32[4,512,4096]{2,1,0:T(8,128)} %get-tuple-element.318, pred[4096]{0:T(1024)(128)(4,1)S(1)} %get-tuple-element.374), kind=kOutput, calls=%fused_computation.27.clone.1 | convolution fusion | flops 1107427328 | bytes 35926016 | tf_op jit(solution)/shard_map/while/body/eval_jaxpr/hqk,khd->qhd/dot_general | solution.py:56
  585.0 2.6 constant_dynamic-slice_fusion.12
  587.7 14.1 %fusion.87 = (f32[4,512]{1,0:T(4,128)S(1)}, f32[4,512,4096]{2,1,0:T(8,128)}) fusion(pred[4096]{0:T(1024)(128)(4,1)S(1)} %get-tuple-element.374, bf16[512,4,64]{0,2,1:T(8,128)(2,1)S(1)} %bitcast.139, bf16[4096,4,64]{0,2,1:T(8,128)(2,1)S(1)} %bitcast.127), kind=kOutput, calls=%fused_computation.24.clone.1 | convolution fusion | flops 1098905600 | bytes 35926016 | tf_op jit(solution)/shard_map/while/body/eval_jaxpr/qhd,khd->hqk/dot_general | solution.py:51
  602.5 14.8 %select_reduce_fusion.2 = f32[4096]{0:T(1024)S(1)} fusion(pred[512]{0:T(512)(128)(4,1)S(1)} %add_compare_fusion.2, f32[4,512]{1,0:T(4,128)S(1)} %get-tuple-element.317, f32[4,512,4096]{2,1,0:T(8,128)} %get-tuple-element.318, pred[4096]{0:T(1024)(128)(4,1)S(1)} %get-tuple-element.374), kind=kLoop, calls=%fused_computation.21.clone.1 | loop fusion | flops 41938944 | bytes 33583616 | tf_op jit(solution)/shard_map/while/body/eval_jaxpr/reduce_sum | solution.py:65
  617.5 14.1 %fusion.88 = bf16[4,64,512]{2,1,0:T(8,128)(2,1)S(1)} fusion(bf16[4096,4,64]{0,2,1:T(8,128)(2,1)S(1)} %bitcast.126, f32[4,512]{1,0:T(4,128)S(1)} %get-tuple-element.317, f32[4,512,4096]{2,1,0:T(8,128)} %get-tuple-element.318, pred[4096]{0:T(1024)(128)(4,1)S(1)} %get-tuple-element.374), kind=kOutput, calls=%fused_computation.27.clone.1 | convolution fusion | flops 1107427328 | bytes 35926016 | tf_op jit(solution)/shard_map/while/body/eval_jaxpr/hqk,khd->qhd/dot_general | solution.py:56
  632.7 22.9 %psum.15 = f32[512]{0:T(512)S(1)} all-reduce(f32[512]{0:T(512)S(1)} %reduce_sum.109), channel_id=1, replica_groups=mesh['doc'=4,'seq'=8] {'seq'}, use_global_device_ids=true, to_apply=%region_20.21 | all-reduce | flops 512 | bytes 4096 | tf_op jit(solution)/shard_map/psum | solution.py:137
  658.7 3.2 fusion.34
  (108 shorter events, 53.3 us)
Async XLA Ops:
  0.6 59.5 %copy-start = (bf16[768,1536]{1,0:T(8,128)(2,1)S(1)}, bf16[768,1536]{1,0:T(8,128)(2,1)}, u32[]{:S(2)}) copy-start(bf16[768,1536]{1,0:T(8,128)(2,1)} %param.17) | copy-start | bytes 7077892
  55.7 3.9 copy-start.4
  55.7 361.5 %all-to-all-start.1 = ((bf16[32,16,2,8,768]{4,3,2,1,0:T(8,128)(2,1)}), bf16[32,16,2,8,768]{4,3,2,1,0:T(8,128)(2,1)}, u32[]{:S(2)}, u32[]{:S(2)}) async-start(bf16[32,16,2,8,768]{4,3,2,1,0:T(8,128)(2,1)} %bitcast.129), calls=%async_computation.1 | async-start | bytes 25165824 | tf_op jit(solution)/shard_map/all_to_all | solution.py:114
  61.6 1.2 copy-start.2
  62.9 6.9 %copy-start.8 = (s32[1,512]{1,0:T(1,128)S(1)}, s32[1,512]{1,0:T(1,128)}, u32[]{:S(2)}) copy-start(s32[1,512]{1,0:T(1,128)} %param.15) | copy-start | bytes 6148
  62.9 295.2 %copy-start.9 = (bf16[768,768]{1,0:T(8,128)(2,1)S(1)}, bf16[768,768]{1,0:T(8,128)(2,1)}, u32[]{:S(2)}) copy-start(bf16[768,768]{1,0:T(8,128)(2,1)} %param.16) | copy-start | bytes 3538948
  64.1 317.3 %collective-permute-start = (bf16[256,1536]{1,0:T(8,128)(2,1)}, bf16[256,1536]{1,0:T(8,128)(2,1)}, u32[]{:S(2)}, u32[]{:S(2)}) collective-permute-start(bf16[256,1536]{1,0:T(8,128)(2,1)} %get-tuple-element.193), channel_id=1, source_target_pairs={{0,1},{1,2},{2,3},{3,4},{4,5},{5,6},{6,7},{8,9},{9,10},{10,11},{11... | collective-permute-start | bytes 2359304 | tf_op jit(solution)/shard_map/ppermute | solution.py:18
  68.5 313.0 %collective-permute-start.1 = (bf16[256,1536]{1,0:T(8,128)(2,1)}, bf16[256,1536]{1,0:T(8,128)(2,1)}, u32[]{:S(2)}, u32[]{:S(2)}) collective-permute-start(bf16[256,1536]{1,0:T(8,128)(2,1)} %get-tuple-element.194), channel_id=1, source_target_pairs={{1,0},{2,1},{3,2},{4,3},{5,4},{6,5},{7,6},{9,8},{10,9},{11,10},{12... | collective-permute-start | bytes 2359304 | tf_op jit(solution)/shard_map/ppermute | solution.py:21
  359.9 21.6 %copy-start.3 = (bf16[512,1536]{1,0:T(8,128)(2,1)S(1)}, bf16[512,1536]{1,0:T(8,128)(2,1)}, u32[]{:S(2)}) copy-start(bf16[512,1536]{1,0:T(8,128)(2,1)} %copy-done.2) | copy-start | bytes 4718596
  412.9 3.1 copy-start.10
  415.7 1.2 copy-start.5
  490.5 165.1 %copy-start.7 = (s32[1024]{0:T(1024)S(1)}, s32[1024]{0:T(1024)}, u32[]{:S(2)}) copy-start(s32[1024]{0:T(1024)} %pad_clamp_fusion) | copy-start | bytes 12292
  632.3 26.3 %copy-start.6 = (bf16[512,768]{1,0:T(8,128)(2,1)S(1)}, bf16[512,768]{1,0:T(8,128)(2,1)}, u32[]{:S(2)}) copy-start(bf16[512,768]{1,0:T(8,128)(2,1)} %copy-done.5) | copy-start | bytes 2359300
  655.6 6.3 copy-start.1
where the time goes:
time: 664 us; the launch traced here: 662 us
  blocking collectives  325 us (49%)
  local copies, waits for them, and re-layouts  161 us (24%)
  matrix products  109 us (16%)
  other arithmetic  55.4 us (8%)
  starting transfers between devices  9.53 us (1%)
    psum x1, blocking collectives, local(): length = lax.psum(local_count, 'seq')  288 us
    dot_general x6, matrix products, head_group(): jnp.einsum('qhd,khd->hqk', query_heads, key_heads, preferred_element_type...  49.9 us
    dot_general x6, matrix products, head_group(): jnp.einsum('hqk,khd->qhd', weights.astype(jnp.bfloat16), value_heads, pre...  49.4 us
    reduce_sum x3, other arithmetic, head_group(): jnp.sum(jnp.where(weigh[None, :, None], weights, 0.0), axis=(0, 1))  44.4 us
    unnamed x24, local copies, waits for them, and re-layouts  27.4 us
    psum x1, blocking collectives, local(): slot_total = lax.psum(local_mass, 'seq')  22.9 us
    gather x1, local copies, waits for them, and re-layouts, local(): code_cache[lax.all_to_all(request, ('doc', 'seq'), split_axis=0, concat_a...  17.9 us
    scatter x2, local copies, waits for them, and re-layouts, local(): jnp.zeros((devices, capacity), jnp.bool_).at[owner_dev, slot_rank].set(True)  17.7 us
  transfers between devices with their start and end apart: 3, of which 0 were waited for; matrix products, arithmetic and copies ran while one was open for 9% of the time, Pallas kernels for 0%

commit v1 on v0

v1 whole, which is shorter than its diff:
```python
import functools
import math

import jax
import jax.numpy as jnp
from jax import lax
from jax.experimental import pallas as pl
from jax.experimental.pallas import tpu as pltpu
from jax.sharding import PartitionSpec as P

HEADS = 12
HEAD = 64
HALF_WIN = 256
DESC = 8
GROUPS = 4
EXP2_SCALE = math.log2(math.e) / math.sqrt(HEAD)
F32 = jnp.float32
BF16 = jnp.bfloat16
NT = (((1,), (1,)), ((), ()))


def layer_norm(values):
    centered = values - jnp.mean(values, axis=-1, keepdims=True)
    spread = jnp.mean(centered * centered, axis=-1, keepdims=True)
    return centered * lax.rsqrt(spread + 1e-05)


def window_kernel(valid_ref, q_ref, kl_ref, ko_ref, kh_ref, vl_ref, vo_ref, vh_ref, o_ref, bias):
    rows = q_ref.shape[0]
    half = HALF_WIN
    blocks = rows // half
    width = 3 * half

    @pl.when(pl.program_id(0) == 0)
    def _():
        for b in range(blocks):
            i = lax.broadcasted_iota(jnp.int32, (half, width), 0)
            j = lax.broadcasted_iota(jnp.int32, (half, width), 1)
            ok = valid_ref[:, b * half : b * half + width] > 0.0
            allowed = (j >= i) & (j <= i + 2 * half) & (ok | (j == i + half))
            bias[b] = jnp.where(allowed, 0.0, -1e30)

    k = jnp.concatenate([kl_ref[...], ko_ref[...], kh_ref[...]], axis=0)
    v = jnp.concatenate([vl_ref[...], vo_ref[...], vh_ref[...]], axis=0)
    v = jnp.concatenate([v, jnp.ones_like(v)], axis=1)
    lane = lax.broadcasted_iota(jnp.int32, (half, 2 * HEAD), 1)
    for b in range(blocks):
        q = q_ref[b * half : (b + 1) * half, :]
        kb = k[b * half : b * half + width]
        vb = v[b * half : b * half + width]
        outs = []
        for h in range(2):
            mine = (lane >= h * HEAD) & (lane < (h + 1) * HEAD)
            s = lax.dot_general(
                jnp.where(mine, q, jnp.zeros_like(q)), kb, NT, preferred_element_type=F32
            )
            e = jnp.exp2(s * EXP2_SCALE + bias[b])
            o = jnp.dot(e.astype(BF16), vb, preferred_element_type=F32)
            outs.append(o[:, : 2 * HEAD] / o[:, 2 * HEAD :])
        o_ref[b * half : (b + 1) * half, :] = jnp.where(lane < HEAD, outs[0], outs[1]).astype(BF16)


def window_attend(valid, query, low, own, high):
    rows, width = query.shape
    pairs = width // (2 * HEAD)
    span = rows + 2 * HALF_WIN

    def cols(r, first):
        return pl.BlockSpec((r, 2 * HEAD), lambda p: (0, p + first))

    return pl.pallas_call(
        window_kernel,
        grid=(pairs,),
        out_shape=jax.ShapeDtypeStruct((rows, width), BF16),
        in_specs=[
            pl.BlockSpec((1, span), lambda p: (0, 0)),
            cols(rows, 0),
            cols(HALF_WIN, 0),
            cols(rows, 0),
            cols(HALF_WIN, 0),
            cols(HALF_WIN, pairs),
            cols(rows, pairs),
            cols(HALF_WIN, pairs),
        ],
        out_specs=cols(rows, 0),
        scratch_shapes=[pltpu.VMEM((rows // HALF_WIN, HALF_WIN, 3 * HALF_WIN), F32)],
        compiler_params=pltpu.CompilerParams(vmem_limit_bytes=48 * 1024 * 1024),
        cost_estimate=pl.CostEstimate(
            flops=8 * rows * 3 * HALF_WIN * width,
            bytes_accessed=8 * rows * width,
            transcendentals=rows * 3 * HALF_WIN * HEADS,
        ),
    )(valid, query, low, own, high, low, own, high)


def cross_kernel(chunk, weigh_ref, q_ref, k_ref, v_ref, o_ref, mass_ref):
    tile = q_ref.shape[0]
    keys, wide = k_ref.shape
    heads = (wide - HEAD) // HEAD
    lane = lax.broadcasted_iota(jnp.int32, (tile, wide), 1)
    q = q_ref[...]
    q = jnp.concatenate([jnp.zeros((tile, HEAD), BF16), q], axis=1)

    @pl.when(pl.program_id(0) == 0)
    def _():
        mass_ref[...] = jnp.zeros_like(mass_ref)

    context = jnp.zeros((tile, wide), F32)
    for h in range(heads):
        qh = jnp.where((lane >= (h + 1) * HEAD) & (lane < (h + 2) * HEAD), q, jnp.zeros_like(q))
        parts = []
        o = jnp.zeros((tile, wide), F32)
        for c in range(0, keys, chunk):
            s = lax.dot_general(qh, k_ref[c : c + chunk, :], NT, preferred_element_type=F32)
            e = jnp.exp2(s * EXP2_SCALE)
            o += jnp.dot(e.astype(BF16), v_ref[c : c + chunk, :], preferred_element_type=F32)
            parts.append(e)
        inverse = 1.0 / o[:, heads * HEAD : heads * HEAD + 1]
        context = jnp.where((lane >= h * HEAD) & (lane < (h + 1) * HEAD), o * inverse, context)
        weight = inverse * weigh_ref[...]
        for c, e in zip(range(0, keys, chunk), parts):
            mass_ref[:, c : c + chunk] += jnp.sum(
                (e * weight).reshape(tile // 8, 8, chunk), axis=0
            )
    o_ref[...] = context[:, : heads * HEAD].astype(BF16)


def cross_attend(weigh, query, key_rows, value_rows):
    rows, width = query.shape
    keys, wide = key_rows.shape
    tile = 256
    return pl.pallas_call(
        functools.partial(cross_kernel, 512),
        grid=(rows // tile,),
        out_shape=(
            jax.ShapeDtypeStruct((rows, width), BF16),
            jax.ShapeDtypeStruct((8, keys), F32),
        ),
        in_specs=[
            pl.BlockSpec((tile, 1), lambda i: (i, 0)),
            pl.BlockSpec((tile, width), lambda i: (i, 0)),
            pl.BlockSpec((keys, wide), lambda i: (0, 0)),
            pl.BlockSpec((keys, wide), lambda i: (0, 0)),
        ],
        out_specs=(
            pl.BlockSpec((tile, width), lambda i: (i, 0)),
            pl.BlockSpec((8, keys), lambda i: (0, 0)),
        ),
        compiler_params=pltpu.CompilerParams(vmem_limit_bytes=48 * 1024 * 1024),
        cost_estimate=pl.CostEstimate(
            flops=16 * rows * keys * width,
            bytes_accessed=4 * keys * wide + 4 * rows * width,
            transcendentals=3 * rows * keys,
        ),
    )(weigh, query, key_rows, value_rows)


def local(
    hidden, token_ids, w_query, w_keyval, w_out, x_query, x_out, shortlist, code_row, code_cache
):
    doc_hidden = hidden[0]
    doc_tokens = token_ids[0]
    tok_rows, width = doc_hidden.shape
    seq_count = lax.axis_size("seq")
    doc_count = lax.axis_size("doc")
    devices = seq_count * doc_count
    across = seq_count // GROUPS
    seq_index = lax.axis_index("seq")
    doc_index = lax.axis_index("doc")
    me = doc_index * seq_count + seq_index
    group = seq_index // across
    cand_count = shortlist.shape[1]
    code_dev = code_cache.shape[0]
    capacity = 8 * cand_count // (5 * devices)
    slots = devices * capacity
    part = width // GROUPS

    cache_rows = code_row[shortlist[0]]
    relative = [cache_rows]
    for r in range(1, doc_count):
        relative.append(
            lax.ppermute(cache_rows, "doc", [(i, (i + r) % doc_count) for i in range(doc_count)])
        )
    relative = jnp.stack(relative)
    docs = jnp.arange(doc_count, dtype=jnp.int32)
    source = (doc_index - docs) % doc_count
    rows_of = jnp.sum(
        jnp.where((source[None, :] == docs[:, None])[:, :, None], relative[None], 0), axis=1
    )
    order = jnp.arange(cand_count, dtype=jnp.int32)
    before = (order[:, None] < order[None, :]).astype(BF16)
    held = rows_of // code_dev == me
    rank = jnp.dot(held.astype(BF16), before, preferred_element_type=F32).astype(jnp.int32)
    slot = jnp.arange(capacity, dtype=jnp.int32)
    request = jnp.sum(
        jnp.where(
            held[:, None, :] & (rank[:, None, :] == slot[None, :, None]),
            (rows_of % code_dev)[:, None, :],
            0,
        ),
        axis=2,
    )
    picked = code_cache[request.reshape(-1)]
    picked = picked.reshape(doc_count, capacity, 2, across, DESC // across, GROUPS, part)
    picked = jnp.flip(picked, axis=2).transpose(0, 5, 3, 4, 1, 2, 6)
    picked = picked.reshape(devices, DESC // across, capacity, 2 * part)
    arrived = lax.all_to_all(picked, ("doc", "seq"), split_axis=0, concat_axis=0, tiled=True)

    owner = cache_rows // code_dev
    onehot = (owner[:, None] == jnp.arange(devices, dtype=jnp.int32)[None, :]).astype(BF16)
    ahead = jnp.dot(before.T, onehot, preferred_element_type=F32)
    slot_rank = jnp.sum(ahead * onehot, axis=1).astype(jnp.int32)
    slot_index = owner * capacity + slot_rank
    choose = (slot_index[:, None] == jnp.arange(slots, dtype=jnp.int32)[None, :]).astype(BF16)

    normed = layer_norm(doc_hidden.astype(F32)).astype(BF16)
    query = jnp.dot(normed, w_query, preferred_element_type=F32).astype(BF16)
    keyval = jnp.dot(normed, w_keyval, preferred_element_type=F32).astype(BF16)
    up = [(i, i + 1) for i in range(seq_count - 1)]
    down = [(i + 1, i) for i in range(seq_count - 1)]
    live = (doc_tokens != 0).astype(F32)
    low_live = lax.ppermute(live[tok_rows - HALF_WIN :], "seq", up)
    high_live = lax.ppermute(live[:HALF_WIN], "seq", down)
    low = lax.ppermute(keyval[tok_rows - HALF_WIN :], "seq", up)
    high = lax.ppermute(keyval[:HALF_WIN], "seq", down)
    length = lax.psum(jnp.sum((doc_tokens != 0).astype(jnp.int32)), "seq")
    valid = jnp.concatenate([low_live, live, high_live])[None]
    context = window_attend(valid, query, low, keyval, high)
    middle = (
        doc_hidden.astype(F32) + jnp.dot(context, w_out, preferred_element_type=F32)
    ).astype(BF16)
    middle_wide = middle.astype(F32)
    cross_normed = layer_norm(middle_wide).astype(BF16)
    cross_query = jnp.dot(cross_normed, x_query, preferred_element_type=F32).astype(BF16)

    def turn(r):
        return [
            (i, (i // across + r) % GROUPS * across + i % across) for i in range(seq_count)
        ]

    def piece(array, g):
        return lax.dynamic_slice_in_dim(array, g * part, part, axis=1)

    queries = [piece(cross_query, group)]
    for r in range(1, GROUPS):
        queries.append(
            lax.ppermute(piece(cross_query, (group + r) % GROUPS), "seq", turn(r))
        )

    arrived = arrived.transpose(1, 0, 2, 3).reshape(DESC // across, slots, 2 * part)
    own_rows = jnp.einsum("cs,tsf->tcf", choose, arrived, preferred_element_type=F32).astype(BF16)
    own_rows = own_rows.reshape(DESC // across * cand_count, 2 * part)
    all_rows = [own_rows]
    for r in range(1, across):
        step = [(i, i // across * across + (i % across + r) % across) for i in range(seq_count)]
        all_rows.append(lax.ppermute(own_rows, "seq", step))
    all_rows = jnp.concatenate(all_rows)
    column = jnp.arange(part + HEAD)
    value_rows = jnp.where(
        column[None, :] < part, all_rows[:, : part + HEAD], jnp.ones((), BF16)
    )
    key_rows = all_rows[:, part - HEAD :]

    mass = 0.0
    returned = [None] * GROUPS
    for r in (2, 1, 3, 0):
        origin = (group - r) % GROUPS * across + seq_index % across
        position = origin * tok_rows + jnp.arange(tok_rows, dtype=jnp.int32)
        weigh = (position < length).astype(F32)[:, None]
        piece_context, piece_mass = cross_attend(weigh, queries[r], key_rows, value_rows)
        mass = mass + piece_mass
        returned[r] = (
            lax.ppermute(piece_context, "seq", turn(GROUPS - r)) if r else piece_context
        )
    total = middle_wide
    for r in range(GROUPS):
        rows = lax.dynamic_slice_in_dim(x_out, (group + r) % GROUPS * part, part, axis=0)
        total = total + jnp.dot(returned[r], rows, preferred_element_type=F32)
    refined = total.astype(BF16)
    local_mass = jnp.sum(mass.reshape(8, DESC, cand_count), axis=(0, 1))
    cand_mass = lax.psum(local_mass, "seq")
    cand_score = cand_count * cand_mass / (HEADS * length.astype(F32))
    return (refined[None], cand_score[None])


def solution(mesh):
    return jax.shard_map(
        local,
        mesh=mesh,
        in_specs=(
            P("doc", "seq", None),
            P("doc", "seq"),
            P(),
            P(),
            P(),
            P(),
            P(),
            P("doc", None),
            P(),
            P(("doc", "seq"), None, None, None),
        ),
        out_specs=(P("doc", "seq", None), P("doc", None)),
        check_vma=False,
    )
```

time: 664 us -> 229 us (0.34)
  blocking collectives: 325 us -> 64.6 us
  local copies, waits for them, and re-layouts: 161 us -> 52.2 us
  matrix products: 109 us -> 12.7 us
  other arithmetic: 55.4 us -> 6.6 us
  Pallas kernels: 0 us -> 31.9 us
  waiting for transfers between devices: 0.01 us -> 30.3 us
  starting transfers between devices: 9.53 us -> 27.1 us
    psum x2, blocking collectives: 311 us -> 64.6 us  [the longest x1 47 us: local(): length = lax.psum(jnp.sum((doc_tokens != 0).astype(jnp.int32)), 'seq')]
    dot_general x17 -> x11, matrix products: 109 us -> 12.7 us  [the longest x4 3.34 us: local(): total = total + jnp.dot(returned[r], rows, preferred_element_type=F32)]
    reduce_sum x7 -> x5, other arithmetic: 45.2 us -> 0.99 us  [the longest x1 0.64 us: local(): length = lax.psum(jnp.sum((doc_tokens != 0).astype(jnp.int32)), 'seq')]
    another operation x5 -> x4, local copies, waits for them, and re-layouts: 36.5 us -> 0.01 us  [local(): relative = jnp.stack(relative)]
    scatter x3 -> x0, local copies, waits for them, and re-layouts: 34.8 us -> none  [the longest x2 17.7 us: local(): jnp.zeros((devices, capacity), jnp.bool_).at[owner_dev, slot_rank].set(True)]
    pallas_call x0 -> x5, Pallas kernels: none -> 31.9 us  [the longest x4 23.5 us: cross_attend(): pl.pallas_call(functools.partial(cross_kernel, 512), grid=(rows // tile,)...]
    ppermute x2 -> x14, waiting for transfers between devices: 0.01 us -> 30.2 us  [the longest x1 18 us: local(): all_rows.append(lax.ppermute(own_rows, 'seq', step))]
    unnamed x24, local copies, waits for them, and re-layouts: 27.4 us -> 2.89 us
  transfers between devices with their start and end apart: 3 -> 15, of which waited for: 0 -> 3; matrix products, arithmetic and copies ran while one was open for 9% -> 8% of each run, Pallas kernels for 0% -> 11%
where the time goes in v1:
time: 229 us; the launch traced here: 227 us
  blocking collectives  64.6 us (28%)
  local copies, waits for them, and re-layouts  52.2 us (23%)
  Pallas kernels  31.9 us (14%)
  waiting for transfers between devices  30.3 us (13%)
  starting transfers between devices  27.1 us (12%)
  matrix products  12.7 us (6%)
  other arithmetic  6.6 us (3%)
    psum x1, blocking collectives, local(): length = lax.psum(jnp.sum((doc_tokens != 0).astype(jnp.int32)), 'seq')  47 us
    pallas_call x4, Pallas kernels, cross_attend(): pl.pallas_call(functools.partial(cross_kernel, 512), grid=(rows // tile,)...  23.5 us
    rev x1, local copies, waits for them, and re-layouts, local(): picked = jnp.flip(picked, axis=2).transpose(0, 5, 3, 4, 1, 2, 6)  19.7 us
    ppermute x1, waiting for transfers between devices, local(): all_rows.append(lax.ppermute(own_rows, 'seq', step))  18 us
    psum x1, blocking collectives, local(): cand_mass = lax.psum(local_mass, 'seq')  17.7 us
    ppermute x3, waiting for transfers between devices, local(): lax.ppermute(piece_context, 'seq', turn(GROUPS - r))  12.3 us
    reshape x2, local copies, waits for them, and re-layouts, local(): picked.reshape(doc_count, capacity, 2, across, DESC // across, GROUPS, part)  10.4 us
    pallas_call x1, Pallas kernels, window_attend(): pl.pallas_call(window_kernel, grid=(pairs,), out_shape=jax.ShapeDtypeStru...  8.41 us
  transfers between devices with their start and end apart: 15, of which 3 were waited for; matrix products, arithmetic and copies ran while one was open for 8% of the time, Pallas kernels for 11%

profile of v1, /device:TPU:0, one launch (start us, length us, event | category | flops | bytes accessed | tf_op | source)
XLA Modules:
  0.0 227.3 jit_solution(2518521227220614603)
XLA Ops:
  1.5 3.5 %gather_fusion = s32[320]{0:T(512)S(1)} fusion(s32[9216]{0:T(1024)} %param.18, s32[1024]{0:T(1024)S(1)} %pad_clamp_fusion.1), kind=kCustom, calls=%fused_computation | custom fusion | bytes 3840 | tf_op jit(solution)/shard_map/gather | solution.py:178
  5.5 2.6 %collective-permute-start.5 = (s32[320]{0:T(512)S(1)}, s32[320]{0:T(512)S(1)}, u32[]{:S(2)}, u32[]{:S(2)}) collective-permute-start(s32[320]{0:T(512)S(1)} %gather_fusion), channel_id=1, source_target_pairs={{0,16},{8,24},{16,0},{24,8},{1,17},{9,25},{17,1},{25,9},{2,18},{10... | collective-permute-start | bytes 3848 | tf_op jit(solution)/shard_map/ppermute | solution.py:182
  8.1 1.4 collective-permute-start.6
  10.1 2.6 %convolution_convert_fusion.ko_ref.vo_ref = bf16[512,1536]{1,0:T(8,128)(2,1)} fusion(bf16[768,1536]{1,0:T(8,128)(2,1)S(1)} %copy-done, bf16[1,512,768]{2,1,0:T(8,128)(2,1)S(1)} %copy-done.4, f32[512]{0:T(512)S(1)} %add_rsqrt_fusion.1, f32[512]{0:T(512)S(1)} %broadcast_multiply_fusion.1), kind=kOutput, calls=%fused_computation.2 | convolution fusion | flops 1210318848 | bytes 4722688 | tf_op jit(solution)/shard_map/dot_general | solution.py:218
  13.4 4.9 %gather_fusion.1 = bf16[64,2,8,768]{3,2,1,0:T(8,128)(2,1)} fusion(bf16[288,2,8,768]{3,2,1,0:T(8,128)(2,1)} %param.19, s32[1024]{0:T(1024)S(1)} %pad_clamp_fusion), kind=kCustom, calls=%fused_computation.1 | custom fusion | bytes 3145984 | tf_op jit(solution)/shard_map/gather | solution.py:203
  18.3 5.3 %reshape.236 = bf16[4,16,2,2,4,4,192]{6,5,4,3,2,1,0:T(4,128)(2,1)} reshape(bf16[64,2,8,768]{3,2,1,0:T(8,128)(2,1)} %gather_fusion.1) | data formatting | bytes 3145728 | tf_op jit(solution)/shard_map/reshape | solution.py:204
  23.5 5.1 %copy.19 = bf16[4,16,2,2,4,4,192]{6,2,1,4,3,5,0:T(2,128)(2,1)} copy(bf16[4,16,2,2,4,4,192]{6,5,4,3,2,1,0:T(4,128)(2,1)} %reshape.236) | data formatting | bytes 3145728 | tf_op jit(solution)/shard_map/reshape | solution.py:204
  28.6 19.7 %rev.4 = bf16[4,16,2,2,4,4,192]{6,2,1,4,3,5,0:T(2,128)(2,1)} reverse(bf16[4,16,2,2,4,4,192]{6,2,1,4,3,5,0:T(2,128)(2,1)} %copy.19), dimensions={2} | reverse | bytes 3145728 | tf_op jit(solution)/shard_map/jit(_flip)/rev | solution.py:205
  48.4 5.5 %reshape.237 = bf16[32,4,16,384]{3,2,1,0:T(8,128)(2,1)} reshape(bf16[4,4,2,4,16,2,192]{6,5,4,3,2,1,0:T(2,128)(2,1)} %bitcast.51) | data formatting | bytes 3145728 | tf_op jit(solution)/shard_map/reshape | solution.py:206
  53.8 5.0 %all-to-all-start = ((bf16[32,4,16,384]{3,2,1,0:T(8,128)(2,1)}), bf16[32,4,16,384]{3,2,1,0:T(8,128)(2,1)}, u32[]{:S(2)}, u32[]{:S(2)}) async-start(bf16[32,4,16,384]{3,2,1,0:T(8,128)(2,1)} %reshape.237), calls=%async_computation | async-start | bytes 3145728 | tf_op jit(solution)/shard_map/all_to_all | solution.py:207
  58.8 2.6 %fusion.55 = (bf16[256,1536]{1,0:T(8,128)(2,1)}, bf16[256,1536]{1,0:T(8,128)(2,1)}) fusion(bf16[512,1536]{1,0:T(8,128)(2,1)} %convolution_convert_fusion.ko_ref.vo_ref), kind=kLoop, calls=%fused_computation.106 | loop fusion | bytes 3145728 | tf_op jit(solution)/shard_map/slice | solution.py:225
  61.5 4.5 %collective-permute-start.2 = (bf16[256,1536]{1,0:T(8,128)(2,1)}, bf16[256,1536]{1,0:T(8,128)(2,1)}, u32[]{:S(2)}, u32[]{:S(2)}) collective-permute-start(bf16[256,1536]{1,0:T(8,128)(2,1)} %get-tuple-element.21), channel_id=1, source_target_pairs={{0,1},{1,2},{2,3},{3,4},{4,5},{5,6},{6,7},{8,9},{9,10},{10,11},{11... | collective-permute-start | bytes 2359304 | tf_op jit(solution)/shard_map/ppermute | solution.py:224
  67.3 4.5 %collective-permute-start = (f32[256]{0:T(256)S(1)}, f32[256]{0:T(256)S(1)}, u32[]{:S(2)}, u32[]{:S(2)}) collective-permute-start(f32[256]{0:T(256)S(1)} %bitcast.57), channel_id=1, source_target_pairs={{0,1},{1,2},{2,3},{3,4},{4,5},{5,6},{6,7},{8,9},{9,10},{10,11},{11... | collective-permute-start | bytes 3080 | tf_op jit(solution)/shard_map/ppermute | solution.py:222
  73.8 47.0 %psum.14 = s32[]{:T(128)} all-reduce(s32[]{:T(128)} %fusion.44), channel_id=1, replica_groups=mesh['doc'=4,'seq'=8] {'seq'}, use_global_device_ids=true, to_apply=%region_3.4 | all-reduce | flops 1 | bytes 8 | tf_op jit(solution)/shard_map/psum | solution.py:226
  123.1 1.4 fusion.37.weigh_ref
  124.5 3.2 %convolution_convert_fusion.3.q_ref = bf16[512,768]{1,0:T(8,128)(2,1)} fusion(bf16[768,768]{1,0:T(8,128)(2,1)} %param.12, bf16[1,512,768]{2,1,0:T(8,128)(2,1)} %param.10, f32[512]{0:T(512)S(1)} %add_rsqrt_fusion.1, f32[512]{0:T(512)S(1)} %broadcast_multiply_fusion.1), kind=kOutput, calls=%fused_computation.27 | convolution fusion | flops 605945856 | bytes 2756608 | tf_op jit(solution)/shard_map/dot_general | solution.py:217
  128.5 1.4 copy-done.1
  131.0 8.4 %shard_map.113 = bf16[512,768]{1,0:T(8,128)(2,1)S(1)} custom-call(f32[1,1024]{1,0:T(1,128)S(1)} %bitcast.50, bf16[512,768]{1,0:T(8,128)(2,1)S(1)} %copy-done.3, bf16[256,1536]{1,0:T(8,128)(2,1)} %collective-permute-done.2.kl_ref.vl_ref, bf16[512,1536]{1,0:T(8,128)(2,1)S(1)} %copy-done.1, bf16[256,1536]{1,0:T(8,128)(2,1)} %collective-permute-done.3.kh_ref.vh_ref, ...), custom_call_target="tpu_custom_call" | custom-call | flops 2415919104 | bytes 3145728 | tf_op jit(solution)/shard_map/pallas_call | solution.py:71
  139.5 1.7 convert_reduce_fusion
  141.1 1.6 copy.20
  145.6 2.0 collective-permute-start.8
  147.6 18.0 %collective-permute-done.7 = bf16[1280,384]{1,0:T(8,128)(2,1)S(1)} collective-permute-done((bf16[1280,384]{1,0:T(8,128)(2,1)S(1)}, bf16[1280,384]{1,0:T(8,128)(2,1)S(1)}, u32[]{:S(2)}, u32[]{:S(2)}) %collective-permute-start.7) | collective-permute-done | bytes 983072 | tf_op jit(solution)/shard_map/ppermute | solution.py:256
  165.8 5.9 %shard_map.114 = (bf16[512,192]{1,0:T(8,128)(2,1)S(1)}, f32[8,2560]{1,0:T(8,128)S(1)}) custom-call(f32[512,1]{1,0:T(8,128)S(1)} %fusion.35.weigh_ref, bf16[512,192]{1,0:T(8,128)(2,1)S(1)} %get-tuple-element.25.q_ref, bf16[2560,256]{1,0:T(8,128)(2,1)S(1)} %get-tuple-element.19.k_ref, bf16[2560,256]{1,0:T(8,128)(2,1)S(1)} %get-tuple-element.18.v_ref), custom_call_target="tpu_custom_call" | custom-call | flops 4026531840 | bytes 3014656 | tf_op jit(solution)/shard_map/pallas_call | solution.py:132
  171.7 5.9 %shard_map.117 = (bf16[512,192]{1,0:T(8,128)(2,1)S(1)}, f32[8,2560]{1,0:T(8,128)S(1)}) custom-call(f32[512,1]{1,0:T(8,128)S(1)} %fusion.38.weigh_ref, bf16[512,192]{1,0:T(8,128)(2,1)S(1)} %collective-permute-done.12.q_ref, bf16[2560,256]{1,0:T(8,128)(2,1)S(1)} %get-tuple-element.19.k_ref, bf16[2560,256]{1,0:T(8,128)(2,1)S(1)} %get-tuple-element.18.v_ref), custom_call_target="tpu_custom_call" | custom-call | flops 4026531840 | bytes 3014656 | tf_op jit(solution)/shard_map/pallas_call | solution.py:132
  177.6 5.9 %shard_map.115 = (bf16[512,192]{1,0:T(8,128)(2,1)S(1)}, f32[8,2560]{1,0:T(8,128)S(1)}) custom-call(f32[512,1]{1,0:T(8,128)S(1)} %fusion.36.weigh_ref, bf16[512,192]{1,0:T(8,128)(2,1)S(1)} %collective-permute-done.8.q_ref, bf16[2560,256]{1,0:T(8,128)(2,1)S(1)} %get-tuple-element.19.k_ref, bf16[2560,256]{1,0:T(8,128)(2,1)S(1)} %get-tuple-element.18.v_ref), custom_call_target="tpu_custom_call" | custom-call | flops 4026531840 | bytes 3014656 | tf_op jit(solution)/shard_map/pallas_call | solution.py:132
  183.5 5.9 %shard_map.116 = (bf16[512,192]{1,0:T(8,128)(2,1)S(1)}, f32[8,2560]{1,0:T(8,128)S(1)}) custom-call(f32[512,1]{1,0:T(8,128)S(1)} %copy-done.2, bf16[512,192]{1,0:T(8,128)(2,1)S(1)} %collective-permute-done.10.q_ref, bf16[2560,256]{1,0:T(8,128)(2,1)S(1)} %get-tuple-element.19.k_ref, bf16[2560,256]{1,0:T(8,128)(2,1)S(1)} %get-tuple-element.18.v_ref), custom_call_target="tpu_custom_call" | custom-call | flops 4026531840 | bytes 3014656 | tf_op jit(solution)/shard_map/pallas_call | solution.py:132
  189.5 17.7 %psum.15 = f32[320]{0:T(512)S(1)} all-reduce(f32[320]{0:T(512)S(1)} %reduce_sum.98), channel_id=1, replica_groups=mesh['doc'=4,'seq'=8] {'seq'}, use_global_device_ids=true, to_apply=%region_11.12 | all-reduce | flops 320 | bytes 2560 | tf_op jit(solution)/shard_map/psum | solution.py:281
  207.8 3.8 %collective-permute-start.9 = (bf16[512,192]{1,0:T(8,128)(2,1)S(1)}, bf16[512,192]{1,0:T(8,128)(2,1)S(1)}, u32[]{:S(2)}, u32[]{:S(2)}) collective-permute-start(bf16[512,192]{1,0:T(8,128)(2,1)S(1)} %get-tuple-element.11), channel_id=1, source_target_pairs={{0,6},{1,7},{2,0},{3,1},{4,2},{5,3},{6,4},{7,5},{8,14},{9,15},{10,... | collective-permute-start | bytes 589832 | tf_op jit(solution)/shard_map/ppermute | solution.py:273
  211.6 1.3 fusion.33
  212.9 3.5 %collective-permute-done.9 = bf16[512,192]{1,0:T(8,128)(2,1)S(1)} collective-permute-done((bf16[512,192]{1,0:T(8,128)(2,1)S(1)}, bf16[512,192]{1,0:T(8,128)(2,1)S(1)}, u32[]{:S(2)}, u32[]{:S(2)}) %collective-permute-start.9) | collective-permute-done | bytes 196640 | tf_op jit(solution)/shard_map/ppermute | solution.py:273
  216.8 8.7 %collective-permute-done.11 = bf16[512,192]{1,0:T(8,128)(2,1)S(1)} collective-permute-done((bf16[512,192]{1,0:T(8,128)(2,1)S(1)}, bf16[512,192]{1,0:T(8,128)(2,1)S(1)}, u32[]{:S(2)}, u32[]{:S(2)}) %collective-permute-start.11) | collective-permute-done | bytes 196640 | tf_op jit(solution)/shard_map/ppermute | solution.py:273
  225.9 1.3 fusion.18
  (89 shorter events, 13.7 us)
Async XLA Ops:
  0.6 9.5 %copy-start = (bf16[768,1536]{1,0:T(8,128)(2,1)S(1)}, bf16[768,1536]{1,0:T(8,128)(2,1)}, u32[]{:S(2)}) copy-start(bf16[768,1536]{1,0:T(8,128)(2,1)} %param.13) | copy-start | bytes 7077892
  0.6 8.9 %copy-start.4 = (bf16[1,512,768]{2,1,0:T(8,128)(2,1)S(1)}, bf16[1,512,768]{2,1,0:T(8,128)(2,1)}, u32[]{:S(2)}) copy-start(bf16[1,512,768]{2,1,0:T(8,128)(2,1)} %param.10) | copy-start | bytes 2359300
  5.0 7.7 %collective-permute-start.4 = (s32[320]{0:T(512)S(1)}, s32[320]{0:T(512)S(1)}, u32[]{:S(2)}, u32[]{:S(2)}) collective-permute-start(s32[320]{0:T(512)S(1)} %gather_fusion), channel_id=1, source_target_pairs={{0,8},{8,16},{16,24},{24,0},{1,9},{9,17},{17,25},{25,1},{2,10},{10... | collective-permute-start | bytes 3848 | tf_op jit(solution)/shard_map/ppermute | solution.py:182
  5.5 7.2 %collective-permute-start.5 = (s32[320]{0:T(512)S(1)}, s32[320]{0:T(512)S(1)}, u32[]{:S(2)}, u32[]{:S(2)}) collective-permute-start(s32[320]{0:T(512)S(1)} %gather_fusion), channel_id=1, source_target_pairs={{0,16},{8,24},{16,0},{24,8},{1,17},{9,25},{17,1},{25,9},{2,18},{10... | collective-permute-start | bytes 3848 | tf_op jit(solution)/shard_map/ppermute | solution.py:182
  8.1 4.6 %collective-permute-start.6 = (s32[320]{0:T(512)S(1)}, s32[320]{0:T(512)S(1)}, u32[]{:S(2)}, u32[]{:S(2)}) collective-permute-start(s32[320]{0:T(512)S(1)} %gather_fusion), channel_id=1, source_target_pairs={{0,24},{8,0},{16,8},{24,16},{1,25},{9,1},{17,9},{25,17},{2,26},{10... | collective-permute-start | bytes 3848 | tf_op jit(solution)/shard_map/ppermute | solution.py:182
  53.8 87.3 %all-to-all-start = ((bf16[32,4,16,384]{3,2,1,0:T(8,128)(2,1)}), bf16[32,4,16,384]{3,2,1,0:T(8,128)(2,1)}, u32[]{:S(2)}, u32[]{:S(2)}) async-start(bf16[32,4,16,384]{3,2,1,0:T(8,128)(2,1)} %reshape.237), calls=%async_computation | async-start | bytes 3145728 | tf_op jit(solution)/shard_map/all_to_all | solution.py:207
  58.8 8.4 %copy-start.9 = (s32[1,512]{1,0:T(1,128)S(1)}, s32[1,512]{1,0:T(1,128)}, u32[]{:S(2)}) copy-start(s32[1,512]{1,0:T(1,128)} %param.11) | copy-start | bytes 6148
  61.5 67.0 %collective-permute-start.2 = (bf16[256,1536]{1,0:T(8,128)(2,1)}, bf16[256,1536]{1,0:T(8,128)(2,1)}, u32[]{:S(2)}, u32[]{:S(2)}) collective-permute-start(bf16[256,1536]{1,0:T(8,128)(2,1)} %get-tuple-element.21), channel_id=1, source_target_pairs={{0,1},{1,2},{2,3},{3,4},{4,5},{5,6},{6,7},{8,9},{9,10},{10,11},{11... | collective-permute-start | bytes 2359304 | tf_op jit(solution)/shard_map/ppermute | solution.py:224
  66.0 62.5 %collective-permute-start.3 = (bf16[256,1536]{1,0:T(8,128)(2,1)}, bf16[256,1536]{1,0:T(8,128)(2,1)}, u32[]{:S(2)}, u32[]{:S(2)}) collective-permute-start(bf16[256,1536]{1,0:T(8,128)(2,1)} %get-tuple-element.20), channel_id=1, source_target_pairs={{1,0},{2,1},{3,2},{4,3},{5,4},{6,5},{7,6},{9,8},{10,9},{11,10},{12... | collective-permute-start | bytes 2359304 | tf_op jit(solution)/shard_map/ppermute | solution.py:225
  67.3 61.1 %collective-permute-start = (f32[256]{0:T(256)S(1)}, f32[256]{0:T(256)S(1)}, u32[]{:S(2)}, u32[]{:S(2)}) collective-permute-start(f32[256]{0:T(256)S(1)} %bitcast.57), channel_id=1, source_target_pairs={{0,1},{1,2},{2,3},{3,4},{4,5},{5,6},{6,7},{8,9},{9,10},{10,11},{11... | collective-permute-start | bytes 3080 | tf_op jit(solution)/shard_map/ppermute | solution.py:222
  72.5 55.9 %collective-permute-start.1 = (f32[256]{0:T(256)S(1)}, f32[256]{0:T(256)S(1)}, u32[]{:S(2)}, u32[]{:S(2)}) collective-permute-start(f32[256]{0:T(256)S(1)} %bitcast.56), channel_id=1, source_target_pairs={{1,0},{2,1},{3,2},{4,3},{5,4},{6,5},{7,6},{9,8},{10,9},{11,10},{12... | collective-permute-start | bytes 3080 | tf_op jit(solution)/shard_map/ppermute | solution.py:223
  128.5 1.4 copy-start.1
  129.9 1.1 copy-start.3
  131.0 8.4 %copy-start.5 = (bf16[1,512,768]{2,1,0:T(8,128)(2,1)S(1)}, bf16[1,512,768]{2,1,0:T(8,128)(2,1)}, u32[]{:S(2)}) copy-start(bf16[1,512,768]{2,1,0:T(8,128)(2,1)} %param.10) | copy-start | bytes 2359300
  131.0 8.4 %copy-start.10 = (bf16[768,768]{1,0:T(8,128)(2,1)S(1)}, bf16[768,768]{1,0:T(8,128)(2,1)}, u32[]{:S(2)}) copy-start(bf16[768,768]{1,0:T(8,128)(2,1)} %param.14) | copy-start | bytes 3538948
  142.7 1.1 copy-start.6
  142.7 1.5 copy-start.11
  143.5 22.1 %collective-permute-start.7 = (bf16[1280,384]{1,0:T(8,128)(2,1)S(1)}, bf16[1280,384]{1,0:T(8,128)(2,1)S(1)}, u32[]{:S(2)}, u32[]{:S(2)}) collective-permute-start(bf16[1280,384]{1,0:T(8,128)(2,1)S(1)} %bitcast.53), channel_id=1, source_target_pairs={{0,1},{1,0},{2,3},{3,2},{4,5},{5,4},{6,7},{7,6},{8,9},{9,8},{10,11... | collective-permute-start | bytes 2949128 | tf_op jit(solution)/shard_map/ppermute | solution.py:256
  145.5 26.2 %collective-permute-start.12 = (bf16[512,192]{1,0:T(8,128)(2,1)S(1)}, bf16[512,192]{1,0:T(8,128)(2,1)S(1)}, u32[]{:S(2)}, u32[]{:S(2)}) collective-permute-start(bf16[512,192]{1,0:T(8,128)(2,1)S(1)} %get-tuple-element.22), channel_id=1, source_target_pairs={{0,6},{1,7},{2,0},{3,1},{4,2},{5,3},{6,4},{7,5},{8,14},{9,15},{10,... | collective-permute-start | bytes 589832 | tf_op jit(solution)/shard_map/ppermute | solution.py:247
  145.6 32.0 %collective-permute-start.8 = (bf16[512,192]{1,0:T(8,128)(2,1)S(1)}, bf16[512,192]{1,0:T(8,128)(2,1)S(1)}, u32[]{:S(2)}, u32[]{:S(2)}) collective-permute-start(bf16[512,192]{1,0:T(8,128)(2,1)S(1)} %get-tuple-element.24), channel_id=1, source_target_pairs={{0,2},{1,3},{2,4},{3,5},{4,6},{5,7},{6,0},{7,1},{8,10},{9,11},{10,... | collective-permute-start | bytes 589832 | tf_op jit(solution)/shard_map/ppermute | solution.py:247
  147.6 35.9 %collective-permute-start.10 = (bf16[512,192]{1,0:T(8,128)(2,1)S(1)}, bf16[512,192]{1,0:T(8,128)(2,1)S(1)}, u32[]{:S(2)}, u32[]{:S(2)}) collective-permute-start(bf16[512,192]{1,0:T(8,128)(2,1)S(1)} %get-tuple-element.23), channel_id=1, source_target_pairs={{0,4},{1,5},{2,6},{3,7},{4,0},{5,1},{6,2},{7,3},{8,12},{9,13},{10,... | collective-permute-start | bytes 589832 | tf_op jit(solution)/shard_map/ppermute | solution.py:247
  177.6 5.9 %copy-start.2 = (f32[512,1]{1,0:T(8,128)S(1)}, f32[512,1]{1,0:T(8,128)}, u32[]{:S(2)}) copy-start(f32[512,1]{1,0:T(8,128)} %fusion.37.weigh_ref) | copy-start | bytes 6148
  207.2 9.2 %copy-start.8 = (bf16[768,768]{1,0:T(8,128)(2,1)S(1)}, bf16[768,768]{1,0:T(8,128)(2,1)}, u32[]{:S(2)}) copy-start(bf16[768,768]{1,0:T(8,128)(2,1)} %param.16) | copy-start | bytes 3538948
  207.8 18.1 %collective-permute-start.13 = (bf16[512,192]{1,0:T(8,128)(2,1)S(1)}, bf16[512,192]{1,0:T(8,128)(2,1)S(1)}, u32[]{:S(2)}, u32[]{:S(2)}) collective-permute-start(bf16[512,192]{1,0:T(8,128)(2,1)S(1)} %get-tuple-element.13), channel_id=1, source_target_pairs={{0,2},{1,3},{2,4},{3,5},{4,6},{5,7},{6,0},{7,1},{8,10},{9,11},{10,... | collective-permute-start | bytes 589832 | tf_op jit(solution)/shard_map/ppermute | solution.py:273
  207.8 8.7 %collective-permute-start.9 = (bf16[512,192]{1,0:T(8,128)(2,1)S(1)}, bf16[512,192]{1,0:T(8,128)(2,1)S(1)}, u32[]{:S(2)}, u32[]{:S(2)}) collective-permute-start(bf16[512,192]{1,0:T(8,128)(2,1)S(1)} %get-tuple-element.11), channel_id=1, source_target_pairs={{0,6},{1,7},{2,0},{3,1},{4,2},{5,3},{6,4},{7,5},{8,14},{9,15},{10,... | collective-permute-start | bytes 589832 | tf_op jit(solution)/shard_map/ppermute | solution.py:273
  211.6 14.0 %collective-permute-start.11 = (bf16[512,192]{1,0:T(8,128)(2,1)S(1)}, bf16[512,192]{1,0:T(8,128)(2,1)S(1)}, u32[]{:S(2)}, u32[]{:S(2)}) collective-permute-start(bf16[512,192]{1,0:T(8,128)(2,1)S(1)} %get-tuple-element.12), channel_id=1, source_target_pairs={{0,4},{1,5},{2,6},{3,7},{4,0},{5,1},{6,2},{7,3},{8,12},{9,13},{10,... | collective-permute-start | bytes 589832 | tf_op jit(solution)/shard_map/ppermute | solution.py:273
  216.8 9.1 %copy-start.7 = (bf16[512,768]{1,0:T(8,128)(2,1)S(1)}, bf16[512,768]{1,0:T(8,128)(2,1)}, u32[]{:S(2)}) copy-start(bf16[512,768]{1,0:T(8,128)(2,1)} %get-tuple-element.29) | copy-start | bytes 2359300

commit v2 on v1

--- a/solution.py
+++ b/solution.py
@@ -93,66 +93,209 @@
     )(valid, query, low, own, high, low, own, high)
 
 
-def cross_kernel(chunk, weigh_ref, q_ref, k_ref, v_ref, o_ref, mass_ref):
-    tile = q_ref.shape[0]
-    keys, wide = k_ref.shape
-    heads = (wide - HEAD) // HEAD
-    lane = lax.broadcasted_iota(jnp.int32, (tile, wide), 1)
-    q = q_ref[...]
-    q = jnp.concatenate([jnp.zeros((tile, HEAD), BF16), q], axis=1)
-
-    @pl.when(pl.program_id(0) == 0)
-    def _():
-        mass_ref[...] = jnp.zeros_like(mass_ref)
-
-    context = jnp.zeros((tile, wide), F32)
-    for h in range(heads):
-        qh = jnp.where((lane >= (h + 1) * HEAD) & (lane < (h + 2) * HEAD), q, jnp.zeros_like(q))
-        parts = []
-        o = jnp.zeros((tile, wide), F32)
-        for c in range(0, keys, chunk):
-            s = lax.dot_general(qh, k_ref[c : c + chunk, :], NT, preferred_element_type=F32)
-            e = jnp.exp2(s * EXP2_SCALE)
-            o += jnp.dot(e.astype(BF16), v_ref[c : c + chunk, :], preferred_element_type=F32)
-            parts.append(e)
-        inverse = 1.0 / o[:, heads * HEAD : heads * HEAD + 1]
-        context = jnp.where((lane >= h * HEAD) & (lane < (h + 1) * HEAD), o * inverse, context)
-        weight = inverse * weigh_ref[...]
-        for c, e in zip(range(0, keys, chunk), parts):
-            mass_ref[:, c : c + chunk] += jnp.sum(
-                (e * weight).reshape(tile // 8, 8, chunk), axis=0
-            )
-    o_ref[...] = context[:, : heads * HEAD].astype(BF16)
-
-
-def cross_attend(weigh, query, key_rows, value_rows):
-    rows, width = query.shape
-    keys, wide = key_rows.shape
-    tile = 256
+def gather_kernel(docs, capacity, request_ref, cache_ref, order_ref, out_ref, held, sems):
+    count = docs * capacity
+    step = 2 * DESC
+    part = out_ref.shape[-1] // 2
+
+    def fetch(i):
+        row = pl.multiple_of(request_ref[i] * step, step)
+        return pltpu.make_async_copy(
+            cache_ref.at[pl.ds(row, step)], held.at[pl.ds(i * step, step)], sems.at[i]
+        )
+
+    for i in range(count):
+        fetch(i).start()
+    rows = capacity * step
+    half = capacity * DESC
+    for d in range(docs):
+        for i in range(d * capacity, (d + 1) * capacity):
+            fetch(i).wait()
+        ordered = jnp.dot(
+            order_ref[...], held[d * rows : (d + 1) * rows, :], preferred_element_type=F32
+        ).astype(BF16)
+        for g in range(GROUPS):
+            cols = slice(g * part, (g + 1) * part)
+            out_ref[d, g] = jnp.concatenate([ordered[:half, cols], ordered[half:, cols]], axis=1)
+
+
+def gather_rows(request, cache, capacity):
+    docs = request.shape[0] // capacity
+    codes, pair, desc, width = cache.shape
+    part = width // GROUPS
+    rows = capacity * pair * desc
+    out = jnp.arange(rows)
+    source = out % capacity * (2 * desc) + (1 - out // (desc * capacity)) * desc
+    source = source + out // capacity % desc
+    order = (source[:, None] == out[None, :]).astype(BF16)
     return pl.pallas_call(
-        functools.partial(cross_kernel, 512),
-        grid=(rows // tile,),
-        out_shape=(
-            jax.ShapeDtypeStruct((rows, width), BF16),
-            jax.ShapeDtypeStruct((8, keys), F32),
-        ),
+        functools.partial(gather_kernel, docs, capacity),
+        out_shape=jax.ShapeDtypeStruct((docs, GROUPS, rows // 2, 2 * part), BF16),
         in_specs=[
-            pl.BlockSpec((tile, 1), lambda i: (i, 0)),
-            pl.BlockSpec((tile, width), lambda i: (i, 0)),
-            pl.BlockSpec((keys, wide), lambda i: (0, 0)),
-            pl.BlockSpec((keys, wide), lambda i: (0, 0)),
+            pl.BlockSpec(memory_space=pltpu.SMEM),
+            pl.BlockSpec(memory_space=pl.ANY),
+            pl.BlockSpec(memory_space=pltpu.VMEM),
         ],
-        out_specs=(
-            pl.BlockSpec((tile, width), lambda i: (i, 0)),
-            pl.BlockSpec((8, keys), lambda i: (0, 0)),
-        ),
+        out_specs=pl.BlockSpec(memory_space=pltpu.VMEM),
+        scratch_shapes=[
+            pltpu.VMEM((docs * rows, width), BF16),
+            pltpu.SemaphoreType.DMA((docs * capacity,)),
+        ],
         compiler_params=pltpu.CompilerParams(vmem_limit_bytes=48 * 1024 * 1024),
         cost_estimate=pl.CostEstimate(
-            flops=16 * rows * keys * width,
-            bytes_accessed=4 * keys * wide + 4 * rows * width,
-            transcendentals=3 * rows * keys,
-        ),
-    )(weigh, query, key_rows, value_rows)
+            flops=2 * docs * rows * rows * width,
+            bytes_accessed=4 * docs * rows * width,
+            transcendentals=0,
+        ),
+    )(request, cache.reshape(codes * pair * desc, width), order)
+
+
+def cross_kernel(
+    seq_count,
+    chunk,
+    count_ref,
+    q_ref,
+    k_ref,
+    v_ref,
+    middle_ref,
+    w_ref,
+    o_ref,
+    mass_ref,
+    context,
+    landed,
+    mass,
+    masses,
+    send_sem,
+    recv_sem,
+    mass_send,
+    mass_recv,
+):
+    me = lax.axis_index("seq")
+    across = seq_count // GROUPS
+    group = me // across
+    column = me % across
+    keys, wide = k_ref.shape
+    tile = 256
+    tiles = q_ref.shape[1] // tile
+    part = wide - HEAD
+    heads = part // HEAD
+    lane = lax.broadcasted_iota(jnp.int32, (tile, wide), 1)
+
+    barrier = pltpu.get_barrier_semaphore()
+    for p in range(1, seq_count):
+        pl.semaphore_signal(
+            barrier,
+            inc=1,
+            device_id={"seq": (me + p) % seq_count},
+            device_id_type=pl.DeviceIdType.MESH,
+        )
+    mass[...] = jnp.zeros_like(mass)
+
+    def send_back(r):
+        return pltpu.make_async_remote_copy(
+            src_ref=context.at[r],
+            dst_ref=landed.at[r],
+            send_sem=send_sem.at[r],
+            recv_sem=recv_sem.at[r],
+            device_id={"seq": (group + GROUPS - r) % GROUPS * across + column},
+            device_id_type=pl.DeviceIdType.MESH,
+        )
+
+    def send_mass(p):
+        return pltpu.make_async_remote_copy(
+            src_ref=masses.at[0],
+            dst_ref=masses.at[p],
+            send_sem=mass_send.at[p],
+            recv_sem=mass_recv.at[p],
+            device_id={"seq": (me + p) % seq_count},
+            device_id_type=pl.DeviceIdType.MESH,
+        )
+
+    def work(t, carry):
+        r = (t // tiles + 1) % GROUPS
+        first = pl.multiple_of(t % tiles * tile, tile)
+        q = q_ref[r, pl.ds(first, tile), :]
+        weigh = q[:, 0:1].astype(F32)
+        result = jnp.zeros((tile, wide), F32)
+        for h in range(heads):
+            mine = (lane >= (h + 1) * HEAD) & (lane < (h + 2) * HEAD)
+            qh = jnp.where(mine, q, jnp.zeros_like(q))
+            parts = []
+            o = jnp.zeros((tile, wide), F32)
+            for c in range(0, keys, chunk):
+                s = lax.dot_general(qh, k_ref[c : c + chunk, :], NT, preferred_element_type=F32)
+                e = jnp.exp2(s * EXP2_SCALE)
+                o += jnp.dot(e.astype(BF16), v_ref[c : c + chunk, :], preferred_element_type=F32)
+                parts.append(e)
+            inverse = 1.0 / o[:, part : part + 1]
+            result = jnp.where((lane >= h * HEAD) & (lane < (h + 1) * HEAD), o * inverse, result)
+            weight = inverse * weigh
+            for c, e in zip(range(0, keys, chunk), parts):
+                mass[:, c : c + chunk] += jnp.sum((e * weight).reshape(tile // 8, 8, chunk), axis=0)
+        context[r, pl.ds(first, tile), :] = result[:, :part].astype(BF16)
+
+        @pl.when(t == tiles - 1)
+        def _():
+            pl.semaphore_wait(barrier, seq_count - 1)
+
+        @pl.when((t % tiles == tiles - 1) & (t < (GROUPS - 1) * tiles))
+        def _():
+            send_back(r).start()
+
+        return carry
+
+    lax.fori_loop(0, GROUPS * tiles, work, 0)
+    masses[0, :, :keys] = jnp.sum(mass[...], axis=0, keepdims=True)
+    masses[0, :, keys:] = count_ref[...]
+    for p in range(1, seq_count):
+        send_mass(p).start()
+
+    def weights(r):
+        return w_ref[pl.ds(pl.multiple_of((group + r) % GROUPS * part, part), part), :]
+
+    total = middle_ref[...].astype(F32)
+    total += jnp.dot(context[0], weights(0), preferred_element_type=F32)
+    for r in range(1, GROUPS):
+        send_back(r).wait()
+        total += jnp.dot(landed[r], weights(r), preferred_element_type=F32)
+    o_ref[...] = total.astype(BF16)
+    for p in range(1, seq_count):
+        send_mass(p).wait()
+    mass_ref[...] = jnp.sum(masses[...], axis=0)
+
+
+def cross_attend(seq_count, count, queries, key_rows, value_rows, middle, x_out):
+    groups, rows, wide = queries.shape
+    keys = key_rows.shape[0]
+    part = wide - HEAD
+    vmem = pl.BlockSpec(memory_space=pltpu.VMEM)
+    return pl.pallas_call(
+        functools.partial(cross_kernel, seq_count, 512),
+        out_shape=(
+            jax.ShapeDtypeStruct(middle.shape, BF16),
+            jax.ShapeDtypeStruct((1, keys + 128), F32),
+        ),
+        in_specs=[vmem] * 6,
+        out_specs=(vmem, vmem),
+        scratch_shapes=[
+            pltpu.VMEM((groups, rows, part), BF16),
+            pltpu.VMEM((groups, rows, part), BF16),
+            pltpu.VMEM((8, keys), F32),
+            pltpu.VMEM((seq_count, 1, keys + 128), F32),
+            pltpu.SemaphoreType.DMA((groups,)),
+            pltpu.SemaphoreType.DMA((groups,)),
+            pltpu.SemaphoreType.DMA((seq_count,)),
+            pltpu.SemaphoreType.DMA((seq_count,)),
+        ],
+        compiler_params=pltpu.CompilerParams(
+            vmem_limit_bytes=48 * 1024 * 1024, collective_id=0, has_side_effects=True
+        ),
+        cost_estimate=pl.CostEstimate(
+            flops=16 * groups * rows * keys * part,
+            bytes_accessed=4 * keys * wide + 4 * rows * wide,
+            transcendentals=3 * groups * rows * keys,
+        ),
+    )(count, queries, key_rows, value_rows, middle, x_out)
 
 
 def local(
@@ -200,10 +343,8 @@
         ),
         axis=2,
     )
-    picked = code_cache[request.reshape(-1)]
-    picked = picked.reshape(doc_count, capacity, 2, across, DESC // across, GROUPS, part)
-    picked = jnp.flip(picked, axis=2).transpose(0, 5, 3, 4, 1, 2, 6)
-    picked = picked.reshape(devices, DESC // across, capacity, 2 * part)
+    picked = gather_rows(request.reshape(-1), code_cache, capacity)
+    picked = picked.reshape(devices, DESC // across * capacity, 2 * part)
     arrived = lax.all_to_all(picked, ("doc", "seq"), split_axis=0, concat_axis=0, tiled=True)
 
     owner = cache_rows // code_dev
@@ -211,7 +352,15 @@
     ahead = jnp.dot(before.T, onehot, preferred_element_type=F32)
     slot_rank = jnp.sum(ahead * onehot, axis=1).astype(jnp.int32)
     slot_index = owner * capacity + slot_rank
-    choose = (slot_index[:, None] == jnp.arange(slots, dtype=jnp.int32)[None, :]).astype(BF16)
+    spot = jnp.arange(slots * DESC // across, dtype=jnp.int32)
+    inner = DESC // across * capacity
+    spot_slot = spot // inner * capacity + spot % capacity
+    spot_desc = spot // capacity % (DESC // across)
+    descs = jnp.arange(DESC // across, dtype=jnp.int32)
+    choose = (slot_index[None, :, None] == spot_slot[None, None, :]) & (
+        descs[:, None, None] == spot_desc[None, None, :]
+    )
+    choose = choose.astype(BF16).reshape(DESC // across * cand_count, -1)
 
     normed = layer_norm(doc_hidden.astype(F32)).astype(BF16)
     query = jnp.dot(normed, w_query, preferred_element_type=F32).astype(BF16)
@@ -223,7 +372,6 @@
     high_live = lax.ppermute(live[:HALF_WIN], "seq", down)
     low = lax.ppermute(keyval[tok_rows - HALF_WIN :], "seq", up)
     high = lax.ppermute(keyval[:HALF_WIN], "seq", down)
-    length = lax.psum(jnp.sum((doc_tokens != 0).astype(jnp.int32)), "seq")
     valid = jnp.concatenate([low_live, live, high_live])[None]
     context = window_attend(valid, query, low, keyval, high)
     middle = (
@@ -231,7 +379,12 @@
     ).astype(BF16)
     middle_wide = middle.astype(F32)
     cross_normed = layer_norm(middle_wide).astype(BF16)
-    cross_query = jnp.dot(cross_normed, x_query, preferred_element_type=F32).astype(BF16)
+    wide = part + HEAD
+    spread = jnp.pad(x_query.reshape(width, GROUPS, part), ((0, 0), (0, 0), (HEAD, 0)))
+    spread = spread.reshape(width, GROUPS * wide)
+    flag = (jnp.arange(GROUPS * wide) % wide < HEAD)[None, :]
+    cross_query = jnp.dot(cross_normed, spread, preferred_element_type=F32)
+    cross_query = jnp.where(flag, live[:, None], cross_query).astype(BF16)
 
     def turn(r):
         return [
@@ -239,7 +392,7 @@
         ]
 
     def piece(array, g):
-        return lax.dynamic_slice_in_dim(array, g * part, part, axis=1)
+        return lax.dynamic_slice_in_dim(array, g * wide, wide, axis=1)
 
     queries = [piece(cross_query, group)]
     for r in range(1, GROUPS):
@@ -247,9 +400,8 @@
             lax.ppermute(piece(cross_query, (group + r) % GROUPS), "seq", turn(r))
         )
 
-    arrived = arrived.transpose(1, 0, 2, 3).reshape(DESC // across, slots, 2 * part)
-    own_rows = jnp.einsum("cs,tsf->tcf", choose, arrived, preferred_element_type=F32).astype(BF16)
-    own_rows = own_rows.reshape(DESC // across * cand_count, 2 * part)
+    arrived = arrived.reshape(-1, 2 * part)
+    own_rows = jnp.dot(choose, arrived, preferred_element_type=F32).astype(BF16)
     all_rows = [own_rows]
     for r in range(1, across):
         step = [(i, i // across * across + (i % across + r) % across) for i in range(seq_count)]
@@ -261,25 +413,12 @@
     )
     key_rows = all_rows[:, part - HEAD :]
 
-    mass = 0.0
-    returned = [None] * GROUPS
-    for r in (2, 1, 3, 0):
-        origin = (group - r) % GROUPS * across + seq_index % across
-        position = origin * tok_rows + jnp.arange(tok_rows, dtype=jnp.int32)
-        weigh = (position < length).astype(F32)[:, None]
-        piece_context, piece_mass = cross_attend(weigh, queries[r], key_rows, value_rows)
-        mass = mass + piece_mass
-        returned[r] = (
-            lax.ppermute(piece_context, "seq", turn(GROUPS - r)) if r else piece_context
-        )
-    total = middle_wide
-    for r in range(GROUPS):
-        rows = lax.dynamic_slice_in_dim(x_out, (group + r) % GROUPS * part, part, axis=0)
-        total = total + jnp.dot(returned[r], rows, preferred_element_type=F32)
-    refined = total.astype(BF16)
-    local_mass = jnp.sum(mass.reshape(8, DESC, cand_count), axis=(0, 1))
-    cand_mass = lax.psum(local_mass, "seq")
-    cand_score = cand_count * cand_mass / (HEADS * length.astype(F32))
+    count = jnp.full((1, 128), jnp.sum(live))
+    refined, mass = cross_attend(
+        seq_count, count, jnp.stack(queries), key_rows, value_rows, middle, x_out
+    )
+    cand_mass = jnp.sum(mass[0, :-128].reshape(DESC, cand_count), axis=0)
+    cand_score = cand_count * cand_mass / (HEADS * mass[0, -1])
     return (refined[None], cand_score[None])
 
 

time: 229 us -> 148 us (0.65)
  blocking collectives: 64.6 us -> 0 us
  local copies, waits for them, and re-layouts: 52.2 us -> 16.6 us
  Pallas kernels: 31.9 us -> 44.8 us
  waiting for transfers between devices: 30.3 us -> 35.7 us
  other arithmetic: 6.6 us -> 9.47 us
    psum x2 -> x0, blocking collectives: 64.6 us -> none  [the longest x1 47 us: local(): length = lax.psum(jnp.sum((doc_tokens != 0).astype(jnp.int32)), 'seq')]
    ppermute x3, waiting for transfers between devices: 0.01 us -> 20.3 us  [local(): lax.ppermute(piece(cross_query, (group + r) % GROUPS), 'seq', turn(r))]
    rev x1 -> x0, local copies, waits for them, and re-layouts: 19.7 us -> none  [local(): picked = jnp.flip(picked, axis=2).transpose(0, 5, 3, 4, 1, 2, 6)]
    ppermute x1, waiting for transfers between devices: 18 us -> 0.01 us  [local(): all_rows.append(lax.ppermute(own_rows, 'seq', step))]
    reshape x4 -> x1, local copies, waits for them, and re-layouts: 15.9 us -> 0.08 us  [local(): picked = gather_rows(request.reshape(-1), code_cache, capacity)]
    pallas_call x4 -> x2, Pallas kernels: 23.5 us -> 36.3 us  [the longest x1 32.7 us: cross_attend(): pl.pallas_call(functools.partial(cross_kernel, seq_count, 512), out_shape...]
    ppermute x3 -> x0, waiting for transfers between devices: 12.3 us -> none  [local(): lax.ppermute(piece_context, 'seq', turn(GROUPS - r))]
    ppermute x1, waiting for transfers between devices: 0.01 us -> 9.03 us  [local(): low_live = lax.ppermute(live[tok_rows - HALF_WIN:], 'seq', up)]
  transfers between devices with their start and end apart: 15 -> 12, of which waited for: 3 -> 5; matrix products, arithmetic and copies ran while one was open for 8% -> 14% of each run, Pallas kernels for 11% -> 8%
where the time goes in v2:
time: 148 us; the launch traced here: 147 us
  Pallas kernels  44.8 us (30%)
  waiting for transfers between devices  35.7 us (24%)
  starting transfers between devices  27 us (18%)
  local copies, waits for them, and re-layouts  16.6 us (11%)
  matrix products  12.1 us (8%)
  other arithmetic  9.47 us (6%)
  between operations  1.75 us (1%)
    pallas_call x1, Pallas kernels, cross_attend(): pl.pallas_call(functools.partial(cross_kernel, seq_count, 512), out_shape...  32.7 us
    ppermute x3, waiting for transfers between devices, local(): lax.ppermute(piece(cross_query, (group + r) % GROUPS), 'seq', turn(r))  20.3 us
    ppermute x1, waiting for transfers between devices, local(): low_live = lax.ppermute(live[tok_rows - HALF_WIN:], 'seq', up)  9.03 us
    pallas_call x1, Pallas kernels, window_attend(): pl.pallas_call(window_kernel, grid=(pairs,), out_shape=jax.ShapeDtypeStru...  8.47 us
    all_to_all x1, starting transfers between devices, local(): lax.all_to_all(picked, ('doc', 'seq'), split_axis=0, concat_axis=0, tiled...  8 us
    unnamed x26, local copies, waits for them, and re-layouts  6.81 us
    all_to_all x1, waiting for transfers between devices, local(): lax.all_to_all(picked, ('doc', 'seq'), split_axis=0, concat_axis=0, tiled...  6.36 us
    dot_general x1, matrix products, local(): own_rows = jnp.dot(choose, arrived, preferred_element_type=F32).astype(BF16)  5.19 us
  transfers between devices with their start and end apart: 12, of which 5 were waited for; matrix products, arithmetic and copies ran while one was open for 14% of the time, Pallas kernels for 8%

profile of v2, /device:TPU:0, one launch (start us, length us, event | category | flops | bytes accessed | tf_op | source)
XLA Modules:
  0.0 147.4 jit_solution(1190317197152562195)
XLA Ops:
  1.5 3.5 %gather_fusion = s32[320]{0:T(512)S(1)} fusion(s32[9216]{0:T(1024)} %param.18, s32[1024]{0:T(1024)S(1)} %pad_clamp_fusion), kind=kCustom, calls=%fused_computation | custom fusion | bytes 3840 | tf_op jit(solution)/shard_map/gather | solution.py:321
  5.5 2.6 %collective-permute-start.8 = (s32[320]{0:T(512)S(1)}, s32[320]{0:T(512)S(1)}, u32[]{:S(2)}, u32[]{:S(2)}) collective-permute-start(s32[320]{0:T(512)S(1)} %gather_fusion), channel_id=1, source_target_pairs={{0,16},{8,24},{16,0},{24,8},{1,17},{9,25},{17,1},{25,9},{2,18},{10... | collective-permute-start | bytes 3848 | tf_op jit(solution)/shard_map/ppermute | solution.py:325
  8.1 1.4 collective-permute-start.9
  10.1 1.5 convolution_convert_fusion.ko_ref.vo_ref
  11.6 1.3 fusion.54
  13.2 3.4 %collective-permute-start.2 = (bf16[256,1536]{1,0:T(8,128)(2,1)}, bf16[256,1536]{1,0:T(8,128)(2,1)S(1)}, u32[]{:S(2)}, u32[]{:S(2)}) collective-permute-start(bf16[256,1536]{1,0:T(8,128)(2,1)} %get-tuple-element.9), channel_id=1, source_target_pairs={{0,1},{1,2},{2,3},{3,4},{4,5},{5,6},{6,7},{8,9},{9,10},{10,11},{11... | collective-permute-start | bytes 2359304 | tf_op jit(solution)/shard_map/ppermute | solution.py:373
  16.6 1.3 collective-permute-start.3
  18.4 4.5 %collective-permute-start = (f32[256]{0:T(256)S(1)}, f32[256]{0:T(256)S(1)}, u32[]{:S(2)}, u32[]{:S(2)}) collective-permute-start(f32[256]{0:T(256)S(1)} %bitcast.58), channel_id=1, source_target_pairs={{0,1},{1,2},{2,3},{3,4},{4,5},{5,6},{6,7},{8,9},{9,10},{10,11},{11... | collective-permute-start | bytes 3080 | tf_op jit(solution)/shard_map/ppermute | solution.py:371
  23.0 1.3 collective-permute-start.1
  24.9 3.6 %shard_map.114 = bf16[4,4,128,384]{3,2,1,0:T(8,128)(2,1)S(1)} custom-call(s32[64]{0:T(128)S(1)} %reshape.352.request_ref, bf16[4608,768]{1,0:T(8,128)(2,1)} %bitcast.48, bf16[256,256]{1,0:T(8,128)(2,1)S(1)} %fusion.17.order_ref), custom_call_target="tpu_custom_call" | custom-call | flops 402653184 | bytes 3145728 | tf_op jit(solution)/shard_map/pallas_call | solution.py:131
  28.5 1.2 copy-done.1
  29.7 8.0 %all-to-all-start = ((bf16[32,64,384]{2,1,0:T(8,128)(2,1)}), bf16[32,64,384]{2,1,0:T(8,128)(2,1)}, u32[]{:S(2)}, u32[]{:S(2)}) async-start(bf16[32,64,384]{2,1,0:T(8,128)(2,1)} %bitcast.45), calls=%async_computation | async-start | bytes 3145728 | tf_op jit(solution)/shard_map/all_to_all | solution.py:348
  37.7 3.2 %convolution_convert_fusion.2.q_ref = bf16[512,768]{1,0:T(8,128)(2,1)} fusion(bf16[768,768]{1,0:T(8,128)(2,1)} %param.12, bf16[1,512,768]{2,1,0:T(8,128)(2,1)} %param.10, f32[512]{0:T(512)S(1)} %add_rsqrt_fusion.1, f32[512]{0:T(512)S(1)} %broadcast_multiply_fusion.1), kind=kOutput, calls=%fused_computation.22 | convolution fusion | flops 605945856 | bytes 2756608 | tf_op jit(solution)/shard_map/dot_general | solution.py:366
  41.0 1.3 broadcast_compare_fusion
  42.2 3.8 %broadcast_and_fusion = pred[4,320,2048]{2,1,0:T(32,128)(4,1)} fusion(pred[4,2048]{1,0:T(4,128)(4,1)S(1)} %iota_compare_fusion.7, pred[320,2048]{1,0:T(8,128)(4,1)} %broadcast_compare_fusion), kind=kLoop, calls=%fused_computation.1 | loop fusion | flops 2621440 | bytes 3284992 | tf_op jit(solution)/shard_map/and | solution.py:360
  46.0 2.4 %copy.13 = bf16[768,768]{0,1:T(8,128)(2,1)} copy(bf16[768,768]{1,0:T(8,128)(2,1)} %param.15) | data formatting | bytes 2359296 | tf_op args[5]
  48.4 2.8 %pad.4 = bf16[768,4,256]{0,2,1:T(8,128)(2,1)} pad(bf16[768,4,192]{0,2,1:T(8,128)(2,1)} %bitcast.49, bf16[]{:T(256)} %constant.191.clone.1), padding=0_0x0_0x64_0 | pad | bytes 2752514 | tf_op jit(solution)/shard_map/jit(_pad)/pad | solution.py:383
  51.1 9.0 %collective-permute-done = f32[256]{0:T(256)S(1)} collective-permute-done((f32[256]{0:T(256)S(1)}, f32[256]{0:T(256)S(1)}, u32[]{:S(2)}, u32[]{:S(2)}) %collective-permute-start) | collective-permute-done | bytes 1056 | tf_op jit(solution)/shard_map/ppermute | solution.py:371
  60.2 8.5 %shard_map.113 = bf16[512,768]{1,0:T(8,128)(2,1)S(1)} custom-call(f32[1,1024]{1,0:T(1,128)S(1)} %bitcast.47, bf16[512,768]{1,0:T(8,128)(2,1)S(1)} %copy-done.6, bf16[256,1536]{1,0:T(8,128)(2,1)S(1)} %collective-permute-done.2.kl_ref.vl_ref, bf16[512,1536]{1,0:T(8,128)(2,1)S(1)} %copy-done.3, bf16[256,1536]{1,0:T(8,128)(2,1)} %collective-permute-done.3.kh_ref.vh_ref, ...), custom_call_target="tpu_custom_call" | custom-call | flops 2415919104 | bytes 3145728 | tf_op jit(solution)/shard_map/pallas_call | solution.py:71
  70.0 6.4 %all-to-all-done = bf16[32,64,384]{2,1,0:T(8,128)(2,1)} async-done(((bf16[32,64,384]{2,1,0:T(8,128)(2,1)}), bf16[32,64,384]{2,1,0:T(8,128)(2,1)}, u32[]{:S(2)}, u32[]{:S(2)}) %all-to-all-start) | async-done | bytes 1572896 | tf_op jit(solution)/shard_map/all_to_all | solution.py:348
  76.3 5.2 %convolution_convert_fusion.1 = bf16[1280,384]{1,0:T(8,128)(2,1)S(1)} fusion(pred[1280,2048]{1,0:T(32,128)(4,1)} %bitcast.50, bf16[2048,384]{1,0:T(8,128)(2,1)} %bitcast.15), kind=kOutput, calls=%fused_computation.3 | convolution fusion | flops 2013757440 | bytes 5177344 | tf_op jit(solution)/shard_map/dot_general | solution.py:404
  82.1 1.0 select_convert_fusion
  83.3 1.1 collective-permute-start.6
  84.4 1.0 collective-permute-start.4
  85.3 1.4 collective-permute-start.5
  87.3 9.4 %collective-permute-done.6 = bf16[512,256]{1,0:T(8,128)(2,1)S(1)} collective-permute-done((bf16[512,256]{1,0:T(8,128)(2,1)S(1)}, bf16[512,256]{1,0:T(8,128)(2,1)S(1)}, u32[]{:S(2)}, u32[]{:S(2)}) %collective-permute-start.6) | collective-permute-done | bytes 262176 | tf_op jit(solution)/shard_map/ppermute | solution.py:400
  96.7 2.4 %collective-permute-done.4 = bf16[512,256]{1,0:T(8,128)(2,1)S(1)} collective-permute-done((bf16[512,256]{1,0:T(8,128)(2,1)S(1)}, bf16[512,256]{1,0:T(8,128)(2,1)S(1)}, u32[]{:S(2)}, u32[]{:S(2)}) %collective-permute-start.4) | collective-permute-done | bytes 262176 | tf_op jit(solution)/shard_map/ppermute | solution.py:400
  99.1 8.6 %collective-permute-done.5 = bf16[512,256]{1,0:T(8,128)(2,1)S(1)} collective-permute-done((bf16[512,256]{1,0:T(8,128)(2,1)S(1)}, bf16[512,256]{1,0:T(8,128)(2,1)S(1)}, u32[]{:S(2)}, u32[]{:S(2)}) %collective-permute-start.5) | collective-permute-done | bytes 262176 | tf_op jit(solution)/shard_map/ppermute | solution.py:400
  107.8 1.4 fusion.12
  109.8 32.7 %shard_map.115 = (bf16[512,768]{1,0:T(8,128)(2,1)S(1)}, f32[1,2688]{1,0:T(1,128)S(1)}) custom-call(f32[1,128]{1,0:T(1,128)S(1)} %broadcast_in_dim.62.count_ref, bf16[4,512,256]{2,1,0:T(8,128)(2,1)S(1)} %pad_maximum_fusion.1.q_ref, bf16[2560,256]{1,0:T(8,128)(2,1)S(1)} %get-tuple-element.7.k_ref, bf16[2560,256]{1,0:T(8,128)(2,1)} %get-tuple-element.6.v_ref, ...), custom_call_target="tpu_custom_call" | custom-call | flops 16106127360 | bytes 3145728 | tf_op jit(solution)/shard_map/pallas_call | solution.py:272
  142.5 0.9 copy-done.4
  145.3 2.1 %copy.17 = bf16[1,512,768]{2,1,0:T(8,128)(2,1)} copy(bf16[1,512,768]{2,1,0:T(8,128)(2,1)} %bitcast.46) | data formatting | bytes 1572864
  (77 shorter events, 7.7 us)
Async XLA Ops:
  0.6 9.5 %copy-start = (bf16[768,1536]{1,0:T(8,128)(2,1)S(1)}, bf16[768,1536]{1,0:T(8,128)(2,1)}, u32[]{:S(2)}) copy-start(bf16[768,1536]{1,0:T(8,128)(2,1)} %param.13) | copy-start | bytes 7077892
  0.6 8.9 %copy-start.7 = (bf16[1,512,768]{2,1,0:T(8,128)(2,1)S(1)}, bf16[1,512,768]{2,1,0:T(8,128)(2,1)}, u32[]{:S(2)}) copy-start(bf16[1,512,768]{2,1,0:T(8,128)(2,1)} %param.10) | copy-start | bytes 2359300
  5.0 13.3 %collective-permute-start.7 = (s32[320]{0:T(512)S(1)}, s32[320]{0:T(512)S(1)}, u32[]{:S(2)}, u32[]{:S(2)}) collective-permute-start(s32[320]{0:T(512)S(1)} %gather_fusion), channel_id=1, source_target_pairs={{0,8},{8,16},{16,24},{24,0},{1,9},{9,17},{17,25},{25,1},{2,10},{10... | collective-permute-start | bytes 3848 | tf_op jit(solution)/shard_map/ppermute | solution.py:325
  5.5 17.4 %collective-permute-start.8 = (s32[320]{0:T(512)S(1)}, s32[320]{0:T(512)S(1)}, u32[]{:S(2)}, u32[]{:S(2)}) collective-permute-start(s32[320]{0:T(512)S(1)} %gather_fusion), channel_id=1, source_target_pairs={{0,16},{8,24},{16,0},{24,8},{1,17},{9,25},{17,1},{25,9},{2,18},{10... | collective-permute-start | bytes 3848 | tf_op jit(solution)/shard_map/ppermute | solution.py:325
  8.1 16.1 %collective-permute-start.9 = (s32[320]{0:T(512)S(1)}, s32[320]{0:T(512)S(1)}, u32[]{:S(2)}, u32[]{:S(2)}) collective-permute-start(s32[320]{0:T(512)S(1)} %gather_fusion), channel_id=1, source_target_pairs={{0,24},{8,0},{16,8},{24,16},{1,25},{9,1},{17,9},{25,17},{2,26},{10... | collective-permute-start | bytes 3848 | tf_op jit(solution)/shard_map/ppermute | solution.py:325
  11.6 1.6 %copy-start.2 = (bf16[512,1536]{1,0:T(8,128)(2,1)}, bf16[512,1536]{1,0:T(8,128)(2,1)S(1)}, u32[]{:S(2)}) copy-start(bf16[512,1536]{1,0:T(8,128)(2,1)S(1)} %convolution_convert_fusion.ko_ref.vo_ref) | copy-start | bytes 4718596
  11.6 6.4 %copy-start.10 = (s32[1,512]{1,0:T(1,128)S(1)}, s32[1,512]{1,0:T(1,128)}, u32[]{:S(2)}) copy-start(s32[1,512]{1,0:T(1,128)} %param.11) | copy-start | bytes 6148
  13.2 47.0 %collective-permute-start.2 = (bf16[256,1536]{1,0:T(8,128)(2,1)}, bf16[256,1536]{1,0:T(8,128)(2,1)S(1)}, u32[]{:S(2)}, u32[]{:S(2)}) collective-permute-start(bf16[256,1536]{1,0:T(8,128)(2,1)} %get-tuple-element.9), channel_id=1, source_target_pairs={{0,1},{1,2},{2,3},{3,4},{4,5},{5,6},{6,7},{8,9},{9,10},{10,11},{11... | collective-permute-start | bytes 2359304 | tf_op jit(solution)/shard_map/ppermute | solution.py:373
  16.6 43.6 %collective-permute-start.3 = (bf16[256,1536]{1,0:T(8,128)(2,1)}, bf16[256,1536]{1,0:T(8,128)(2,1)}, u32[]{:S(2)}, u32[]{:S(2)}) collective-permute-start(bf16[256,1536]{1,0:T(8,128)(2,1)} %get-tuple-element.8), channel_id=1, source_target_pairs={{1,0},{2,1},{3,2},{4,3},{5,4},{6,5},{7,6},{9,8},{10,9},{11,10},{12... | collective-permute-start | bytes 2359304 | tf_op jit(solution)/shard_map/ppermute | solution.py:374
  18.4 41.8 %collective-permute-start = (f32[256]{0:T(256)S(1)}, f32[256]{0:T(256)S(1)}, u32[]{:S(2)}, u32[]{:S(2)}) collective-permute-start(f32[256]{0:T(256)S(1)} %bitcast.58), channel_id=1, source_target_pairs={{0,1},{1,2},{2,3},{3,4},{4,5},{5,6},{6,7},{8,9},{9,10},{10,11},{11... | collective-permute-start | bytes 3080 | tf_op jit(solution)/shard_map/ppermute | solution.py:371
  23.0 37.2 %collective-permute-start.1 = (f32[256]{0:T(256)S(1)}, f32[256]{0:T(256)S(1)}, u32[]{:S(2)}, u32[]{:S(2)}) collective-permute-start(f32[256]{0:T(256)S(1)} %bitcast.57), channel_id=1, source_target_pairs={{1,0},{2,1},{3,2},{4,3},{5,4},{6,5},{7,6},{9,8},{10,9},{11,10},{12... | collective-permute-start | bytes 3080 | tf_op jit(solution)/shard_map/ppermute | solution.py:372
  28.5 1.2 copy-start.1
  29.7 46.6 %all-to-all-start = ((bf16[32,64,384]{2,1,0:T(8,128)(2,1)}), bf16[32,64,384]{2,1,0:T(8,128)(2,1)}, u32[]{:S(2)}, u32[]{:S(2)}) async-start(bf16[32,64,384]{2,1,0:T(8,128)(2,1)} %bitcast.45), calls=%async_computation | async-start | bytes 3145728 | tf_op jit(solution)/shard_map/all_to_all | solution.py:348
  48.4 11.8 %copy-start.3 = (bf16[512,1536]{1,0:T(8,128)(2,1)S(1)}, bf16[512,1536]{1,0:T(8,128)(2,1)}, u32[]{:S(2)}) copy-start(bf16[512,1536]{1,0:T(8,128)(2,1)} %copy-done.2) | copy-start | bytes 4718596
  48.4 11.8 %copy-start.6 = (bf16[512,768]{1,0:T(8,128)(2,1)S(1)}, bf16[512,768]{1,0:T(8,128)(2,1)}, u32[]{:S(2)}) copy-start(bf16[512,768]{1,0:T(8,128)(2,1)} %convolution_convert_fusion.2.q_ref) | copy-start | bytes 2359300
  60.2 8.5 %copy-start.8 = (bf16[1,512,768]{2,1,0:T(8,128)(2,1)S(1)}, bf16[1,512,768]{2,1,0:T(8,128)(2,1)}, u32[]{:S(2)}) copy-start(bf16[1,512,768]{2,1,0:T(8,128)(2,1)} %param.10) | copy-start | bytes 2359300
  60.2 8.5 %copy-start.11 = (bf16[768,768]{1,0:T(8,128)(2,1)S(1)}, bf16[768,768]{1,0:T(8,128)(2,1)}, u32[]{:S(2)}) copy-start(bf16[768,768]{1,0:T(8,128)(2,1)} %param.14) | copy-start | bytes 3538948
  76.3 5.7 %copy-start.9 = (bf16[768,4,256]{0,2,1:T(8,128)(2,1)S(1)}, bf16[768,4,256]{0,2,1:T(8,128)(2,1)}, u32[]{:S(2)}) copy-start(bf16[768,4,256]{0,2,1:T(8,128)(2,1)} %pad.4) | copy-start | bytes 4718596
  81.5 26.3 %collective-permute-start.10 = (bf16[1280,384]{1,0:T(8,128)(2,1)S(1)}, bf16[1280,384]{1,0:T(8,128)(2,1)S(1)}, u32[]{:S(2)}, u32[]{:S(2)}) collective-permute-start(bf16[1280,384]{1,0:T(8,128)(2,1)S(1)} %convolution_convert_fusion.1), channel_id=1, source_target_pairs={{0,1},{1,0},{2,3},{3,2},{4,5},{5,4},{6,7},{7,6},{8,9},{9,8},{10,11... | collective-permute-start | bytes 2949128 | tf_op jit(solution)/shard_map/ppermute | solution.py:408
  83.3 13.5 %collective-permute-start.6 = (bf16[512,256]{1,0:T(8,128)(2,1)S(1)}, bf16[512,256]{1,0:T(8,128)(2,1)S(1)}, u32[]{:S(2)}, u32[]{:S(2)}) collective-permute-start(bf16[512,256]{1,0:T(8,128)(2,1)S(1)} %get-tuple-element.11), channel_id=1, source_target_pairs={{0,6},{1,7},{2,0},{3,1},{4,2},{5,3},{6,4},{7,5},{8,14},{9,15},{10,... | collective-permute-start | bytes 786440 | tf_op jit(solution)/shard_map/ppermute | solution.py:400
  84.4 14.7 %collective-permute-start.4 = (bf16[512,256]{1,0:T(8,128)(2,1)S(1)}, bf16[512,256]{1,0:T(8,128)(2,1)S(1)}, u32[]{:S(2)}, u32[]{:S(2)}) collective-permute-start(bf16[512,256]{1,0:T(8,128)(2,1)S(1)} %get-tuple-element.13), channel_id=1, source_target_pairs={{0,2},{1,3},{2,4},{3,5},{4,6},{5,7},{6,0},{7,1},{8,10},{9,11},{10,... | collective-permute-start | bytes 786440 | tf_op jit(solution)/shard_map/ppermute | solution.py:400
  85.3 22.3 %collective-permute-start.5 = (bf16[512,256]{1,0:T(8,128)(2,1)S(1)}, bf16[512,256]{1,0:T(8,128)(2,1)S(1)}, u32[]{:S(2)}, u32[]{:S(2)}) collective-permute-start(bf16[512,256]{1,0:T(8,128)(2,1)S(1)} %get-tuple-element.12), channel_id=1, source_target_pairs={{0,4},{1,5},{2,6},{3,7},{4,0},{5,1},{6,2},{7,3},{8,12},{9,13},{10,... | collective-permute-start | bytes 786440 | tf_op jit(solution)/shard_map/ppermute | solution.py:400
  107.8 2.0 %copy-start.5 = (bf16[768,768]{1,0:T(8,128)(2,1)S(1)}, bf16[768,768]{1,0:T(8,128)(2,1)}, u32[]{:S(2)}) copy-start(bf16[768,768]{1,0:T(8,128)(2,1)} %w_ref.1) | copy-start | bytes 3538948
  142.5 0.9 copy-start.4

commit v3 on v2

--- a/solution.py
+++ b/solution.py
@@ -13,6 +13,7 @@
 HALF_WIN = 256
 DESC = 8
 GROUPS = 4
+CHUNKS = 2
 EXP2_SCALE = math.log2(math.e) / math.sqrt(HEAD)
 F32 = jnp.float32
 BF16 = jnp.bfloat16
@@ -93,10 +94,11 @@
     )(valid, query, low, own, high, low, own, high)
 
 
-def gather_kernel(docs, capacity, request_ref, cache_ref, order_ref, out_ref, held, sems):
+def gather_kernel(docs, capacity, request_ref, cache_ref, order_ref, *refs):
+    *outs, held, sems = refs
     count = docs * capacity
     step = 2 * DESC
-    part = out_ref.shape[-1] // 2
+    part = outs[0].shape[-1] // 2
 
     def fetch(i):
         row = pl.multiple_of(request_ref[i] * step, step)
@@ -116,27 +118,34 @@
         ).astype(BF16)
         for g in range(GROUPS):
             cols = slice(g * part, (g + 1) * part)
-            out_ref[d, g] = jnp.concatenate([ordered[:half, cols], ordered[half:, cols]], axis=1)
-
-
-def gather_rows(request, cache, capacity):
+            both = jnp.concatenate([ordered[:half, cols], ordered[half:, cols]], axis=1)
+            size = half // len(outs)
+            for c, out_ref in enumerate(outs):
+                out_ref[d, g] = both[c * size : (c + 1) * size]
+
+
+def gather_rows(request, cache, capacity, across):
     docs = request.shape[0] // capacity
     codes, pair, desc, width = cache.shape
     part = width // GROUPS
     rows = capacity * pair * desc
     out = jnp.arange(rows)
-    source = out % capacity * (2 * desc) + (1 - out // (desc * capacity)) * desc
-    source = source + out // capacity % desc
+    inner = desc // across // CHUNKS
+    chunk = out // (desc * capacity // CHUNKS) % CHUNKS
+    column = out // (inner * capacity) % across
+    position = (column * CHUNKS + chunk) * inner + out // capacity % inner
+    source = out % capacity * (2 * desc) + (1 - out // (desc * capacity)) * desc + position
     order = (source[:, None] == out[None, :]).astype(BF16)
     return pl.pallas_call(
         functools.partial(gather_kernel, docs, capacity),
-        out_shape=jax.ShapeDtypeStruct((docs, GROUPS, rows // 2, 2 * part), BF16),
+        out_shape=[jax.ShapeDtypeStruct((docs, GROUPS, rows // 2 // CHUNKS, 2 * part), BF16)]
+        * CHUNKS,
         in_specs=[
             pl.BlockSpec(memory_space=pltpu.SMEM),
             pl.BlockSpec(memory_space=pl.ANY),
             pl.BlockSpec(memory_space=pltpu.VMEM),
         ],
-        out_specs=pl.BlockSpec(memory_space=pltpu.VMEM),
+        out_specs=[pl.BlockSpec(memory_space=pltpu.VMEM)] * CHUNKS,
         scratch_shapes=[
             pltpu.VMEM((docs * rows, width), BF16),
             pltpu.SemaphoreType.DMA((docs * capacity,)),
@@ -153,23 +162,16 @@
 def cross_kernel(
     seq_count,
     chunk,
+    pieces,
     count_ref,
-    q_ref,
-    k_ref,
-    v_ref,
     middle_ref,
     w_ref,
-    o_ref,
-    mass_ref,
-    context,
-    landed,
-    mass,
-    masses,
-    send_sem,
-    recv_sem,
-    mass_send,
-    mass_recv,
+    *refs,
 ):
+    queries, refs = refs[:GROUPS], refs[GROUPS:]
+    rows_in, refs = refs[:pieces], refs[pieces:]
+    o_ref, mass_ref, q_ref, k_ref, v_ref, context, landed, mass, masses = refs[:9]
+    send_sem, recv_sem, mass_send, mass_recv = refs[9:]
     me = lax.axis_index("seq")
     across = seq_count // GROUPS
     group = me // across
@@ -190,6 +192,13 @@
             device_id_type=pl.DeviceIdType.MESH,
         )
     mass[...] = jnp.zeros_like(mass)
+    size = keys // pieces
+    for n, piece in enumerate(rows_in):
+        k_ref[n * size : (n + 1) * size, :] = piece[:, part - HEAD :]
+        ahead = lax.broadcasted_iota(jnp.int32, (size, wide), 1) < part
+        v_ref[n * size : (n + 1) * size, :] = jnp.where(ahead, piece[:, :wide], jnp.ones((), BF16))
+    for r, query in enumerate(queries):
+        q_ref[r] = query[...]
 
     def send_back(r):
         return pltpu.make_async_remote_copy(
@@ -264,20 +273,24 @@
     mass_ref[...] = jnp.sum(masses[...], axis=0)
 
 
-def cross_attend(seq_count, count, queries, key_rows, value_rows, middle, x_out):
-    groups, rows, wide = queries.shape
-    keys = key_rows.shape[0]
+def cross_attend(seq_count, count, queries, pieces, middle, x_out):
+    groups = len(queries)
+    rows, wide = queries[0].shape
+    keys = sum(piece.shape[0] for piece in pieces)
     part = wide - HEAD
     vmem = pl.BlockSpec(memory_space=pltpu.VMEM)
     return pl.pallas_call(
-        functools.partial(cross_kernel, seq_count, 512),
+        functools.partial(cross_kernel, seq_count, 512, len(pieces)),
         out_shape=(
             jax.ShapeDtypeStruct(middle.shape, BF16),
             jax.ShapeDtypeStruct((1, keys + 128), F32),
         ),
-        in_specs=[vmem] * 6,
+        in_specs=[vmem] * (3 + groups + len(pieces)),
         out_specs=(vmem, vmem),
         scratch_shapes=[
+            pltpu.VMEM((groups, rows, wide), BF16),
+            pltpu.VMEM((keys, wide), BF16),
+            pltpu.VMEM((keys, wide), BF16),
             pltpu.VMEM((groups, rows, part), BF16),
             pltpu.VMEM((groups, rows, part), BF16),
             pltpu.VMEM((8, keys), F32),
@@ -295,7 +308,7 @@
             bytes_accessed=4 * keys * wide + 4 * rows * wide,
             transcendentals=3 * groups * rows * keys,
         ),
-    )(count, queries, key_rows, value_rows, middle, x_out)
+    )(count, middle, x_out, *queries, *pieces)
 
 
 def local(
@@ -343,24 +356,29 @@
         ),
         axis=2,
     )
-    picked = gather_rows(request.reshape(-1), code_cache, capacity)
-    picked = picked.reshape(devices, DESC // across * capacity, 2 * part)
-    arrived = lax.all_to_all(picked, ("doc", "seq"), split_axis=0, concat_axis=0, tiled=True)
+    picked = gather_rows(request.reshape(-1), code_cache, capacity, across)
+    inner = DESC // across // CHUNKS
+    arrived = []
+    for chunk in picked:
+        chunk = chunk.reshape(devices, inner * capacity, 2 * part)
+        if arrived:
+            chunk, arrived[-1] = lax.optimization_barrier((chunk, arrived[-1]))
+        arrived.append(
+            lax.all_to_all(chunk, ("doc", "seq"), split_axis=0, concat_axis=0, tiled=True)
+        )
 
     owner = cache_rows // code_dev
     onehot = (owner[:, None] == jnp.arange(devices, dtype=jnp.int32)[None, :]).astype(BF16)
     ahead = jnp.dot(before.T, onehot, preferred_element_type=F32)
     slot_rank = jnp.sum(ahead * onehot, axis=1).astype(jnp.int32)
     slot_index = owner * capacity + slot_rank
-    spot = jnp.arange(slots * DESC // across, dtype=jnp.int32)
-    inner = DESC // across * capacity
-    spot_slot = spot // inner * capacity + spot % capacity
-    spot_desc = spot // capacity % (DESC // across)
-    descs = jnp.arange(DESC // across, dtype=jnp.int32)
+    spot = jnp.arange(slots * inner, dtype=jnp.int32)
+    spot_slot = spot // (inner * capacity) * capacity + spot % capacity
+    descs = jnp.arange(inner, dtype=jnp.int32)
     choose = (slot_index[None, :, None] == spot_slot[None, None, :]) & (
-        descs[:, None, None] == spot_desc[None, None, :]
-    )
-    choose = choose.astype(BF16).reshape(DESC // across * cand_count, -1)
+        descs[:, None, None] == (spot // capacity % inner)[None, None, :]
+    )
+    choose = choose.astype(BF16).reshape(inner * cand_count, -1)
 
     normed = layer_norm(doc_hidden.astype(F32)).astype(BF16)
     query = jnp.dot(normed, w_query, preferred_element_type=F32).astype(BF16)
@@ -368,11 +386,13 @@
     up = [(i, i + 1) for i in range(seq_count - 1)]
     down = [(i + 1, i) for i in range(seq_count - 1)]
     live = (doc_tokens != 0).astype(F32)
-    low_live = lax.ppermute(live[tok_rows - HALF_WIN :], "seq", up)
-    high_live = lax.ppermute(live[:HALF_WIN], "seq", down)
-    low = lax.ppermute(keyval[tok_rows - HALF_WIN :], "seq", up)
-    high = lax.ppermute(keyval[:HALF_WIN], "seq", down)
-    valid = jnp.concatenate([low_live, live, high_live])[None]
+    flagged = jnp.concatenate(
+        [keyval, jnp.broadcast_to(live.astype(BF16)[:, None], (tok_rows, 2 * HEAD))], axis=1
+    )
+    low = lax.ppermute(flagged[tok_rows - HALF_WIN :], "seq", up)
+    high = lax.ppermute(flagged[:HALF_WIN], "seq", down)
+    valid = jnp.concatenate([low[:, 2 * width], live.astype(BF16), high[:, 2 * width]])
+    valid = valid.astype(F32)[None]
     context = window_attend(valid, query, low, keyval, high)
     middle = (
         doc_hidden.astype(F32) + jnp.dot(context, w_out, preferred_element_type=F32)
@@ -380,8 +400,11 @@
     middle_wide = middle.astype(F32)
     cross_normed = layer_norm(middle_wide).astype(BF16)
     wide = part + HEAD
-    spread = jnp.pad(x_query.reshape(width, GROUPS, part), ((0, 0), (0, 0), (HEAD, 0)))
-    spread = spread.reshape(width, GROUPS * wide)
+    blank = jnp.zeros((width, HEAD), BF16)
+    spread = []
+    for g in range(GROUPS):
+        spread += [blank, x_query[:, g * part : (g + 1) * part]]
+    spread = jnp.concatenate(spread, axis=1)
     flag = (jnp.arange(GROUPS * wide) % wide < HEAD)[None, :]
     cross_query = jnp.dot(cross_normed, spread, preferred_element_type=F32)
     cross_query = jnp.where(flag, live[:, None], cross_query).astype(BF16)
@@ -400,22 +423,19 @@
             lax.ppermute(piece(cross_query, (group + r) % GROUPS), "seq", turn(r))
         )
 
-    arrived = arrived.reshape(-1, 2 * part)
-    own_rows = jnp.dot(choose, arrived, preferred_element_type=F32).astype(BF16)
-    all_rows = [own_rows]
-    for r in range(1, across):
-        step = [(i, i // across * across + (i % across + r) % across) for i in range(seq_count)]
-        all_rows.append(lax.ppermute(own_rows, "seq", step))
-    all_rows = jnp.concatenate(all_rows)
-    column = jnp.arange(part + HEAD)
-    value_rows = jnp.where(
-        column[None, :] < part, all_rows[:, : part + HEAD], jnp.ones((), BF16)
-    )
-    key_rows = all_rows[:, part - HEAD :]
+    pieces = []
+    for chunk in arrived:
+        own_rows = jnp.dot(
+            choose, chunk.reshape(-1, 2 * part), preferred_element_type=F32
+        ).astype(BF16)
+        pieces.append(own_rows)
+        for r in range(1, across):
+            step = [(i, i // across * across + (i % across + r) % across) for i in range(seq_count)]
+            pieces.append(lax.ppermute(own_rows, "seq", step))
 
     count = jnp.full((1, 128), jnp.sum(live))
     refined, mass = cross_attend(
-        seq_count, count, jnp.stack(queries), key_rows, value_rows, middle, x_out
+        seq_count, count, queries, pieces, middle, x_out
     )
     cand_mass = jnp.sum(mass[0, :-128].reshape(DESC, cand_count), axis=0)
     cand_score = cand_count * cand_mass / (HEADS * mass[0, -1])

time: 148 us -> 159 us (1.074)
  Pallas kernels: 44.8 us -> 50.3 us
  waiting for transfers between devices: 35.7 us -> 39.9 us
  other arithmetic: 9.47 us -> 5.76 us
  starting transfers between devices: 27 us -> 30.2 us
  local copies, waits for them, and re-layouts: 16.6 us -> 18.2 us
    ppermute x5 -> x4, waiting for transfers between devices: 9.04 us -> 17.9 us  [the longest x1 17.9 us: local(): low = lax.ppermute(flagged[tok_rows - HALF_WIN:], 'seq', up)]
    all_to_all x1 -> x2, starting transfers between devices: 8 us -> 14.7 us  [local(): lax.all_to_all(chunk, ('doc', 'seq'), split_axis=0, concat_axis=0, tiled=...]
    pallas_call x1, Pallas kernels: 32.7 us -> 37 us  [cross_attend(): pl.pallas_call(functools.partial(cross_kernel, seq_count, 512, len(pieces...]
    concatenate x0 -> x3, local copies, waits for them, and re-layouts: none -> 4.13 us  [the longest x1 4.12 us: local(): spread = jnp.concatenate(spread, axis=1)]
    ppermute x5 -> x4, starting transfers between devices: 11.1 us -> 7.12 us  [the longest x1 3.43 us: local(): low = lax.ppermute(flagged[tok_rows - HALF_WIN:], 'seq', up)]
    ppermute x3, waiting for transfers between devices: 20.3 us -> 16.8 us  [local(): lax.ppermute(piece(cross_query, (group + r) % GROUPS), 'seq', turn(r))]
    pad x1 -> x0, local copies, waits for them, and re-layouts: 2.76 us -> none  [local(): jnp.pad(x_query.reshape(width, GROUPS, part), ((0, 0), (0, 0), (HEAD, 0)))]
    and x1, other arithmetic: 3.77 us -> 1.21 us  [local(): (slot_index[None, :, None] == spot_slot[None, None, :]) & (descs[:, None,...]
  transfers between devices with their start and end apart: 12 -> 12, of which waited for: 5 -> 4; matrix products, arithmetic and copies ran while one was open for 14% -> 15% of each run, Pallas kernels for 8% -> 8%
where the time goes in v3:
time: 159 us; the launch traced here: 158 us
  Pallas kernels  50.3 us (32%)
  waiting for transfers between devices  39.9 us (25%)
  starting transfers between devices  30.2 us (19%)
  local copies, waits for them, and re-layouts  18.2 us (11%)
  matrix products  12 us (8%)
  other arithmetic  5.76 us (4%)
  between operations  1.87 us (1%)
    pallas_call x1, Pallas kernels, cross_attend(): pl.pallas_call(functools.partial(cross_kernel, seq_count, 512, len(pieces...  37 us
    ppermute x1, waiting for transfers between devices, local(): low = lax.ppermute(flagged[tok_rows - HALF_WIN:], 'seq', up)  17.9 us
    ppermute x3, waiting for transfers between devices, local(): lax.ppermute(piece(cross_query, (group + r) % GROUPS), 'seq', turn(r))  16.8 us
    all_to_all x2, starting transfers between devices, local(): lax.all_to_all(chunk, ('doc', 'seq'), split_axis=0, concat_axis=0, tiled=...  14.7 us
    pallas_call x1, Pallas kernels, window_attend(): pl.pallas_call(window_kernel, grid=(pairs,), out_shape=jax.ShapeDtypeStru...  8.45 us
    unnamed x27, local copies, waits for them, and re-layouts  5.72 us
    all_to_all x2, waiting for transfers between devices, local(): lax.all_to_all(chunk, ('doc', 'seq'), split_axis=0, concat_axis=0, tiled=...  5.17 us
    dot_general x2, matrix products, local(): jnp.dot(choose, chunk.reshape(-1, 2 * part), preferred_element_type=F32)  5.07 us
  transfers between devices with their start and end apart: 12, of which 4 were waited for; matrix products, arithmetic and copies ran while one was open for 15% of the time, Pallas kernels for 8%

profile of v3, /device:TPU:0, one launch (start us, length us, event | category | flops | bytes accessed | tf_op | source)
XLA Modules:
  0.0 158.1 jit_solution(1695033354648145763)
XLA Ops:
  1.5 3.5 %gather_fusion = s32[320]{0:T(512)S(1)} fusion(s32[9216]{0:T(1024)} %param.18, s32[1024]{0:T(1024)S(1)} %pad_clamp_fusion), kind=kCustom, calls=%fused_computation | custom fusion | bytes 3840 | tf_op jit(solution)/shard_map/gather | solution.py:334
  5.6 2.6 %collective-permute-start.6 = (s32[320]{0:T(512)S(1)}, s32[320]{0:T(512)S(1)}, u32[]{:S(2)}, u32[]{:S(2)}) collective-permute-start(s32[320]{0:T(512)S(1)} %gather_fusion), channel_id=1, source_target_pairs={{0,16},{8,24},{16,0},{24,8},{1,17},{9,25},{17,1},{25,9},{2,18},{10... | collective-permute-start | bytes 3848 | tf_op jit(solution)/shard_map/ppermute | solution.py:338
  8.2 1.4 collective-permute-start.7
  10.1 1.5 convolution_convert_fusion.ko_ref.vo_ref
  11.8 1.3 fusion.12
  13.3 3.4 %collective-permute-start = (bf16[256,1664]{1,0:T(8,128)(2,1)}, bf16[256,1664]{1,0:T(8,128)(2,1)S(1)}, u32[]{:S(2)}, u32[]{:S(2)}) collective-permute-start(bf16[256,1664]{1,0:T(8,128)(2,1)} %get-tuple-element.14), channel_id=1, source_target_pairs={{0,1},{1,2},{2,3},{3,4},{4,5},{5,6},{6,7},{8,9},{9,10},{10,11},{11... | collective-permute-start | bytes 2555912 | tf_op jit(solution)/shard_map/ppermute | solution.py:392
  16.8 1.3 collective-permute-start.1
  18.1 1.5 fusion.60
  20.6 4.8 %shard_map.114 = (bf16[4,4,64,384]{3,2,1,0:T(8,128)(2,1)}, bf16[4,4,64,384]{3,2,1,0:T(8,128)(2,1)}) custom-call(s32[64]{0:T(128)S(1)} %reshape.434.request_ref, bf16[4608,768]{1,0:T(8,128)(2,1)} %bitcast.40, bf16[256,256]{1,0:T(8,128)(2,1)S(1)} %fusion.16.order_ref), custom_call_target="tpu_custom_call" | custom-call | flops 402653184 | bytes 3145728 | tf_op jit(solution)/shard_map/pallas_call | solution.py:139
  25.4 7.9 %all-to-all-start = ((bf16[32,32,384]{2,1,0:T(8,128)(2,1)}), bf16[32,32,384]{2,1,0:T(8,128)(2,1)}, u32[]{:S(2)}, u32[]{:S(2)}) async-start(bf16[32,32,384]{2,1,0:T(8,128)(2,1)} %bitcast.6), calls=%async_computation | async-start | bytes 1572864 | tf_op jit(solution)/shard_map/all_to_all | solution.py:367
  33.4 4.1 %concatenate.24 = bf16[768,1024]{1,0:T(8,128)(2,1)} concatenate(bf16[768,64]{1,0:T(8,128)(2,1)S(1)} %broadcast_in_dim.54, bf16[768,192]{1,0:T(8,128)(2,1)} %get-tuple-element.18, bf16[768,64]{1,0:T(8,128)(2,1)S(1)} %broadcast_in_dim.54, bf16[768,192]{1,0:T(8,128)(2,1)} %get-tuple-element.17, bf16[768,64]{1,0:T(8,128)(2,1)S(1)} %broadcast_in_dim.54, ...), dimensions={1} | concatenate | bytes 3145728 | tf_op jit(solution)/shard_map/concatenate | solution.py:407
  37.8 1.2 broadcast_and_fusion
  39.0 3.2 %convolution_convert_fusion.1.q_ref = bf16[512,768]{1,0:T(8,128)(2,1)} fusion(bf16[768,768]{1,0:T(8,128)(2,1)} %param.12, bf16[1,512,768]{2,1,0:T(8,128)(2,1)} %param.10, f32[512]{0:T(512)S(1)} %add_rsqrt_fusion.1, f32[512]{0:T(512)S(1)} %broadcast_multiply_fusion.1), kind=kOutput, calls=%fused_computation.20 | convolution fusion | flops 605945856 | bytes 2756608 | tf_op jit(solution)/shard_map/dot_general | solution.py:384
  42.2 17.9 %collective-permute-done.kl_ref.vl_ref = bf16[256,1664]{1,0:T(8,128)(2,1)S(1)} collective-permute-done((bf16[256,1664]{1,0:T(8,128)(2,1)}, bf16[256,1664]{1,0:T(8,128)(2,1)S(1)}, u32[]{:S(2)}, u32[]{:S(2)}) %collective-permute-start) | collective-permute-done | bytes 852000 | tf_op jit(solution)/shard_map/ppermute | solution.py:392
  60.3 0.9 slice_reduce_fusion
  61.2 6.8 %all-to-all-start.1 = ((bf16[32,32,384]{2,1,0:T(8,128)(2,1)}), bf16[32,32,384]{2,1,0:T(8,128)(2,1)}, u32[]{:S(2)}, u32[]{:S(2)}) async-start(bf16[32,32,384]{2,1,0:T(8,128)(2,1)} %bitcast.5), calls=%async_computation.1 | async-start | bytes 1572864 | tf_op jit(solution)/shard_map/all_to_all | solution.py:367
  68.1 1.4 copy-done.2
  69.5 1.1 copy-done.5
  70.6 8.5 %shard_map.113 = bf16[512,768]{1,0:T(8,128)(2,1)S(1)} custom-call(f32[1,1024]{1,0:T(1,128)S(1)} %maximum_convert_fusion.valid_ref, bf16[512,768]{1,0:T(8,128)(2,1)S(1)} %copy-done.5, bf16[256,1664]{1,0:T(8,128)(2,1)S(1)} %collective-permute-done.kl_ref.vl_ref, bf16[512,1536]{1,0:T(8,128)(2,1)S(1)} %copy-done.2, ...), custom_call_target="tpu_custom_call" | custom-call | flops 2415919104 | bytes 3145728 | tf_op jit(solution)/shard_map/pallas_call | solution.py:72
  79.1 0.9 convert_reduce_fusion
  80.4 2.8 %convolution_convert_fusion.3.refs_4_ = bf16[640,384]{1,0:T(8,128)(2,1)} fusion(pred[640,1024]{1,0:T(32,128)(4,1)S(1)} %bitcast.42, bf16[1024,384]{1,0:T(8,128)(2,1)} %bitcast.7), kind=kOutput, calls=%fused_computation.23 | convolution fusion | flops 503562240 | bytes 1933312 | tf_op jit(solution)/shard_map/dot_general | solution.py:428
  83.1 1.5 collective-permute-start.8
  84.7 5.2 %all-to-all-done.1 = bf16[32,32,384]{2,1,0:T(8,128)(2,1)} async-done(((bf16[32,32,384]{2,1,0:T(8,128)(2,1)}), bf16[32,32,384]{2,1,0:T(8,128)(2,1)}, u32[]{:S(2)}, u32[]{:S(2)}) %all-to-all-start.1) | async-done | bytes 786464 | tf_op jit(solution)/shard_map/all_to_all | solution.py:367
  89.9 2.3 %convolution_convert_fusion.2.refs_6_ = bf16[640,384]{1,0:T(8,128)(2,1)S(1)} fusion(pred[640,1024]{1,0:T(32,128)(4,1)} %bitcast.41, bf16[1024,384]{1,0:T(8,128)(2,1)} %bitcast.8), kind=kOutput, calls=%fused_computation.22 | convolution fusion | flops 503562240 | bytes 1933312 | tf_op jit(solution)/shard_map/dot_general | solution.py:428
  93.0 1.0 select_convert_fusion
  94.3 2.0 %collective-permute-start.3 = (bf16[512,256]{1,0:T(8,128)(2,1)S(1)}, bf16[512,256]{1,0:T(8,128)(2,1)S(1)}, u32[]{:S(2)}, u32[]{:S(2)}) collective-permute-start(bf16[512,256]{1,0:T(8,128)(2,1)S(1)} %get-tuple-element.21), channel_id=1, source_target_pairs={{0,4},{1,5},{2,6},{3,7},{4,0},{5,1},{6,2},{7,3},{8,12},{9,13},{10,... | collective-permute-start | bytes 786440 | tf_op jit(solution)/shard_map/ppermute | solution.py:423
  96.3 1.9 %collective-permute-start.4 = (bf16[512,256]{1,0:T(8,128)(2,1)S(1)}, bf16[512,256]{1,0:T(8,128)(2,1)S(1)}, u32[]{:S(2)}, u32[]{:S(2)}) collective-permute-start(bf16[512,256]{1,0:T(8,128)(2,1)S(1)} %get-tuple-element.20), channel_id=1, source_target_pairs={{0,6},{1,7},{2,0},{3,1},{4,2},{5,3},{6,4},{7,5},{8,14},{9,15},{10,... | collective-permute-start | bytes 786440 | tf_op jit(solution)/shard_map/ppermute | solution.py:423
  98.7 6.7 %collective-permute-done.2.refs_1_ = bf16[512,256]{1,0:T(8,128)(2,1)S(1)} collective-permute-done((bf16[512,256]{1,0:T(8,128)(2,1)S(1)}, bf16[512,256]{1,0:T(8,128)(2,1)S(1)}, u32[]{:S(2)}, u32[]{:S(2)}) %collective-permute-start.2) | collective-permute-done | bytes 262176 | tf_op jit(solution)/shard_map/ppermute | solution.py:423
  105.4 10.1 %collective-permute-done.3.refs_2_ = bf16[512,256]{1,0:T(8,128)(2,1)S(1)} collective-permute-done((bf16[512,256]{1,0:T(8,128)(2,1)S(1)}, bf16[512,256]{1,0:T(8,128)(2,1)S(1)}, u32[]{:S(2)}, u32[]{:S(2)}) %collective-permute-start.3) | collective-permute-done | bytes 262176 | tf_op jit(solution)/shard_map/ppermute | solution.py:423
  116.2 37.0 %shard_map.115 = (bf16[512,768]{1,0:T(8,128)(2,1)S(1)}, f32[1,2688]{1,0:T(1,128)S(1)}) custom-call(f32[1,128]{1,0:T(1,128)S(1)} %broadcast_in_dim.50.count_ref, bf16[512,768]{1,0:T(8,128)(2,1)S(1)} %get-tuple-element.27.middle_ref, bf16[768,768]{1,0:T(8,128)(2,1)S(1)} %copy-done.4, bf16[512,256]{1,0:T(8,128)(2,1)S(1)} %get-tuple-element.23.refs_0_, ...), custom_call_target="tpu_custom_call" | custom-call | flops 16106127360 | bytes 3145728 | tf_op jit(solution)/shard_map/pallas_call | solution.py:282
  153.2 0.9 copy-done.3
  156.1 2.1 %copy.16 = bf16[1,512,768]{2,1,0:T(8,128)(2,1)} copy(bf16[1,512,768]{2,1,0:T(8,128)(2,1)} %bitcast.39) | data formatting | bytes 1572864
  (83 shorter events, 7.6 us)
Async XLA Ops:
  0.6 9.5 %copy-start = (bf16[768,1536]{1,0:T(8,128)(2,1)S(1)}, bf16[768,1536]{1,0:T(8,128)(2,1)}, u32[]{:S(2)}) copy-start(bf16[768,1536]{1,0:T(8,128)(2,1)} %param.13) | copy-start | bytes 7077892
  0.6 8.9 %copy-start.6 = (bf16[1,512,768]{2,1,0:T(8,128)(2,1)S(1)}, bf16[1,512,768]{2,1,0:T(8,128)(2,1)}, u32[]{:S(2)}) copy-start(bf16[1,512,768]{2,1,0:T(8,128)(2,1)} %param.10) | copy-start | bytes 2359300
  1.5 8.6 %copy-start.11 = (s32[1,512]{1,0:T(1,128)S(1)}, s32[1,512]{1,0:T(1,128)}, u32[]{:S(2)}) copy-start(s32[1,512]{1,0:T(1,128)} %param.11) | copy-start | bytes 6148
  5.1 14.9 %collective-permute-start.5 = (s32[320]{0:T(512)S(1)}, s32[320]{0:T(512)S(1)}, u32[]{:S(2)}, u32[]{:S(2)}) collective-permute-start(s32[320]{0:T(512)S(1)} %gather_fusion), channel_id=1, source_target_pairs={{0,8},{8,16},{16,24},{24,0},{1,9},{9,17},{17,25},{25,1},{2,10},{10... | collective-permute-start | bytes 3848 | tf_op jit(solution)/shard_map/ppermute | solution.py:338
  5.6 14.4 %collective-permute-start.6 = (s32[320]{0:T(512)S(1)}, s32[320]{0:T(512)S(1)}, u32[]{:S(2)}, u32[]{:S(2)}) collective-permute-start(s32[320]{0:T(512)S(1)} %gather_fusion), channel_id=1, source_target_pairs={{0,16},{8,24},{16,0},{24,8},{1,17},{9,25},{17,1},{25,9},{2,18},{10... | collective-permute-start | bytes 3848 | tf_op jit(solution)/shard_map/ppermute | solution.py:338
  8.2 11.8 %collective-permute-start.7 = (s32[320]{0:T(512)S(1)}, s32[320]{0:T(512)S(1)}, u32[]{:S(2)}, u32[]{:S(2)}) collective-permute-start(s32[320]{0:T(512)S(1)} %gather_fusion), channel_id=1, source_target_pairs={{0,24},{8,0},{16,8},{24,16},{1,25},{9,1},{17,9},{25,17},{2,26},{10... | collective-permute-start | bytes 3848 | tf_op jit(solution)/shard_map/ppermute | solution.py:338
  11.6 1.7 %copy-start.1 = (bf16[512,1536]{1,0:T(8,128)(2,1)}, bf16[512,1536]{1,0:T(8,128)(2,1)S(1)}, u32[]{:S(2)}) copy-start(bf16[512,1536]{1,0:T(8,128)(2,1)S(1)} %convolution_convert_fusion.ko_ref.vo_ref) | copy-start | bytes 4718596
  11.8 6.3 %copy-start.8 = (bf16[768,768]{1,0:T(8,128)(2,1)S(1)}, bf16[768,768]{1,0:T(8,128)(2,1)}, u32[]{:S(2)}) copy-start(bf16[768,768]{1,0:T(8,128)(2,1)} %param.15) | copy-start | bytes 3538948
  13.3 46.8 %collective-permute-start = (bf16[256,1664]{1,0:T(8,128)(2,1)}, bf16[256,1664]{1,0:T(8,128)(2,1)S(1)}, u32[]{:S(2)}, u32[]{:S(2)}) collective-permute-start(bf16[256,1664]{1,0:T(8,128)(2,1)} %get-tuple-element.14), channel_id=1, source_target_pairs={{0,1},{1,2},{2,3},{3,4},{4,5},{5,6},{6,7},{8,9},{9,10},{10,11},{11... | collective-permute-start | bytes 2555912 | tf_op jit(solution)/shard_map/ppermute | solution.py:392
  16.8 43.5 %collective-permute-start.1 = (bf16[256,1664]{1,0:T(8,128)(2,1)}, bf16[256,1664]{1,0:T(8,128)(2,1)}, u32[]{:S(2)}, u32[]{:S(2)}) collective-permute-start(bf16[256,1664]{1,0:T(8,128)(2,1)} %get-tuple-element.15), channel_id=1, source_target_pairs={{1,0},{2,1},{3,2},{4,3},{5,4},{6,5},{7,6},{9,8},{10,9},{11,10},{12... | collective-permute-start | bytes 2555912 | tf_op jit(solution)/shard_map/ppermute | solution.py:393
  25.4 35.9 %all-to-all-start = ((bf16[32,32,384]{2,1,0:T(8,128)(2,1)}), bf16[32,32,384]{2,1,0:T(8,128)(2,1)}, u32[]{:S(2)}, u32[]{:S(2)}) async-start(bf16[32,32,384]{2,1,0:T(8,128)(2,1)} %bitcast.6), calls=%async_computation | async-start | bytes 1572864 | tf_op jit(solution)/shard_map/all_to_all | solution.py:367
  61.2 28.6 %all-to-all-start.1 = ((bf16[32,32,384]{2,1,0:T(8,128)(2,1)}), bf16[32,32,384]{2,1,0:T(8,128)(2,1)}, u32[]{:S(2)}, u32[]{:S(2)}) async-start(bf16[32,32,384]{2,1,0:T(8,128)(2,1)} %bitcast.5), calls=%async_computation.1 | async-start | bytes 1572864 | tf_op jit(solution)/shard_map/all_to_all | solution.py:367
  68.1 1.4 copy-start.2
  69.5 1.1 copy-start.5
  70.6 8.5 %copy-start.7 = (bf16[1,512,768]{2,1,0:T(8,128)(2,1)S(1)}, bf16[1,512,768]{2,1,0:T(8,128)(2,1)}, u32[]{:S(2)}) copy-start(bf16[1,512,768]{2,1,0:T(8,128)(2,1)} %param.10) | copy-start | bytes 2359300
  70.6 8.5 %copy-start.12 = (bf16[768,768]{1,0:T(8,128)(2,1)S(1)}, bf16[768,768]{1,0:T(8,128)(2,1)}, u32[]{:S(2)}) copy-start(bf16[768,768]{1,0:T(8,128)(2,1)} %param.14) | copy-start | bytes 3538948
  79.1 1.3 copy-start.10
  83.1 32.4 %collective-permute-start.8 = (bf16[640,384]{1,0:T(8,128)(2,1)}, bf16[640,384]{1,0:T(8,128)(2,1)}, u32[]{:S(2)}, u32[]{:S(2)}) collective-permute-start(bf16[640,384]{1,0:T(8,128)(2,1)} %convolution_convert_fusion.3.refs_4_), channel_id=1, source_target_pairs={{0,1},{1,0},{2,3},{3,2},{4,5},{5,4},{6,7},{7,6},{8,9},{9,8},{10,11... | collective-permute-start | bytes 1474568 | tf_op jit(solution)/shard_map/ppermute | solution.py:434
  89.8 3.2 %copy-start.9 = (bf16[768,1024]{1,0:T(8,128)(2,1)S(1)}, bf16[768,1024]{1,0:T(8,128)(2,1)}, u32[]{:S(2)}) copy-start(bf16[768,1024]{1,0:T(8,128)(2,1)} %concatenate.24) | copy-start | bytes 4718596
  92.2 23.4 %collective-permute-start.9 = (bf16[640,384]{1,0:T(8,128)(2,1)S(1)}, bf16[640,384]{1,0:T(8,128)(2,1)S(1)}, u32[]{:S(2)}, u32[]{:S(2)}) collective-permute-start(bf16[640,384]{1,0:T(8,128)(2,1)S(1)} %convolution_convert_fusion.2.refs_6_), channel_id=1, source_target_pairs={{0,1},{1,0},{2,3},{3,2},{4,5},{5,4},{6,7},{7,6},{8,9},{9,8},{10,11... | collective-permute-start | bytes 1474568 | tf_op jit(solution)/shard_map/ppermute | solution.py:434
  94.1 22.1 %copy-start.4 = (bf16[768,768]{1,0:T(8,128)(2,1)S(1)}, bf16[768,768]{1,0:T(8,128)(2,1)}, u32[]{:S(2)}) copy-start(bf16[768,768]{1,0:T(8,128)(2,1)} %w_ref.1) | copy-start | bytes 3538948
  94.2 11.1 %collective-permute-start.2 = (bf16[512,256]{1,0:T(8,128)(2,1)S(1)}, bf16[512,256]{1,0:T(8,128)(2,1)S(1)}, u32[]{:S(2)}, u32[]{:S(2)}) collective-permute-start(bf16[512,256]{1,0:T(8,128)(2,1)S(1)} %get-tuple-element.22), channel_id=1, source_target_pairs={{0,2},{1,3},{2,4},{3,5},{4,6},{5,7},{6,0},{7,1},{8,10},{9,11},{10,... | collective-permute-start | bytes 786440 | tf_op jit(solution)/shard_map/ppermute | solution.py:423
  94.3 21.2 %collective-permute-start.3 = (bf16[512,256]{1,0:T(8,128)(2,1)S(1)}, bf16[512,256]{1,0:T(8,128)(2,1)S(1)}, u32[]{:S(2)}, u32[]{:S(2)}) collective-permute-start(bf16[512,256]{1,0:T(8,128)(2,1)S(1)} %get-tuple-element.21), channel_id=1, source_target_pairs={{0,4},{1,5},{2,6},{3,7},{4,0},{5,1},{6,2},{7,3},{8,12},{9,13},{10,... | collective-permute-start | bytes 786440 | tf_op jit(solution)/shard_map/ppermute | solution.py:423
  96.3 19.3 %collective-permute-start.4 = (bf16[512,256]{1,0:T(8,128)(2,1)S(1)}, bf16[512,256]{1,0:T(8,128)(2,1)S(1)}, u32[]{:S(2)}, u32[]{:S(2)}) collective-permute-start(bf16[512,256]{1,0:T(8,128)(2,1)S(1)} %get-tuple-element.20), channel_id=1, source_target_pairs={{0,6},{1,7},{2,0},{3,1},{4,2},{5,3},{6,4},{7,5},{8,14},{9,15},{10,... | collective-permute-start | bytes 786440 | tf_op jit(solution)/shard_map/ppermute | solution.py:423
  153.2 0.9 copy-start.3

commit v4 on v3

--- a/solution.py
+++ b/solution.py
@@ -13,7 +13,7 @@
 HALF_WIN = 256
 DESC = 8
 GROUPS = 4
-CHUNKS = 2
+CHUNKS = 1
 EXP2_SCALE = math.log2(math.e) / math.sqrt(HEAD)
 F32 = jnp.float32
 BF16 = jnp.bfloat16
@@ -26,7 +26,7 @@
     return centered * lax.rsqrt(spread + 1e-05)
 
 
-def window_kernel(valid_ref, q_ref, kl_ref, ko_ref, kh_ref, vl_ref, vo_ref, vh_ref, o_ref, bias):
+def window_kernel(valid_ref, q_ref, k_ref, v_ref, o_ref, bias):
     rows = q_ref.shape[0]
     half = HALF_WIN
     blocks = rows // half
@@ -41,8 +41,8 @@
             allowed = (j >= i) & (j <= i + 2 * half) & (ok | (j == i + half))
             bias[b] = jnp.where(allowed, 0.0, -1e30)
 
-    k = jnp.concatenate([kl_ref[...], ko_ref[...], kh_ref[...]], axis=0)
-    v = jnp.concatenate([vl_ref[...], vo_ref[...], vh_ref[...]], axis=0)
+    k = k_ref[...]
+    v = v_ref[...]
     v = jnp.concatenate([v, jnp.ones_like(v)], axis=1)
     lane = lax.broadcasted_iota(jnp.int32, (half, 2 * HEAD), 1)
     for b in range(blocks):
@@ -61,7 +61,7 @@
         o_ref[b * half : (b + 1) * half, :] = jnp.where(lane < HEAD, outs[0], outs[1]).astype(BF16)
 
 
-def window_attend(valid, query, low, own, high):
+def window_attend(valid, query, keyval):
     rows, width = query.shape
     pairs = width // (2 * HEAD)
     span = rows + 2 * HALF_WIN
@@ -76,12 +76,8 @@
         in_specs=[
             pl.BlockSpec((1, span), lambda p: (0, 0)),
             cols(rows, 0),
-            cols(HALF_WIN, 0),
-            cols(rows, 0),
-            cols(HALF_WIN, 0),
-            cols(HALF_WIN, pairs),
-            cols(rows, pairs),
-            cols(HALF_WIN, pairs),
+            cols(span, 0),
+            cols(span, pairs),
         ],
         out_specs=cols(rows, 0),
         scratch_shapes=[pltpu.VMEM((rows // HALF_WIN, HALF_WIN, 3 * HALF_WIN), F32)],
@@ -91,7 +87,7 @@
             bytes_accessed=8 * rows * width,
             transcendentals=rows * 3 * HALF_WIN * HEADS,
         ),
-    )(valid, query, low, own, high, low, own, high)
+    )(valid, query, keyval, keyval)
 
 
 def gather_kernel(docs, capacity, request_ref, cache_ref, order_ref, *refs):
@@ -331,6 +327,16 @@
     slots = devices * capacity
     part = width // GROUPS
 
+    up = [(i, i + 1) for i in range(seq_count - 1)]
+    down = [(i + 1, i) for i in range(seq_count - 1)]
+    live = (doc_tokens != 0).astype(F32)
+    flagged = jnp.concatenate(
+        [doc_hidden, jnp.broadcast_to(live.astype(BF16)[:, None], (tok_rows, 2 * HEAD))], axis=1
+    )
+    low = lax.ppermute(flagged[tok_rows - HALF_WIN :], "seq", up)
+    high = lax.ppermute(flagged[:HALF_WIN], "seq", down)
+    extended = jnp.concatenate([low, flagged, high])
+
     cache_rows = code_row[shortlist[0]]
     relative = [cache_rows]
     for r in range(1, doc_count):
@@ -380,20 +386,13 @@
     )
     choose = choose.astype(BF16).reshape(inner * cand_count, -1)
 
-    normed = layer_norm(doc_hidden.astype(F32)).astype(BF16)
-    query = jnp.dot(normed, w_query, preferred_element_type=F32).astype(BF16)
+    normed = layer_norm(extended[:, :width].astype(F32)).astype(BF16)
     keyval = jnp.dot(normed, w_keyval, preferred_element_type=F32).astype(BF16)
-    up = [(i, i + 1) for i in range(seq_count - 1)]
-    down = [(i + 1, i) for i in range(seq_count - 1)]
-    live = (doc_tokens != 0).astype(F32)
-    flagged = jnp.concatenate(
-        [keyval, jnp.broadcast_to(live.astype(BF16)[:, None], (tok_rows, 2 * HEAD))], axis=1
-    )
-    low = lax.ppermute(flagged[tok_rows - HALF_WIN :], "seq", up)
-    high = lax.ppermute(flagged[:HALF_WIN], "seq", down)
-    valid = jnp.concatenate([low[:, 2 * width], live.astype(BF16), high[:, 2 * width]])
-    valid = valid.astype(F32)[None]
-    context = window_attend(valid, query, low, keyval, high)
+    query = jnp.dot(
+        normed[HALF_WIN : HALF_WIN + tok_rows], w_query, preferred_element_type=F32
+    ).astype(BF16)
+    valid = extended[:, width].astype(F32)[None]
+    context = window_attend(valid, query, keyval)
     middle = (
         doc_hidden.astype(F32) + jnp.dot(context, w_out, preferred_element_type=F32)
     ).astype(BF16)

time: 159 us -> 141 us (0.89)
  waiting for transfers between devices: 39.9 us -> 28.7 us
  starting transfers between devices: 30.2 us -> 20.8 us
  other arithmetic: 5.76 us -> 14 us
  Pallas kernels: 50.3 us -> 46.7 us
    ppermute x1, waiting for transfers between devices: 17.9 us -> 0.01 us  [local(): low = lax.ppermute(flagged[tok_rows - HALF_WIN:], 'seq', up)]
    all_to_all x2 -> x1, starting transfers between devices: 14.7 us -> 6.52 us  [local(): lax.all_to_all(chunk, ('doc', 'seq'), split_axis=0, concat_axis=0, tiled=...]
    all_to_all x2 -> x1, waiting for transfers between devices: 5.17 us -> 11.7 us  [local(): lax.all_to_all(chunk, ('doc', 'seq'), split_axis=0, concat_axis=0, tiled=...]
    convert_element_type x1 -> x3, other arithmetic: 0.01 us -> 4.33 us  [the longest x1 3.31 us: local(): normed = layer_norm(extended[:, :width].astype(F32)).astype(BF16)]
    dot_general x1, matrix products: 3.23 us -> 0.78 us  [local(): jnp.dot(normed[HALF_WIN:HALF_WIN + tok_rows], w_query, preferred_element_...]
    ppermute x2 -> x1, starting transfers between devices: 2.4 us -> 0.51 us  [local(): pieces.append(lax.ppermute(own_rows, 'seq', step))]
    pallas_call x1, Pallas kernels: 37 us -> 35.4 us  [cross_attend(): pl.pallas_call(functools.partial(cross_kernel, seq_count, 512, len(pieces...]
    unnamed x27 -> x25, local copies, waits for them, and re-layouts: 5.72 us -> 4.8 us
  transfers between devices with their start and end apart: 12 -> 10, of which waited for: 4 -> 3; matrix products, arithmetic and copies ran while one was open for 15% -> 19% of each run, Pallas kernels for 8% -> 8%
where the time goes in v4:
time: 141 us
  Pallas kernels  46.7 us (33%)
  waiting for transfers between devices  28.7 us (20%)
  starting transfers between devices  20.8 us (15%)
  local copies, waits for them, and re-layouts  17.8 us (13%)
  other arithmetic  14 us (10%)
  matrix products  11 us (8%)
  between operations  1.75 us (1%)
    pallas_call x1, Pallas kernels, cross_attend(): pl.pallas_call(functools.partial(cross_kernel, seq_count, 512, len(pieces...  35.4 us
    ppermute x3, waiting for transfers between devices, local(): lax.ppermute(piece(cross_query, (group + r) % GROUPS), 'seq', turn(r))  17 us
    all_to_all x1, waiting for transfers between devices, local(): lax.all_to_all(chunk, ('doc', 'seq'), split_axis=0, concat_axis=0, tiled=...  11.7 us
    pallas_call x1, Pallas kernels, window_attend(): pl.pallas_call(window_kernel, grid=(pairs,), out_shape=jax.ShapeDtypeStru...  7.63 us
    all_to_all x1, starting transfers between devices, local(): lax.all_to_all(chunk, ('doc', 'seq'), split_axis=0, concat_axis=0, tiled=...  6.52 us
    dot_general x1, matrix products, local(): jnp.dot(choose, chunk.reshape(-1, 2 * part), preferred_element_type=F32)  5.19 us
    unnamed x25, local copies, waits for them, and re-layouts  4.8 us
    ppermute x3, starting transfers between devices, local(): lax.ppermute(cache_rows, 'doc', [(i, (i + r) % doc_count) for i in range(...  4.48 us
  transfers between devices with their start and end apart: 10, of which 3 were waited for; matrix products, arithmetic and copies ran while one was open for 19% of the time, Pallas kernels for 8%

profile of v4, /device:TPU:0, one launch (start us, length us, event | category | flops | bytes accessed | tf_op | source)
XLA Modules:
  0.0 140.7 jit_solution(18370195886467302227)
XLA Ops:
  0.7 0.8 fusion.39
  1.5 3.5 %gather_fusion = s32[320]{0:T(512)S(1)} fusion(s32[9216]{0:T(1024)} %param.18, s32[1024]{0:T(1024)S(1)} %pad_clamp_fusion), kind=kCustom, calls=%fused_computation | custom fusion | bytes 3840 | tf_op jit(solution)/shard_map/gather | solution.py:340
  5.6 2.6 %collective-permute-start.6 = (s32[320]{0:T(512)S(1)}, s32[320]{0:T(512)S(1)}, u32[]{:S(2)}, u32[]{:S(2)}) collective-permute-start(s32[320]{0:T(512)S(1)} %gather_fusion), channel_id=1, source_target_pairs={{0,16},{8,24},{16,0},{24,8},{1,17},{9,25},{17,1},{25,9},{2,18},{10... | collective-permute-start | bytes 3848 | tf_op jit(solution)/shard_map/ppermute | solution.py:344
  8.2 1.4 collective-permute-start.7
  10.4 1.0 fusion.13
  11.4 4.2 %collective-permute-start = (bf16[256,896]{1,0:T(8,128)(2,1)}, bf16[256,896]{1,0:T(8,128)(2,1)}, u32[]{:S(2)}, u32[]{:S(2)}) collective-permute-start(bf16[256,896]{1,0:T(8,128)(2,1)} %get-tuple-element.14), channel_id=1, source_target_pairs={{0,1},{1,2},{2,3},{3,4},{4,5},{5,6},{6,7},{8,9},{9,10},{10,11},{11... | collective-permute-start | bytes 1376264 | tf_op jit(solution)/shard_map/ppermute | solution.py:336
  15.6 1.3 collective-permute-start.1
  17.7 2.7 %broadcast_and_fusion = pred[4,320,2048]{2,1,0:T(32,128)(4,1)} fusion(pred[4,2048]{1,0:T(4,128)(4,1)S(1)} %iota_compare_fusion.7, pred[320,2048]{1,0:T(8,128)(4,1)S(1)} %broadcast_compare_fusion), kind=kLoop, calls=%fused_computation.1 | loop fusion | flops 2621440 | bytes 3284992 | tf_op jit(solution)/shard_map/and | solution.py:384
  21.0 3.6 %shard_map.114 = bf16[4,4,128,384]{3,2,1,0:T(8,128)(2,1)S(1)} custom-call(s32[64]{0:T(128)S(1)} %reshape.373.request_ref, bf16[4608,768]{1,0:T(8,128)(2,1)} %bitcast.29, bf16[256,256]{1,0:T(8,128)(2,1)S(1)} %fusion.14.order_ref), custom_call_target="tpu_custom_call" | custom-call | flops 402653184 | bytes 3145728 | tf_op jit(solution)/shard_map/pallas_call | solution.py:135
  24.7 1.2 copy-done.1
  25.8 6.5 %all-to-all-start = ((bf16[32,64,384]{2,1,0:T(8,128)(2,1)}), bf16[32,64,384]{2,1,0:T(8,128)(2,1)}, u32[]{:S(2)}, u32[]{:S(2)}) async-start(bf16[32,64,384]{2,1,0:T(8,128)(2,1)} %bitcast.21), calls=%async_computation | async-start | bytes 3145728 | tf_op jit(solution)/shard_map/all_to_all | solution.py:373
  32.4 3.0 %fusion.52 = (bf16[768,192]{1,0:T(8,128)(2,1)}, bf16[768,192]{1,0:T(8,128)(2,1)}, bf16[768,192]{1,0:T(8,128)(2,1)}, bf16[768,192]{1,0:T(8,128)(2,1)}) fusion(bf16[768,768]{1,0:T(8,128)(2,1)} %param.15), kind=kLoop, calls=%fused_computation.133 | loop fusion | bytes 2359296 | tf_op jit(solution)/shard_map/slice | solution.py:405
  35.4 4.2 %concatenate.11 = bf16[768,1024]{1,0:T(8,128)(2,1)} concatenate(bf16[768,64]{1,0:T(8,128)(2,1)S(1)} %broadcast_in_dim.54, bf16[768,192]{1,0:T(8,128)(2,1)} %get-tuple-element.8, bf16[768,64]{1,0:T(8,128)(2,1)S(1)} %broadcast_in_dim.54, bf16[768,192]{1,0:T(8,128)(2,1)} %get-tuple-element.7, bf16[768,64]{1,0:T(8,128)(2,1)S(1)} %broadcast_in_dim.54, ...), dimensions={1} | concatenate | bytes 3145728 | tf_op jit(solution)/shard_map/concatenate | solution.py:406
  39.6 1.0 convert_reduce_fusion.2
  40.6 1.4 convert_reduce_fusion
  42.0 1.7 %fusion.2 = f32[1024]{0:T(1024)S(1)} fusion(f32[1024]{0:T(1024)S(1)} %broadcast_multiply_fusion, bf16[256,896]{1,0:T(8,128)(2,1)} %collective-permute-done.1, bf16[512,128]{1,0:T(8,128)(2,1)S(1)} %copy-done.7, bf16[512,768]{1,0:T(8,128)(2,1)S(1)} %bitcast.27, bf16[256,896]{1,0:T(8,128)(2,1)} %collective-permute-done), kind=kLoop, calls=%fused_computation.7 | loop fusion | flops 8649728 | bytes 1843200 | tf_op jit(solution)/shard_map/reduce_sum | solution.py:25
  43.8 3.3 %fusion.3 = bf16[1024,768]{1,0:T(8,128)(2,1)S(1)} fusion(f32[1024]{0:T(1024)S(1)} %add_rsqrt_fusion, f32[1024]{0:T(1024)S(1)} %broadcast_multiply_fusion, bf16[256,896]{1,0:T(8,128)(2,1)} %collective-permute-done.1, bf16[512,128]{1,0:T(8,128)(2,1)S(1)} %copy-done.7, bf16[512,768]{1,0:T(8,128)(2,1)S(1)} %bitcast.28, bf16[256,896]{1,0:T(8,128)(2,1)} %collective-permute-done), kind=kLoop, calls=%fused_computation.8 | loop fusion | flops 8650752 | bytes 3416064 | tf_op jit(solution)/shard_map/convert_element_type | solution.py:389
  47.1 0.8 convolution_convert_fusion.2.q_ref
  47.9 2.8 %convolution_convert_fusion.k_ref.v_ref = bf16[1024,1536]{1,0:T(8,128)(2,1)S(1)} fusion(bf16[1024,768]{1,0:T(8,128)(2,1)S(1)} %fusion.3, bf16[768,1536]{1,0:T(8,128)(2,1)S(1)} %copy-done), kind=kOutput, calls=%fused_computation.4 | convolution fusion | flops 2417491968 | bytes 7077888 | tf_op jit(solution)/shard_map/dot_general | solution.py:390
  50.8 7.6 %shard_map.113 = bf16[512,768]{1,0:T(8,128)(2,1)S(1)} custom-call(f32[1,1024]{1,0:T(1,128)S(1)} %bitcast.23, bf16[512,768]{1,0:T(8,128)(2,1)S(1)} %convolution_convert_fusion.2.q_ref, bf16[1024,1536]{1,0:T(8,128)(2,1)S(1)} %convolution_convert_fusion.k_ref.v_ref, bf16[1024,1536]{1,0:T(8,128)(2,1)S(1)} %convolution_convert_fusion.k_ref.v_ref), custom_call_target="tpu_custom_call" | custom-call | flops 2415919104 | bytes 3145728 | tf_op jit(solution)/shard_map/pallas_call | solution.py:72
  58.4 0.9 convert_reduce_fusion.1
  59.3 11.7 %all-to-all-done = bf16[32,64,384]{2,1,0:T(8,128)(2,1)} async-done(((bf16[32,64,384]{2,1,0:T(8,128)(2,1)}), bf16[32,64,384]{2,1,0:T(8,128)(2,1)}, u32[]{:S(2)}, u32[]{:S(2)}) %all-to-all-start) | async-done | bytes 1572896 | tf_op jit(solution)/shard_map/all_to_all | solution.py:373
  71.0 5.2 %convolution_convert_fusion.1.refs_4_ = bf16[1280,384]{1,0:T(8,128)(2,1)S(1)} fusion(pred[1280,2048]{1,0:T(32,128)(4,1)} %bitcast.30, bf16[2048,384]{1,0:T(8,128)(2,1)} %bitcast.6), kind=kOutput, calls=%fused_computation.9 | convolution fusion | flops 2013757440 | bytes 5177344 | tf_op jit(solution)/shard_map/dot_general | solution.py:427
  77.1 1.0 select_convert_fusion
  78.4 1.6 %collective-permute-start.3 = (bf16[512,256]{1,0:T(8,128)(2,1)S(1)}, bf16[512,256]{1,0:T(8,128)(2,1)S(1)}, u32[]{:S(2)}, u32[]{:S(2)}) collective-permute-start(bf16[512,256]{1,0:T(8,128)(2,1)S(1)} %get-tuple-element.11), channel_id=1, source_target_pairs={{0,4},{1,5},{2,6},{3,7},{4,0},{5,1},{6,2},{7,3},{8,12},{9,13},{10,... | collective-permute-start | bytes 786440 | tf_op jit(solution)/shard_map/ppermute | solution.py:422
  80.0 2.2 %collective-permute-start.4 = (bf16[512,256]{1,0:T(8,128)(2,1)S(1)}, bf16[512,256]{1,0:T(8,128)(2,1)S(1)}, u32[]{:S(2)}, u32[]{:S(2)}) collective-permute-start(bf16[512,256]{1,0:T(8,128)(2,1)S(1)} %get-tuple-element.10), channel_id=1, source_target_pairs={{0,6},{1,7},{2,0},{3,1},{4,2},{5,3},{6,4},{7,5},{8,14},{9,15},{10,... | collective-permute-start | bytes 786440 | tf_op jit(solution)/shard_map/ppermute | solution.py:422
  82.8 6.7 %collective-permute-done.2.refs_1_ = bf16[512,256]{1,0:T(8,128)(2,1)S(1)} collective-permute-done((bf16[512,256]{1,0:T(8,128)(2,1)S(1)}, bf16[512,256]{1,0:T(8,128)(2,1)S(1)}, u32[]{:S(2)}, u32[]{:S(2)}) %collective-permute-start.2) | collective-permute-done | bytes 262176 | tf_op jit(solution)/shard_map/ppermute | solution.py:422
  89.4 10.3 %collective-permute-done.3.refs_2_ = bf16[512,256]{1,0:T(8,128)(2,1)S(1)} collective-permute-done((bf16[512,256]{1,0:T(8,128)(2,1)S(1)}, bf16[512,256]{1,0:T(8,128)(2,1)S(1)}, u32[]{:S(2)}, u32[]{:S(2)}) %collective-permute-start.3) | collective-permute-done | bytes 262176 | tf_op jit(solution)/shard_map/ppermute | solution.py:422
  99.8 0.6 broadcast_in_dim.50.count_ref
  100.4 35.4 %shard_map.115 = (bf16[512,768]{1,0:T(8,128)(2,1)S(1)}, f32[1,2688]{1,0:T(1,128)S(1)}) custom-call(f32[1,128]{1,0:T(1,128)S(1)} %broadcast_in_dim.50.count_ref, bf16[512,768]{1,0:T(8,128)(2,1)S(1)} %get-tuple-element.17.middle_ref, bf16[768,768]{1,0:T(8,128)(2,1)S(1)} %copy-done.3, bf16[512,256]{1,0:T(8,128)(2,1)S(1)} %get-tuple-element.13.refs_0_, ...), custom_call_target="tpu_custom_call" | custom-call | flops 16106127360 | bytes 3145728 | tf_op jit(solution)/shard_map/pallas_call | solution.py:278
  135.9 0.9 copy-done.2
  138.7 2.1 %copy.15 = bf16[1,512,768]{2,1,0:T(8,128)(2,1)} copy(bf16[1,512,768]{2,1,0:T(8,128)(2,1)} %bitcast.22) | data formatting | bytes 1572864
  (73 shorter events, 5.7 us)
Async XLA Ops:
  0.6 47.3 %copy-start = (bf16[768,1536]{1,0:T(8,128)(2,1)S(1)}, bf16[768,1536]{1,0:T(8,128)(2,1)}, u32[]{:S(2)}) copy-start(bf16[768,1536]{1,0:T(8,128)(2,1)} %param.13) | copy-start | bytes 7077892
  0.6 8.9 %copy-start.9 = (s32[1,512]{1,0:T(1,128)S(1)}, s32[1,512]{1,0:T(1,128)}, u32[]{:S(2)}) copy-start(s32[1,512]{1,0:T(1,128)} %param.11) | copy-start | bytes 6148
  0.7 9.7 %copy-start.4 = (bf16[1,512,768]{2,1,0:T(8,128)(2,1)S(1)}, bf16[1,512,768]{2,1,0:T(8,128)(2,1)}, u32[]{:S(2)}) copy-start(bf16[1,512,768]{2,1,0:T(8,128)(2,1)} %param.10) | copy-start | bytes 2359300
  5.1 15.3 %collective-permute-start.5 = (s32[320]{0:T(512)S(1)}, s32[320]{0:T(512)S(1)}, u32[]{:S(2)}, u32[]{:S(2)}) collective-permute-start(s32[320]{0:T(512)S(1)} %gather_fusion), channel_id=1, source_target_pairs={{0,8},{8,16},{16,24},{24,0},{1,9},{9,17},{17,25},{25,1},{2,10},{10... | collective-permute-start | bytes 3848 | tf_op jit(solution)/shard_map/ppermute | solution.py:344
  5.6 14.8 %collective-permute-start.6 = (s32[320]{0:T(512)S(1)}, s32[320]{0:T(512)S(1)}, u32[]{:S(2)}, u32[]{:S(2)}) collective-permute-start(s32[320]{0:T(512)S(1)} %gather_fusion), channel_id=1, source_target_pairs={{0,16},{8,24},{16,0},{24,8},{1,17},{9,25},{17,1},{25,9},{2,18},{10... | collective-permute-start | bytes 3848 | tf_op jit(solution)/shard_map/ppermute | solution.py:344
  8.2 12.3 %collective-permute-start.7 = (s32[320]{0:T(512)S(1)}, s32[320]{0:T(512)S(1)}, u32[]{:S(2)}, u32[]{:S(2)}) collective-permute-start(s32[320]{0:T(512)S(1)} %gather_fusion), channel_id=1, source_target_pairs={{0,24},{8,0},{16,8},{24,16},{1,25},{9,1},{17,9},{25,17},{2,26},{10... | collective-permute-start | bytes 3848 | tf_op jit(solution)/shard_map/ppermute | solution.py:344
  9.7 0.7 copy-start.6
  11.4 28.2 %collective-permute-start = (bf16[256,896]{1,0:T(8,128)(2,1)}, bf16[256,896]{1,0:T(8,128)(2,1)}, u32[]{:S(2)}, u32[]{:S(2)}) collective-permute-start(bf16[256,896]{1,0:T(8,128)(2,1)} %get-tuple-element.14), channel_id=1, source_target_pairs={{0,1},{1,2},{2,3},{3,4},{4,5},{5,6},{6,7},{8,9},{9,10},{10,11},{11... | collective-permute-start | bytes 1376264 | tf_op jit(solution)/shard_map/ppermute | solution.py:336
  15.6 24.0 %collective-permute-start.1 = (bf16[256,896]{1,0:T(8,128)(2,1)}, bf16[256,896]{1,0:T(8,128)(2,1)}, u32[]{:S(2)}, u32[]{:S(2)}) collective-permute-start(bf16[256,896]{1,0:T(8,128)(2,1)} %get-tuple-element.15), channel_id=1, source_target_pairs={{1,0},{2,1},{3,2},{4,3},{5,4},{6,5},{7,6},{9,8},{10,9},{11,10},{12... | collective-permute-start | bytes 1376264 | tf_op jit(solution)/shard_map/ppermute | solution.py:337
  24.7 1.2 copy-start.1
  25.8 45.2 %all-to-all-start = ((bf16[32,64,384]{2,1,0:T(8,128)(2,1)}), bf16[32,64,384]{2,1,0:T(8,128)(2,1)}, u32[]{:S(2)}, u32[]{:S(2)}) async-start(bf16[32,64,384]{2,1,0:T(8,128)(2,1)} %bitcast.21), calls=%async_computation | async-start | bytes 3145728 | tf_op jit(solution)/shard_map/all_to_all | solution.py:373
  35.4 4.2 %copy-start.7 = (bf16[512,128]{1,0:T(8,128)(2,1)S(1)}, bf16[512,128]{1,0:T(8,128)(2,1)}, u32[]{:S(2)}) copy-start(bf16[512,128]{1,0:T(8,128)(2,1)} %copy-done.6) | copy-start | bytes 393220
  43.8 3.3 %copy-start.10 = (bf16[768,768]{1,0:T(8,128)(2,1)S(1)}, bf16[768,768]{1,0:T(8,128)(2,1)}, u32[]{:S(2)}) copy-start(bf16[768,768]{1,0:T(8,128)(2,1)} %param.12) | copy-start | bytes 3538948
  50.8 7.7 %copy-start.5 = (bf16[1,512,768]{2,1,0:T(8,128)(2,1)S(1)}, bf16[1,512,768]{2,1,0:T(8,128)(2,1)}, u32[]{:S(2)}) copy-start(bf16[1,512,768]{2,1,0:T(8,128)(2,1)} %param.10) | copy-start | bytes 2359300
  50.8 7.7 %copy-start.11 = (bf16[768,768]{1,0:T(8,128)(2,1)S(1)}, bf16[768,768]{1,0:T(8,128)(2,1)}, u32[]{:S(2)}) copy-start(bf16[768,768]{1,0:T(8,128)(2,1)} %param.14) | copy-start | bytes 3538948
  71.0 6.1 %copy-start.8 = (bf16[768,1024]{1,0:T(8,128)(2,1)S(1)}, bf16[768,1024]{1,0:T(8,128)(2,1)}, u32[]{:S(2)}) copy-start(bf16[768,1024]{1,0:T(8,128)(2,1)} %concatenate.11) | copy-start | bytes 4718596
  76.2 23.6 %collective-permute-start.8 = (bf16[1280,384]{1,0:T(8,128)(2,1)S(1)}, bf16[1280,384]{1,0:T(8,128)(2,1)S(1)}, u32[]{:S(2)}, u32[]{:S(2)}) collective-permute-start(bf16[1280,384]{1,0:T(8,128)(2,1)S(1)} %convolution_convert_fusion.1.refs_4_), channel_id=1, source_target_pairs={{0,1},{1,0},{2,3},{3,2},{4,5},{5,4},{6,7},{7,6},{8,9},{9,8},{10,11... | collective-permute-start | bytes 2949128 | tf_op jit(solution)/shard_map/ppermute | solution.py:433
  78.1 22.3 %copy-start.3 = (bf16[768,768]{1,0:T(8,128)(2,1)S(1)}, bf16[768,768]{1,0:T(8,128)(2,1)}, u32[]{:S(2)}) copy-start(bf16[768,768]{1,0:T(8,128)(2,1)} %w_ref.1) | copy-start | bytes 3538948
  78.3 11.1 %collective-permute-start.2 = (bf16[512,256]{1,0:T(8,128)(2,1)S(1)}, bf16[512,256]{1,0:T(8,128)(2,1)S(1)}, u32[]{:S(2)}, u32[]{:S(2)}) collective-permute-start(bf16[512,256]{1,0:T(8,128)(2,1)S(1)} %get-tuple-element.12), channel_id=1, source_target_pairs={{0,2},{1,3},{2,4},{3,5},{4,6},{5,7},{6,0},{7,1},{8,10},{9,11},{10,... | collective-permute-start | bytes 786440 | tf_op jit(solution)/shard_map/ppermute | solution.py:422
  78.4 21.4 %collective-permute-start.3 = (bf16[512,256]{1,0:T(8,128)(2,1)S(1)}, bf16[512,256]{1,0:T(8,128)(2,1)S(1)}, u32[]{:S(2)}, u32[]{:S(2)}) collective-permute-start(bf16[512,256]{1,0:T(8,128)(2,1)S(1)} %get-tuple-element.11), channel_id=1, source_target_pairs={{0,4},{1,5},{2,6},{3,7},{4,0},{5,1},{6,2},{7,3},{8,12},{9,13},{10,... | collective-permute-start | bytes 786440 | tf_op jit(solution)/shard_map/ppermute | solution.py:422
  80.0 19.8 %collective-permute-start.4 = (bf16[512,256]{1,0:T(8,128)(2,1)S(1)}, bf16[512,256]{1,0:T(8,128)(2,1)S(1)}, u32[]{:S(2)}, u32[]{:S(2)}) collective-permute-start(bf16[512,256]{1,0:T(8,128)(2,1)S(1)} %get-tuple-element.10), channel_id=1, source_target_pairs={{0,6},{1,7},{2,0},{3,1},{4,2},{5,3},{6,4},{7,5},{8,14},{9,15},{10,... | collective-permute-start | bytes 786440 | tf_op jit(solution)/shard_map/ppermute | solution.py:422
  135.9 0.9 copy-start.2

commit v5 on v4

--- a/solution.py
+++ b/solution.py
@@ -158,16 +158,14 @@
 def cross_kernel(
     seq_count,
     chunk,
-    pieces,
     count_ref,
     middle_ref,
     w_ref,
     *refs,
 ):
     queries, refs = refs[:GROUPS], refs[GROUPS:]
-    rows_in, refs = refs[:pieces], refs[pieces:]
-    o_ref, mass_ref, q_ref, k_ref, v_ref, context, landed, mass, masses = refs[:9]
-    send_sem, recv_sem, mass_send, mass_recv = refs[9:]
+    own_ref, o_ref, mass_ref, q_ref, k_ref, v_ref, context, landed, mass, masses = refs[:10]
+    others, held, partial, send_sem, recv_sem, mass_send, mass_recv, row_send, row_recv = refs[10:]
     me = lax.axis_index("seq")
     across = seq_count // GROUPS
     group = me // across
@@ -188,11 +186,30 @@
             device_id_type=pl.DeviceIdType.MESH,
         )
     mass[...] = jnp.zeros_like(mass)
-    size = keys // pieces
-    for n, piece in enumerate(rows_in):
+    size = own_ref.shape[0]
+
+    def send_rows(p):
+        return pltpu.make_async_remote_copy(
+            src_ref=own_ref,
+            dst_ref=others.at[p - 1],
+            send_sem=row_send.at[p],
+            recv_sem=row_recv.at[p],
+            device_id={"seq": group * across + (column + p) % across},
+            device_id_type=pl.DeviceIdType.MESH,
+        )
+
+    def place(n, piece):
         k_ref[n * size : (n + 1) * size, :] = piece[:, part - HEAD :]
         ahead = lax.broadcasted_iota(jnp.int32, (size, wide), 1) < part
         v_ref[n * size : (n + 1) * size, :] = jnp.where(ahead, piece[:, :wide], jnp.ones((), BF16))
+
+    def cuts(start, stop):
+        return [(c, min(c + chunk, stop)) for c in range(start, stop, chunk)]
+
+    pl.semaphore_wait(barrier, seq_count - 1)
+    for p in range(1, across):
+        send_rows(p).start()
+    place(0, own_ref[...])
     for r, query in enumerate(queries):
         q_ref[r] = query[...]
 
@@ -216,32 +233,59 @@
             device_id_type=pl.DeviceIdType.MESH,
         )
 
-    def work(t, carry):
+    def tile_queries(t):
         r = (t // tiles + 1) % GROUPS
         first = pl.multiple_of(t % tiles * tile, tile)
-        q = q_ref[r, pl.ds(first, tile), :]
-        weigh = q[:, 0:1].astype(F32)
+        return r, first, q_ref[r, pl.ds(first, tile), :]
+
+    def scored(q, h, c, d):
+        mine = (lane >= (h + 1) * HEAD) & (lane < (h + 2) * HEAD)
+        qh = jnp.where(mine, q, jnp.zeros_like(q))
+        s = lax.dot_general(qh, k_ref[c:d, :], NT, preferred_element_type=F32)
+        e = jnp.exp2(s * EXP2_SCALE)
+        eb = e.astype(BF16)
+        return e, eb, jnp.dot(eb, v_ref[c:d, :], preferred_element_type=F32)
+
+    def own_work(t, carry):
+        r, first, q = tile_queries(t)
         result = jnp.zeros((tile, wide), F32)
         for h in range(heads):
-            mine = (lane >= (h + 1) * HEAD) & (lane < (h + 2) * HEAD)
-            qh = jnp.where(mine, q, jnp.zeros_like(q))
+            o = jnp.zeros((tile, wide), F32)
+            for c, d in cuts(0, size):
+                e, eb, more = scored(q, h, c, d)
+                held[t, h, :, c:d] = eb
+                o += more
+            kept = ((lane >= h * HEAD) & (lane < (h + 1) * HEAD)) | (lane == part + h)
+            result = jnp.where(kept, o, result)
+        partial[t] = result
+        return carry
+
+    lax.fori_loop(0, GROUPS * tiles, own_work, 0)
+    for p in range(1, across):
+        send_rows(p).wait()
+        place(p, others[p - 1])
+
+    def work(t, carry):
+        r, first, q = tile_queries(t)
+        weigh = q[:, 0:1].astype(F32)
+        before = partial[t]
+        result = jnp.zeros((tile, wide), F32)
+        for h in range(heads):
+            o = before
             parts = []
-            o = jnp.zeros((tile, wide), F32)
-            for c in range(0, keys, chunk):
-                s = lax.dot_general(qh, k_ref[c : c + chunk, :], NT, preferred_element_type=F32)
-                e = jnp.exp2(s * EXP2_SCALE)
-                o += jnp.dot(e.astype(BF16), v_ref[c : c + chunk, :], preferred_element_type=F32)
+            for c, d in cuts(size, keys):
+                e, eb, more = scored(q, h, c, d)
+                o += more
                 parts.append(e)
-            inverse = 1.0 / o[:, part : part + 1]
+            inverse = 1.0 / o[:, part + h : part + h + 1]
             result = jnp.where((lane >= h * HEAD) & (lane < (h + 1) * HEAD), o * inverse, result)
             weight = inverse * weigh
-            for c, e in zip(range(0, keys, chunk), parts):
-                mass[:, c : c + chunk] += jnp.sum((e * weight).reshape(tile // 8, 8, chunk), axis=0)
+            for c, d in cuts(0, size):
+                share = held[t, h, :, c:d].astype(F32) * weight
+                mass[:, c:d] += jnp.sum(share.reshape(tile // 8, 8, d - c), axis=0)
+            for (c, d), e in zip(cuts(size, keys), parts):
+                mass[:, c:d] += jnp.sum((e * weight).reshape(tile // 8, 8, d - c), axis=0)
         context[r, pl.ds(first, tile), :] = result[:, :part].astype(BF16)
-
-        @pl.when(t == tiles - 1)
-        def _():
-            pl.semaphore_wait(barrier, seq_count - 1)
 
         @pl.when((t % tiles == tiles - 1) & (t < (GROUPS - 1) * tiles))
         def _():
@@ -269,19 +313,22 @@
     mass_ref[...] = jnp.sum(masses[...], axis=0)
 
 
-def cross_attend(seq_count, count, queries, pieces, middle, x_out):
+def cross_attend(seq_count, count, queries, own_rows, middle, x_out):
     groups = len(queries)
     rows, wide = queries[0].shape
-    keys = sum(piece.shape[0] for piece in pieces)
+    across = seq_count // groups
+    size = own_rows.shape[0]
+    keys = across * size
+    tiles = groups * rows // 256
     part = wide - HEAD
     vmem = pl.BlockSpec(memory_space=pltpu.VMEM)
     return pl.pallas_call(
-        functools.partial(cross_kernel, seq_count, 512, len(pieces)),
+        functools.partial(cross_kernel, seq_count, 512),
         out_shape=(
             jax.ShapeDtypeStruct(middle.shape, BF16),
             jax.ShapeDtypeStruct((1, keys + 128), F32),
         ),
-        in_specs=[vmem] * (3 + groups + len(pieces)),
+        in_specs=[vmem] * (4 + groups),
         out_specs=(vmem, vmem),
         scratch_shapes=[
             pltpu.VMEM((groups, rows, wide), BF16),
@@ -291,20 +338,25 @@
             pltpu.VMEM((groups, rows, part), BF16),
             pltpu.VMEM((8, keys), F32),
             pltpu.VMEM((seq_count, 1, keys + 128), F32),
+            pltpu.VMEM((max(across - 1, 1), size, own_rows.shape[1]), BF16),
+            pltpu.VMEM((tiles, (wide - HEAD) // HEAD, 256, size), BF16),
+            pltpu.VMEM((tiles, 256, wide), F32),
             pltpu.SemaphoreType.DMA((groups,)),
             pltpu.SemaphoreType.DMA((groups,)),
             pltpu.SemaphoreType.DMA((seq_count,)),
             pltpu.SemaphoreType.DMA((seq_count,)),
+            pltpu.SemaphoreType.DMA((across,)),
+            pltpu.SemaphoreType.DMA((across,)),
         ],
         compiler_params=pltpu.CompilerParams(
-            vmem_limit_bytes=48 * 1024 * 1024, collective_id=0, has_side_effects=True
+            vmem_limit_bytes=56 * 1024 * 1024, collective_id=0, has_side_effects=True
         ),
         cost_estimate=pl.CostEstimate(
             flops=16 * groups * rows * keys * part,
             bytes_accessed=4 * keys * wide + 4 * rows * wide,
             transcendentals=3 * groups * rows * keys,
         ),
-    )(count, middle, x_out, *queries, *pieces)
+    )(count, middle, x_out, *queries, own_rows)
 
 
 def local(
@@ -422,19 +474,12 @@
             lax.ppermute(piece(cross_query, (group + r) % GROUPS), "seq", turn(r))
         )
 
-    pieces = []
-    for chunk in arrived:
-        own_rows = jnp.dot(
-            choose, chunk.reshape(-1, 2 * part), preferred_element_type=F32
-        ).astype(BF16)
-        pieces.append(own_rows)
-        for r in range(1, across):
-            step = [(i, i // across * across + (i % across + r) % across) for i in range(seq_count)]
-            pieces.append(lax.ppermute(own_rows, "seq", step))
-
+    own_rows = jnp.dot(
+        choose, arrived[0].reshape(-1, 2 * part), preferred_element_type=F32
+    ).astype(BF16)
     count = jnp.full((1, 128), jnp.sum(live))
     refined, mass = cross_attend(
-        seq_count, count, queries, pieces, middle, x_out
+        seq_count, count, queries, own_rows, middle, x_out
     )
     cand_mass = jnp.sum(mass[0, :-128].reshape(DESC, cand_count), axis=0)
     cand_score = cand_count * cand_mass / (HEADS * mass[0, -1])

time: 141 us -> 165 us (1.17)
  Pallas kernels: 46.7 us -> 73.2 us
  waiting for transfers between devices: 28.7 us -> 22.4 us
  local copies, waits for them, and re-layouts: 17.8 us -> 19.6 us
    pallas_call x1, Pallas kernels: 35.4 us -> 61.7 us  [cross_attend(): pl.pallas_call(functools.partial(cross_kernel, seq_count, 512), out_shape...]
    ppermute x3, waiting for transfers between devices: 17 us -> 0.01 us  [local(): lax.ppermute(piece(cross_query, (group + r) % GROUPS), 'seq', turn(r))]
    all_to_all x1, waiting for transfers between devices: 11.7 us -> 22.4 us  [local(): lax.all_to_all(chunk, ('doc', 'seq'), split_axis=0, concat_axis=0, tiled=...]
    unnamed x25 -> x23, local copies, waits for them, and re-layouts: 4.8 us -> 4.07 us
  transfers between devices with their start and end apart: 10 -> 9, of which waited for: 3 -> 1; matrix products, arithmetic and copies ran while one was open for 19% -> 20% of each run, Pallas kernels for 8% -> 7%
where the time goes in v5:
time: 165 us; the launch traced here: 164 us
  Pallas kernels  73.2 us (44%)
  waiting for transfers between devices  22.4 us (14%)
  starting transfers between devices  21.4 us (13%)
  local copies, waits for them, and re-layouts  19.6 us (12%)
  other arithmetic  14 us (8%)
  matrix products  11.8 us (7%)
  between operations  1.75 us (1%)
    pallas_call x1, Pallas kernels, cross_attend(): pl.pallas_call(functools.partial(cross_kernel, seq_count, 512), out_shape...  61.7 us
    all_to_all x1, waiting for transfers between devices, local(): lax.all_to_all(chunk, ('doc', 'seq'), split_axis=0, concat_axis=0, tiled=...  22.4 us
    pallas_call x1, Pallas kernels, window_attend(): pl.pallas_call(window_kernel, grid=(pairs,), out_shape=jax.ShapeDtypeStru...  7.63 us
    all_to_all x1, starting transfers between devices, local(): lax.all_to_all(chunk, ('doc', 'seq'), split_axis=0, concat_axis=0, tiled=...  6.07 us
    dot_general x1, matrix products, local(): jnp.dot(choose, arrived[0].reshape(-1, 2 * part), preferred_element_type=...  6.01 us
    ppermute x3, starting transfers between devices, local(): lax.ppermute(piece(cross_query, (group + r) % GROUPS), 'seq', turn(r))  5.36 us
    ppermute x3, starting transfers between devices, local(): lax.ppermute(cache_rows, 'doc', [(i, (i + r) % doc_count) for i in range(...  4.48 us
    ppermute x1, starting transfers between devices, local(): low = lax.ppermute(flagged[tok_rows - HALF_WIN:], 'seq', up)  4.16 us
  transfers between devices with their start and end apart: 9, of which 1 were waited for; matrix products, arithmetic and copies ran while one was open for 20% of the time, Pallas kernels for 7%

profile of v5, /device:TPU:0, one launch (start us, length us, event | category | flops | bytes accessed | tf_op | source)
XLA Modules:
  0.0 164.0 jit_solution(4141943278302107812)
XLA Ops:
  0.7 0.8 fusion.39
  1.5 3.5 %gather_fusion = s32[320]{0:T(512)S(1)} fusion(s32[9216]{0:T(1024)} %param.18, s32[1024]{0:T(1024)S(1)} %pad_clamp_fusion), kind=kCustom, calls=%fused_computation | custom fusion | bytes 3840 | tf_op jit(solution)/shard_map/gather | solution.py:392
  5.6 2.6 %collective-permute-start.6 = (s32[320]{0:T(512)S(1)}, s32[320]{0:T(512)S(1)}, u32[]{:S(2)}, u32[]{:S(2)}) collective-permute-start(s32[320]{0:T(512)S(1)} %gather_fusion), channel_id=1, source_target_pairs={{0,16},{8,24},{16,0},{24,8},{1,17},{9,25},{17,1},{25,9},{2,18},{10... | collective-permute-start | bytes 3848 | tf_op jit(solution)/shard_map/ppermute | solution.py:396
  8.2 1.4 collective-permute-start.7
  10.3 1.0 fusion.13
  11.4 4.2 %collective-permute-start = (bf16[256,896]{1,0:T(8,128)(2,1)}, bf16[256,896]{1,0:T(8,128)(2,1)}, u32[]{:S(2)}, u32[]{:S(2)}) collective-permute-start(bf16[256,896]{1,0:T(8,128)(2,1)} %get-tuple-element.14), channel_id=1, source_target_pairs={{0,1},{1,2},{2,3},{3,4},{4,5},{5,6},{6,7},{8,9},{9,10},{10,11},{11... | collective-permute-start | bytes 1376264 | tf_op jit(solution)/shard_map/ppermute | solution.py:388
  15.6 1.3 collective-permute-start.1
  17.6 2.9 %fusion.52 = (bf16[768,192]{1,0:T(8,128)(2,1)}, bf16[768,192]{1,0:T(8,128)(2,1)}, bf16[768,192]{1,0:T(8,128)(2,1)}, bf16[768,192]{1,0:T(8,128)(2,1)}) fusion(bf16[768,768]{1,0:T(8,128)(2,1)} %param.15), kind=kLoop, calls=%fused_computation.133 | loop fusion | bytes 2359296 | tf_op jit(solution)/shard_map/slice | solution.py:457
  21.2 2.7 %broadcast_and_fusion = pred[4,320,2048]{2,1,0:T(32,128)(4,1)} fusion(pred[4,2048]{1,0:T(4,128)(4,1)S(1)} %iota_compare_fusion.7, pred[320,2048]{1,0:T(8,128)(4,1)S(1)} %broadcast_compare_fusion), kind=kLoop, calls=%fused_computation.1 | loop fusion | flops 2621440 | bytes 3284992 | tf_op jit(solution)/shard_map/and | solution.py:436
  24.0 4.1 %concatenate.11 = bf16[768,1024]{1,0:T(8,128)(2,1)} concatenate(bf16[768,64]{1,0:T(8,128)(2,1)S(1)} %broadcast_in_dim.54, bf16[768,192]{1,0:T(8,128)(2,1)} %get-tuple-element.8, bf16[768,64]{1,0:T(8,128)(2,1)S(1)} %broadcast_in_dim.54, bf16[768,192]{1,0:T(8,128)(2,1)} %get-tuple-element.7, bf16[768,64]{1,0:T(8,128)(2,1)S(1)} %broadcast_in_dim.54, ...), dimensions={1} | concatenate | bytes 3145728 | tf_op jit(solution)/shard_map/concatenate | solution.py:458
  28.7 3.8 %shard_map.114 = bf16[4,4,128,384]{3,2,1,0:T(8,128)(2,1)S(1)} custom-call(s32[64]{0:T(128)S(1)} %reshape.373.request_ref, bf16[4608,768]{1,0:T(8,128)(2,1)} %bitcast.28, bf16[256,256]{1,0:T(8,128)(2,1)S(1)} %fusion.14.order_ref), custom_call_target="tpu_custom_call" | custom-call | flops 402653184 | bytes 3145728 | tf_op jit(solution)/shard_map/pallas_call | solution.py:135
  32.6 1.2 copy-done.1
  33.8 6.1 %all-to-all-start = ((bf16[32,64,384]{2,1,0:T(8,128)(2,1)}), bf16[32,64,384]{2,1,0:T(8,128)(2,1)}, u32[]{:S(2)}, u32[]{:S(2)}) async-start(bf16[32,64,384]{2,1,0:T(8,128)(2,1)} %bitcast.21), calls=%async_computation | async-start | bytes 3145728 | tf_op jit(solution)/shard_map/all_to_all | solution.py:425
  39.9 1.4 convert_reduce_fusion
  41.3 1.7 %fusion.2 = f32[1024]{0:T(1024)S(1)} fusion(f32[1024]{0:T(1024)S(1)} %broadcast_multiply_fusion, bf16[256,896]{1,0:T(8,128)(2,1)} %collective-permute-done.1, bf16[512,128]{1,0:T(8,128)(2,1)S(1)} %copy-done.4, bf16[512,768]{1,0:T(8,128)(2,1)S(1)} %bitcast.25, bf16[256,896]{1,0:T(8,128)(2,1)} %collective-permute-done), kind=kLoop, calls=%fused_computation.7 | loop fusion | flops 8649728 | bytes 1843200 | tf_op jit(solution)/shard_map/reduce_sum | solution.py:25
  43.0 1.0 convert_reduce_fusion.2
  44.1 3.3 %fusion.3 = bf16[1024,768]{1,0:T(8,128)(2,1)S(1)} fusion(f32[1024]{0:T(1024)S(1)} %add_rsqrt_fusion, f32[1024]{0:T(1024)S(1)} %broadcast_multiply_fusion, bf16[256,896]{1,0:T(8,128)(2,1)} %collective-permute-done.1, bf16[512,128]{1,0:T(8,128)(2,1)S(1)} %copy-done.4, bf16[512,768]{1,0:T(8,128)(2,1)S(1)} %bitcast.27, bf16[256,896]{1,0:T(8,128)(2,1)} %collective-permute-done), kind=kLoop, calls=%fused_computation.8 | loop fusion | flops 8650752 | bytes 3416064 | tf_op jit(solution)/shard_map/convert_element_type | solution.py:441
  47.4 0.8 convolution_convert_fusion.2.q_ref
  48.2 2.8 %convolution_convert_fusion.k_ref.v_ref = bf16[1024,1536]{1,0:T(8,128)(2,1)S(1)} fusion(bf16[1024,768]{1,0:T(8,128)(2,1)S(1)} %fusion.3, bf16[768,1536]{1,0:T(8,128)(2,1)S(1)} %copy-done), kind=kOutput, calls=%fused_computation.4 | convolution fusion | flops 2417491968 | bytes 7077888 | tf_op jit(solution)/shard_map/dot_general | solution.py:442
  51.0 7.6 %shard_map.113 = bf16[512,768]{1,0:T(8,128)(2,1)S(1)} custom-call(f32[1,1024]{1,0:T(1,128)S(1)} %bitcast.22, bf16[512,768]{1,0:T(8,128)(2,1)S(1)} %convolution_convert_fusion.2.q_ref, bf16[1024,1536]{1,0:T(8,128)(2,1)S(1)} %convolution_convert_fusion.k_ref.v_ref, bf16[1024,1536]{1,0:T(8,128)(2,1)S(1)} %convolution_convert_fusion.k_ref.v_ref), custom_call_target="tpu_custom_call" | custom-call | flops 2415919104 | bytes 3145728 | tf_op jit(solution)/shard_map/pallas_call | solution.py:72
  58.7 0.9 convert_reduce_fusion.1
  60.1 1.0 select_convert_fusion
  61.1 0.8 constant_dynamic-slice_fusion
  62.0 1.5 collective-permute-start.2
  63.5 2.4 %collective-permute-start.3 = (bf16[512,256]{1,0:T(8,128)(2,1)S(1)}, bf16[512,256]{1,0:T(8,128)(2,1)}, u32[]{:S(2)}, u32[]{:S(2)}) collective-permute-start(bf16[512,256]{1,0:T(8,128)(2,1)S(1)} %get-tuple-element.11), channel_id=1, source_target_pairs={{0,4},{1,5},{2,6},{3,7},{4,0},{5,1},{6,2},{7,3},{8,12},{9,13},{10,... | collective-permute-start | bytes 786440 | tf_op jit(solution)/shard_map/ppermute | solution.py:474
  65.9 1.4 collective-permute-start.4
  67.4 22.4 %all-to-all-done = bf16[32,64,384]{2,1,0:T(8,128)(2,1)} async-done(((bf16[32,64,384]{2,1,0:T(8,128)(2,1)}), bf16[32,64,384]{2,1,0:T(8,128)(2,1)}, u32[]{:S(2)}, u32[]{:S(2)}) %all-to-all-start) | async-done | bytes 1572896 | tf_op jit(solution)/shard_map/all_to_all | solution.py:425
  89.7 6.0 %convolution_convert_fusion.1.refs_4_ = bf16[1280,384]{1,0:T(8,128)(2,1)} fusion(pred[1280,2048]{1,0:T(32,128)(4,1)} %bitcast.29, bf16[2048,384]{1,0:T(8,128)(2,1)} %bitcast.6), kind=kOutput, calls=%fused_computation.9 | convolution fusion | flops 2013757440 | bytes 5177344 | tf_op jit(solution)/shard_map/dot_general | solution.py:477
  95.8 1.2 broadcast_in_dim.50.count_ref
  97.0 61.7 %shard_map.115 = (bf16[512,768]{1,0:T(8,128)(2,1)}, f32[1,2688]{1,0:T(1,128)}) custom-call(f32[1,128]{1,0:T(1,128)} %broadcast_in_dim.50.count_ref, bf16[512,768]{1,0:T(8,128)(2,1)} %copy-done.6, bf16[768,768]{1,0:T(8,128)(2,1)} %w_ref.1, bf16[512,256]{1,0:T(8,128)(2,1)} %get-tuple-element.13.refs_0_, bf16[512,256]{1,0:T(8,128)(2,1)} %copy-done.10, ...), custom_call_target="tpu_custom_call" | custom-call | flops 16106127360 | bytes 3145728 | tf_op jit(solution)/shard_map/pallas_call | solution.py:325
  159.4 1.2 slice.43
  162.0 2.1 %copy.15 = bf16[1,512,768]{2,1,0:T(8,128)(2,1)} copy(bf16[1,512,768]{2,1,0:T(8,128)(2,1)} %bitcast.30) | data formatting | bytes 1572864
  (69 shorter events, 5.3 us)
Async XLA Ops:
  0.6 47.5 %copy-start = (bf16[768,1536]{1,0:T(8,128)(2,1)S(1)}, bf16[768,1536]{1,0:T(8,128)(2,1)}, u32[]{:S(2)}) copy-start(bf16[768,1536]{1,0:T(8,128)(2,1)} %param.13) | copy-start | bytes 7077892
  0.6 8.9 %copy-start.7 = (s32[1,512]{1,0:T(1,128)S(1)}, s32[1,512]{1,0:T(1,128)}, u32[]{:S(2)}) copy-start(s32[1,512]{1,0:T(1,128)} %param.11) | copy-start | bytes 6148
  0.7 9.7 %copy-start.2 = (bf16[1,512,768]{2,1,0:T(8,128)(2,1)S(1)}, bf16[1,512,768]{2,1,0:T(8,128)(2,1)}, u32[]{:S(2)}) copy-start(bf16[1,512,768]{2,1,0:T(8,128)(2,1)} %param.10) | copy-start | bytes 2359300
  5.1 23.0 %collective-permute-start.5 = (s32[320]{0:T(512)S(1)}, s32[320]{0:T(512)S(1)}, u32[]{:S(2)}, u32[]{:S(2)}) collective-permute-start(s32[320]{0:T(512)S(1)} %gather_fusion), channel_id=1, source_target_pairs={{0,8},{8,16},{16,24},{24,0},{1,9},{9,17},{17,25},{25,1},{2,10},{10... | collective-permute-start | bytes 3848 | tf_op jit(solution)/shard_map/ppermute | solution.py:396
  5.6 22.6 %collective-permute-start.6 = (s32[320]{0:T(512)S(1)}, s32[320]{0:T(512)S(1)}, u32[]{:S(2)}, u32[]{:S(2)}) collective-permute-start(s32[320]{0:T(512)S(1)} %gather_fusion), channel_id=1, source_target_pairs={{0,16},{8,24},{16,0},{24,8},{1,17},{9,25},{17,1},{25,9},{2,18},{10... | collective-permute-start | bytes 3848 | tf_op jit(solution)/shard_map/ppermute | solution.py:396
  8.2 20.0 %collective-permute-start.7 = (s32[320]{0:T(512)S(1)}, s32[320]{0:T(512)S(1)}, u32[]{:S(2)}, u32[]{:S(2)}) collective-permute-start(s32[320]{0:T(512)S(1)} %gather_fusion), channel_id=1, source_target_pairs={{0,24},{8,0},{16,8},{24,16},{1,25},{9,1},{17,9},{25,17},{2,26},{10... | collective-permute-start | bytes 3848 | tf_op jit(solution)/shard_map/ppermute | solution.py:396
  9.7 0.6 copy-start.3
  11.4 28.5 %collective-permute-start = (bf16[256,896]{1,0:T(8,128)(2,1)}, bf16[256,896]{1,0:T(8,128)(2,1)}, u32[]{:S(2)}, u32[]{:S(2)}) collective-permute-start(bf16[256,896]{1,0:T(8,128)(2,1)} %get-tuple-element.14), channel_id=1, source_target_pairs={{0,1},{1,2},{2,3},{3,4},{4,5},{5,6},{6,7},{8,9},{9,10},{10,11},{11... | collective-permute-start | bytes 1376264 | tf_op jit(solution)/shard_map/ppermute | solution.py:388
  15.6 24.3 %collective-permute-start.1 = (bf16[256,896]{1,0:T(8,128)(2,1)}, bf16[256,896]{1,0:T(8,128)(2,1)}, u32[]{:S(2)}, u32[]{:S(2)}) collective-permute-start(bf16[256,896]{1,0:T(8,128)(2,1)} %get-tuple-element.15), channel_id=1, source_target_pairs={{1,0},{2,1},{3,2},{4,3},{5,4},{6,5},{7,6},{9,8},{10,9},{11,10},{12... | collective-permute-start | bytes 1376264 | tf_op jit(solution)/shard_map/ppermute | solution.py:389
  32.6 1.2 copy-start.1
  33.8 6.1 %copy-start.4 = (bf16[512,128]{1,0:T(8,128)(2,1)S(1)}, bf16[512,128]{1,0:T(8,128)(2,1)}, u32[]{:S(2)}) copy-start(bf16[512,128]{1,0:T(8,128)(2,1)} %copy-done.3) | copy-start | bytes 393220
  33.8 56.0 %all-to-all-start = ((bf16[32,64,384]{2,1,0:T(8,128)(2,1)}), bf16[32,64,384]{2,1,0:T(8,128)(2,1)}, u32[]{:S(2)}, u32[]{:S(2)}) async-start(bf16[32,64,384]{2,1,0:T(8,128)(2,1)} %bitcast.21), calls=%async_computation | async-start | bytes 3145728 | tf_op jit(solution)/shard_map/all_to_all | solution.py:425
  44.0 3.3 %copy-start.8 = (bf16[768,768]{1,0:T(8,128)(2,1)S(1)}, bf16[768,768]{1,0:T(8,128)(2,1)}, u32[]{:S(2)}) copy-start(bf16[768,768]{1,0:T(8,128)(2,1)} %param.12) | copy-start | bytes 3538948
  51.0 7.7 %copy-start.9 = (bf16[768,768]{1,0:T(8,128)(2,1)S(1)}, bf16[768,768]{1,0:T(8,128)(2,1)}, u32[]{:S(2)}) copy-start(bf16[768,768]{1,0:T(8,128)(2,1)} %param.14) | copy-start | bytes 3538948
  58.7 1.4 copy-start.5
  59.6 1.6 copy-start.6
  62.0 33.8 %collective-permute-start.2 = (bf16[512,256]{1,0:T(8,128)(2,1)S(1)}, bf16[512,256]{1,0:T(8,128)(2,1)S(1)}, u32[]{:S(2)}, u32[]{:S(2)}) collective-permute-start(bf16[512,256]{1,0:T(8,128)(2,1)S(1)} %get-tuple-element.12), channel_id=1, source_target_pairs={{0,2},{1,3},{2,4},{3,5},{4,6},{5,7},{6,0},{7,1},{8,10},{9,11},{10,... | collective-permute-start | bytes 786440 | tf_op jit(solution)/shard_map/ppermute | solution.py:474
  63.5 32.2 %collective-permute-start.3 = (bf16[512,256]{1,0:T(8,128)(2,1)S(1)}, bf16[512,256]{1,0:T(8,128)(2,1)}, u32[]{:S(2)}, u32[]{:S(2)}) collective-permute-start(bf16[512,256]{1,0:T(8,128)(2,1)S(1)} %get-tuple-element.11), channel_id=1, source_target_pairs={{0,4},{1,5},{2,6},{3,7},{4,0},{5,1},{6,2},{7,3},{8,12},{9,13},{10,... | collective-permute-start | bytes 786440 | tf_op jit(solution)/shard_map/ppermute | solution.py:474
  65.9 29.8 %collective-permute-start.4 = (bf16[512,256]{1,0:T(8,128)(2,1)S(1)}, bf16[512,256]{1,0:T(8,128)(2,1)}, u32[]{:S(2)}, u32[]{:S(2)}) collective-permute-start(bf16[512,256]{1,0:T(8,128)(2,1)S(1)} %get-tuple-element.10), channel_id=1, source_target_pairs={{0,6},{1,7},{2,0},{3,1},{4,2},{5,3},{6,4},{7,5},{8,14},{9,15},{10,... | collective-permute-start | bytes 786440 | tf_op jit(solution)/shard_map/ppermute | solution.py:474
  95.7 1.2 copy-start.10
